TPU v7x, 32 devices: a whole 2x2x4 slice. The times are simulated.
32 devices in a mesh: dp: 4 (over y, core), tensor: 8 (over z, x).
Axes of the slice: x: 2, y: 2, z: 4, core: 2. Of those that a mesh axis runs over, the one named last changes fastest.
Arguments:
- tokens: bfloat16 [8192, 1024], P(('dp', 'tensor')), may hold values from -6 to 6
- segment_ids: int32 [4, 2048], P('dp'), may hold values from 0 to 3, never falling along the last dimension, each value on 1 to 1024 neighbouring positions
- cotangent: bfloat16 [8192, 1024], P(('dp', 'tensor')), may hold values from -6 to 6
- attn_gain: float32 [1024], replicated, may hold values from 0.5 to 1.5
- query_weight: bfloat16 [1024, 1024], P('dp', 'tensor'), may hold values from -0.1875 to 0.1875
- key_weight: bfloat16 [1024, 512], P('dp', 'tensor'), may hold values from -0.1875 to 0.1875
- value_weight: bfloat16 [1024, 512], P('dp', 'tensor'), may hold values from -0.1875 to 0.1875
- output_weight: bfloat16 [1024, 1024], P('tensor', 'dp'), may hold values from -0.75 to 0.75
- query_gain: float32 [64], replicated, may hold values from 0.5 to 1.5
- key_gain: float32 [64], replicated, may hold values from 0.5 to 1.5
- ffn_gain: float32 [1024], replicated, may hold values from 0.5 to 1.5
- gate_weight: bfloat16 [1024, 4608], P('dp', 'tensor'), may hold values from -0.1875 to 0.1875
- up_weight: bfloat16 [1024, 4608], P('dp', 'tensor'), may hold values from -0.1875 to 0.1875
- down_weight: bfloat16 [4608, 1024], P('tensor', 'dp'), may hold values from -0.09375 to 0.09375
Outputs:
- block_out: bfloat16 [8192, 1024], P(('dp', 'tensor'))
- input_grad: bfloat16 [8192, 1024], P(('dp', 'tensor'))
- attn_gain_grad: float32 [1024], replicated
- query_grad: float32 [1024, 1024], P('dp', 'tensor')
- key_grad: float32 [1024, 512], P('dp', 'tensor')
- value_grad: float32 [1024, 512], P('dp', 'tensor')
- output_grad: float32 [1024, 1024], P('tensor', 'dp')
- query_gain_grad: float32 [64], replicated
- key_gain_grad: float32 [64], replicated
- ffn_gain_grad: float32 [1024], replicated
- gate_grad: float32 [1024, 4608], P('dp', 'tensor')
- up_grad: float32 [1024, 4608], P('dp', 'tensor')
- down_grad: float32 [4608, 1024], P('tensor', 'dp')
Inputs may be any that keep to these rules, and one draw needn't show every extreme that they name: `segment_ids`: in each row the numbers never fall; every run of one number covers 1 to 1024 positions, and some run covers exactly 1024.
All inputs are finite; a program needn't handle non-finite values.
Results may differ from a plain program's by a relative error of at most 0.022.
Values may be sent and summed in bfloat16 or wider, within the bound.
No kernel may reach another device: no remote copies, remote signals or barrier semaphores. Data moves between devices by JAX's collectives and lax.ppermute only.
A program may use at most 128 MiB of HBM per device.

v0:
```python
import math

import jax
import jax.numpy as jnp
from jax import lax
from jax.sharding import PartitionSpec as P

EPSILON = 1e-05
ROPE_BASE = 1000000.0
NEGATIVE = -1e30


def norm_rows(v, scales):
    factor = lax.rsqrt(jnp.mean(v * v, axis=-1, keepdims=True) + EPSILON)
    return v * factor * scales


def rotate(v, cosine, sine):
    half_dim = v.shape[-1] // 2
    first = v[..., :half_dim]
    second = v[..., half_dim:]
    return jnp.concatenate(
        [first * cosine - second * sine, second * cosine + first * sine], axis=-1
    )


def positions(segment):
    index = jnp.arange(segment.shape[0], dtype=jnp.int32)
    first = jnp.concatenate([jnp.ones((1,), dtype=jnp.bool_), segment[1:] != segment[:-1]])
    start = lax.cummax(jnp.where(first, index, jnp.zeros_like(index)), axis=0)
    return index - start


def rope_tables(segment, head_dim):
    half_dim = head_dim // 2
    inverse = ROPE_BASE ** (-(jnp.arange(half_dim, dtype=jnp.float32) * 2.0) / head_dim)
    angles = positions(segment).astype(jnp.float32)[:, None] * inverse[None, :]
    return (jnp.cos(angles)[:, None, :], jnp.sin(angles)[:, None, :])


def mult(a, b):
    return jnp.dot(a, b, preferred_element_type=jnp.float32)


def mult_left(a, b):
    return lax.dot_general(a, b, (((0,), (0,)), ((), ())), preferred_element_type=jnp.float32)


def mult_right(a, b):
    return lax.dot_general(a, b, (((1,), (1,)), ((), ())), preferred_element_type=jnp.float32)


def swiglu(gate_pre, up_pre):
    return jax.nn.silu(gate_pre) * up_pre


def per_device(
    tokens,
    segment_ids,
    cotangent,
    attn_gain,
    query_weight,
    key_weight,
    value_weight,
    output_weight,
    query_gain,
    key_gain,
    ffn_gain,
    gate_weight,
    up_weight,
    down_weight,
):
    head_dim = query_gain.shape[0]
    kv_count = key_weight.shape[1] // head_dim
    head_count = query_weight.shape[1] // head_dim
    group_size = head_count // kv_count
    q_mat, k_mat, v_mat, o_mat, g_mat, u_mat, d_mat = (
        lax.all_gather(query_weight, "dp", axis=0, tiled=True),
        lax.all_gather(key_weight, "dp", axis=0, tiled=True),
        lax.all_gather(value_weight, "dp", axis=0, tiled=True),
        lax.all_gather(output_weight, "dp", axis=1, tiled=True),
        lax.all_gather(gate_weight, "dp", axis=0, tiled=True),
        lax.all_gather(up_weight, "dp", axis=0, tiled=True),
        lax.all_gather(down_weight, "dp", axis=1, tiled=True),
    )
    segment = segment_ids[0]
    total_rows = segment.shape[0]
    cosine, sine = rope_tables(segment, head_dim)

    def head_prep(v, scales):
        return rotate(norm_rows(v, scales), cosine, sine)

    residual = tokens.astype(jnp.float32)
    xa_full, pull_attn_norm = jax.vjp(norm_rows, residual, attn_gain)
    xa_rows = lax.all_gather(xa_full.astype(jnp.bfloat16), "tensor", axis=0, tiled=True)
    query_proj = mult(xa_rows, q_mat).reshape(total_rows, head_count, head_dim)
    key_proj = mult(xa_rows, k_mat).reshape(total_rows, kv_count, head_dim)
    value_proj = mult(xa_rows, v_mat)
    query_rot, pull_query = jax.vjp(head_prep, query_proj, query_gain)
    key_rot, pull_key = jax.vjp(head_prep, key_proj, key_gain)
    q_rot = query_rot.astype(jnp.bfloat16).reshape(total_rows, kv_count, group_size, head_dim)
    k_rot = key_rot.astype(jnp.bfloat16)
    v_low = value_proj.astype(jnp.bfloat16).reshape(total_rows, kv_count, head_dim)
    block_rows = min(512, total_rows)
    starts = jnp.arange(0, total_rows, block_rows, dtype=jnp.int32)
    key_index = jnp.arange(total_rows, dtype=jnp.int32)
    score_scale = 1.0 / math.sqrt(head_dim)

    def scores_of(start):
        q_block = lax.dynamic_slice_in_dim(q_rot, start, block_rows, 0)
        s_block = lax.dynamic_slice_in_dim(segment, start, block_rows, 0)
        row_index = start + jnp.arange(block_rows, dtype=jnp.int32)
        raw_scores = (
            jnp.einsum("qcgd,kcd->cgqk", q_block, k_rot, preferred_element_type=jnp.float32)
            * score_scale
        )
        allowed = (s_block[:, None] == segment[None, :]) & (
            key_index[None, :] <= row_index[:, None]
        )
        return (jnp.where(allowed, raw_scores, NEGATIVE), q_block)

    def attend_block(start):
        masked, q_block = scores_of(start)
        row_max = jnp.max(masked, axis=-1, keepdims=True)
        exponent = jnp.exp(masked - row_max)
        row_total = jnp.sum(exponent, axis=-1, keepdims=True)
        attn_probs = exponent / row_total
        context = jnp.einsum(
            "cgqk,kcd->qcgd",
            attn_probs.astype(jnp.bfloat16),
            v_low,
            preferred_element_type=jnp.float32,
        )
        return (context.astype(jnp.bfloat16), (row_max + jnp.log(row_total))[..., 0])

    contexts, log_total = lax.map(attend_block, starts)
    attn_heads = contexts.reshape(total_rows, head_count * head_dim)
    attn_local = lax.psum_scatter(
        mult(attn_heads, o_mat).astype(jnp.bfloat16), "tensor", scatter_dimension=0, tiled=True
    ).astype(jnp.float32)
    hidden_state = residual + attn_local
    xf_full, pull_ffn_norm = jax.vjp(norm_rows, hidden_state, ffn_gain)
    xf_rows = lax.all_gather(xf_full.astype(jnp.bfloat16), "tensor", axis=0, tiled=True)
    gate_pre = mult(xf_rows, g_mat)
    up_pre = mult(xf_rows, u_mat)
    activation_full, pull_glu = jax.vjp(swiglu, gate_pre, up_pre)
    activation = activation_full.astype(jnp.bfloat16)
    ffn_local = lax.psum_scatter(
        mult(activation, d_mat).astype(jnp.bfloat16), "tensor", scatter_dimension=0, tiled=True
    ).astype(jnp.float32)
    block_out = (hidden_state + ffn_local).astype(jnp.bfloat16)
    grad_out = cotangent.astype(jnp.float32)
    ffn_grad = lax.all_gather(grad_out.astype(jnp.bfloat16), "tensor", axis=0, tiled=True)
    down_part = mult_left(activation, ffn_grad)
    grad_act = mult_right(ffn_grad, d_mat).astype(jnp.bfloat16)
    grad_gate, grad_up = pull_glu(grad_act.astype(jnp.float32))
    grad_gate = grad_gate.astype(jnp.bfloat16)
    grad_up = grad_up.astype(jnp.bfloat16)
    gate_part = mult_left(xf_rows, grad_gate)
    up_part = mult_left(xf_rows, grad_up)
    grad_xf = lax.psum_scatter(
        (mult_right(grad_gate, g_mat) + mult_right(grad_up, u_mat)).astype(jnp.bfloat16),
        "tensor",
        scatter_dimension=0,
        tiled=True,
    ).astype(jnp.float32)
    grad_h_norm, ffn_gain_part = pull_ffn_norm(grad_xf)
    grad_hidden = grad_out + grad_h_norm
    attn_grad = lax.all_gather(grad_hidden.astype(jnp.bfloat16), "tensor", axis=0, tiled=True)
    out_part = mult_left(attn_heads, attn_grad)
    grad_heads = (
        mult_right(attn_grad, o_mat)
        .astype(jnp.bfloat16)
        .reshape(total_rows, kv_count, group_size, head_dim)
    )

    def back_block(carry, operands):
        grad_key, grad_value = carry
        start, log_block = operands
        masked, q_block = scores_of(start)
        attn_probs = jnp.exp(masked - log_block[..., None])
        g_block = lax.dynamic_slice_in_dim(grad_heads, start, block_rows, 0)
        grad_probs = jnp.einsum(
            "qcgd,kcd->cgqk", g_block, v_low, preferred_element_type=jnp.float32
        )
        delta = jnp.sum(attn_probs * grad_probs, axis=-1, keepdims=True)
        grad_score = (attn_probs * (grad_probs - delta)).astype(jnp.bfloat16)
        grad_q_block = (
            jnp.einsum("cgqk,kcd->qcgd", grad_score, k_rot, preferred_element_type=jnp.float32)
            * score_scale
        )
        grad_key = (
            grad_key
            + jnp.einsum("cgqk,qcgd->kcd", grad_score, q_block, preferred_element_type=jnp.float32)
            * score_scale
        )
        grad_value = grad_value + jnp.einsum(
            "cgqk,qcgd->kcd",
            attn_probs.astype(jnp.bfloat16),
            g_block,
            preferred_element_type=jnp.float32,
        )
        return ((grad_key, grad_value), grad_q_block)

    zero_keys = jnp.zeros((total_rows, kv_count, head_dim), jnp.float32)
    (grad_key_rot, grad_value), grad_query_rot = lax.scan(
        back_block, (zero_keys, zero_keys), (starts, log_total)
    )
    grad_query_proj, query_gain_part = pull_query(
        grad_query_rot.reshape(total_rows, head_count, head_dim)
    )
    grad_key_proj, key_gain_part = pull_key(grad_key_rot)
    grad_query_low = grad_query_proj.reshape(total_rows, head_count * head_dim).astype(jnp.bfloat16)
    grad_key_low = grad_key_proj.reshape(total_rows, kv_count * head_dim).astype(jnp.bfloat16)
    grad_value_low = grad_value.reshape(total_rows, kv_count * head_dim).astype(jnp.bfloat16)
    query_part = mult_left(xa_rows, grad_query_low)
    key_part = mult_left(xa_rows, grad_key_low)
    value_part = mult_left(xa_rows, grad_value_low)
    grad_xa = lax.psum_scatter(
        (
            mult_right(grad_query_low, q_mat)
            + mult_right(grad_key_low, k_mat)
            + mult_right(grad_value_low, v_mat)
        ).astype(jnp.bfloat16),
        "tensor",
        scatter_dimension=0,
        tiled=True,
    ).astype(jnp.float32)
    grad_x_norm, attn_gain_part = pull_attn_norm(grad_xa)
    input_grad = (grad_hidden + grad_x_norm).astype(jnp.bfloat16)
    query_grad, key_grad, value_grad, output_grad, gate_grad, up_grad, down_grad = (
        lax.psum_scatter(
            query_part.astype(jnp.bfloat16), "dp", scatter_dimension=0, tiled=True
        ).astype(jnp.float32),
        lax.psum_scatter(
            key_part.astype(jnp.bfloat16), "dp", scatter_dimension=0, tiled=True
        ).astype(jnp.float32),
        lax.psum_scatter(
            value_part.astype(jnp.bfloat16), "dp", scatter_dimension=0, tiled=True
        ).astype(jnp.float32),
        lax.psum_scatter(
            out_part.astype(jnp.bfloat16), "dp", scatter_dimension=1, tiled=True
        ).astype(jnp.float32),
        lax.psum_scatter(
            gate_part.astype(jnp.bfloat16), "dp", scatter_dimension=0, tiled=True
        ).astype(jnp.float32),
        lax.psum_scatter(
            up_part.astype(jnp.bfloat16), "dp", scatter_dimension=0, tiled=True
        ).astype(jnp.float32),
        lax.psum_scatter(
            down_part.astype(jnp.bfloat16), "dp", scatter_dimension=1, tiled=True
        ).astype(jnp.float32),
    )
    attn_gain_grad, query_gain_grad, key_gain_grad, ffn_gain_grad = lax.psum(
        (attn_gain_part, query_gain_part, key_gain_part, ffn_gain_part), ("dp", "tensor")
    )
    return (
        block_out,
        input_grad,
        attn_gain_grad,
        query_grad,
        key_grad,
        value_grad,
        output_grad,
        query_gain_grad,
        key_gain_grad,
        ffn_gain_grad,
        gate_grad,
        up_grad,
        down_grad,
    )


def solution(mesh):
    in_specs = (
        P(("dp", "tensor"), None),
        P("dp", None),
        P(("dp", "tensor"), None),
        P(),
        P("dp", "tensor"),
        P("dp", "tensor"),
        P("dp", "tensor"),
        P("tensor", "dp"),
        P(),
        P(),
        P(),
        P("dp", "tensor"),
        P("dp", "tensor"),
        P("tensor", "dp"),
    )
    out_specs = (
        P(("dp", "tensor"), None),
        P(("dp", "tensor"), None),
        P(),
        P("dp", "tensor"),
        P("dp", "tensor"),
        P("dp", "tensor"),
        P("tensor", "dp"),
        P(),
        P(),
        P(),
        P("dp", "tensor"),
        P("dp", "tensor"),
        P("tensor", "dp"),
    )
    return jax.shard_map(
        per_device, mesh=mesh, in_specs=in_specs, out_specs=out_specs, check_vma=False
    )
```

profile of v0, /device:TPU:0, one launch (start us, length us, event | category | flops | bytes accessed | tf_op | source)
XLA Modules:
  0.0 954.6 jit_solution(16074547679362748660)
XLA Ops:
  12.8 6.7 all_gather.35
  19.5 5.8 all_gather.36
  25.3 6.2 all_gather.34
  31.5 6.1 all_gather.37
  38.8 48.9 %all-gather.8.cloned.1.call-done = bf16[2048,1024]{1,0:T(8,128)(2,1)} async-done(((bf16[256,1024]{1,0:T(8,128)(2,1)}), bf16[2048,1024]{1,0:T(8,128)(2,1)}) %all-gather.8.cloned.1.call-update) | async-done | bytes 4194320 | tf_op jit(solution)/shard_map/all_gather | solution.py:95
  87.7 3.7 multiply_reduce_fusion.4
  97.2 46.7 %while.28 = (s32[]{:T(128)}, bf16[4,512,1,2,64]{1,4,3,2,0:T(8,128)(2,1)S(1)}, f32[4,1,2,512]{3,2,1,0:T(2,128)S(1)}, s32[4]{0:T(128)S(1)}, s32[2048]{0:T(1024)S(1...) while((s32[]{:T(128)}, ...), condition=%wide.region_8.9_spmd.clone, body=%wide.region_5.8_spmd.clone.sunk | while | flops 565247488 | bytes 30197952 | solution.py:136
  145.2 3.3 convolution_convert_fusion.1
  150.3 116.1 %reduce-scatter.12.cloned.1.call-done = bf16[256,1024]{1,0:T(8,128)(2,1)} async-done(((bf16[2048,1024]{1,0:T(8,128)(2,1)}), bf16[256,1024]{1,0:T(8,128)(2,1)}) %reduce-scatter.12.cloned.1.call-update) | async-done | bytes 524304 | tf_op jit(solution)/shard_map/reduce_scatter | solution.py:138
  271.0 6.6 convolution_convert_fusion.2
  277.7 75.9 %all-gather.10.cloned.1.call-done = bf16[2048,1024]{1,0:T(8,128)(2,1)} async-done(((bf16[256,1024]{1,0:T(8,128)(2,1)}), bf16[2048,1024]{1,0:T(8,128)(2,1)}) %all-gather.10.cloned.1.call-update) | async-done | bytes 4194320 | tf_op jit(solution)/shard_map/all_gather | solution.py:143
  353.5 7.3 fusion.117
  360.9 10.2 %all-gather.12.cloned.1.call-done = bf16[1024,576]{0,1:T(8,128)(2,1)} async-done(((bf16[256,576]{0,1:T(8,128)(2,1)}), bf16[1024,576]{0,1:T(8,128)(2,1)}) %all-gather.12.cloned.1.call-update) | async-done | bytes 1179664 | tf_op jit(solution)/shard_map/all_gather | solution.py:82
  371.1 11.0 %fusion.70 = (bf16[2048,576]{0,1:T(8,128)(2,1)S(1)}, bf16[2048,576]{0,1:T(8,128)(2,1)}, bf16[2048,576]{0,1:T(8,128)(2,1)S(1)}) fusion(f32[2048,576]{0,1:T(8,128)} %fusion.117, bf16[2048,576]{0,1:T(8,128)(2,1)} %convolution_convert_fusion.2, bf16[2048,1024]{1,0:T(8,128)(2,1)} %all-gather.10.cloned.1.call-done, ...), kind=kOutput, calls=%fused_computation.76 | convolution fusion | flops 2435973120 | bytes 19529728 | tf_op jit(solution)/shard_map/dot_general | solution.py:42
  382.1 3.7 fusion.118
  385.8 5.2 add_convert_fusion.1
  391.1 88.0 %reduce-scatter.16.cloned.1.call-done = bf16[256,1024]{1,0:T(8,128)(2,1)} async-done(((bf16[2048,1024]{1,0:T(8,128)(2,1)}), bf16[256,1024]{1,0:T(8,128)(2,1)}) %reduce-scatter.16.cloned.1.call-update) | async-done | bytes 524304 | tf_op jit(solution)/shard_map/reduce_scatter | solution.py:161
  483.5 6.6 convolution_convert_fusion.7
  490.2 7.0 convolution_convert_fusion.6
  497.2 6.6 convolution_convert_fusion.5
  503.9 52.3 %all-gather.20.cloned.1.call-done = bf16[2048,1024]{1,0:T(8,128)(2,1)} async-done(((bf16[256,1024]{1,0:T(8,128)(2,1)}), bf16[2048,1024]{1,0:T(8,128)(2,1)}) %all-gather.20.cloned.1.call-update) | async-done | bytes 4194320 | tf_op jit(solution)/shard_map/all_gather | solution.py:169
  556.3 3.7 convolution_convert_fusion.3
  560.0 97.5 %while.29 = (s32[]{:T(128)}, f32[2048,1,64]{0,2,1:T(8,128)S(1)}, f32[2048,1,64]{0,2,1:T(8,128)}, f32[4,512,1,2,64]{1,0,4,3,2:T(4,128)}, s32[4]{0:T(128)S(1)}, /*...) while((s32[]{:T(128)}, f32[2048,1,64]{0,2,1:T(8,128)S(1)}, ...), condition=%wide.region_16.17_spmd.clone, body=%wide.region_14.16_spmd.clone.sunk | while | flops 1377500672 | bytes 71874800 | solution.py:206
  566.0 3.3 fusion.203
  569.3 3.0 fusion.200
  577.5 6.1 dynamic_update_slice.22
  589.5 4.3 fusion.203
  593.8 3.0 fusion.200
  602.1 6.1 dynamic_update_slice.22
  614.0 4.3 fusion.203
  618.4 3.0 fusion.200
  626.6 6.1 dynamic_update_slice.22
  638.6 4.3 fusion.203
  642.9 3.0 fusion.200
  651.2 6.1 dynamic_update_slice.22
  657.6 3.0 reshape.454
  668.5 4.6 fusion.120
  673.4 3.7 convolution_convert_fusion.11
  677.2 3.6 convolution_convert_fusion.8
  680.9 4.2 convolution_convert_fusion.9
  685.1 4.5 fusion.119
  689.7 9.2 add_convert_fusion
  700.2 7.1 convolution_convert_fusion
  715.8 20.8 %reduce-scatter.26.cloned.1.call-done = bf16[128,256]{1,0:T(8,128)(2,1)} async-done(((bf16[128,1024]{1,0:T(8,128)(2,1)}), bf16[128,256]{1,0:T(8,128)(2,1)}) %reduce-scatter.26.cloned.1.call-update) | async-done | bytes 65552 | tf_op jit(solution)/shard_map/reduce_scatter | solution.py:241
  738.1 21.4 %reduce-scatter.20.cloned.1.call-done = bf16[256,128]{1,0:T(8,128)(2,1)} async-done(((bf16[1024,128]{1,0:T(8,128)(2,1)}), bf16[256,128]{1,0:T(8,128)(2,1)}) %reduce-scatter.20.cloned.1.call-update) | async-done | bytes 65552 | tf_op jit(solution)/shard_map/reduce_scatter | solution.py:232
  761.0 90.5 %reduce-scatter.18.cloned.1.call-done = bf16[256,1024]{1,0:T(8,128)(2,1)} async-done(((bf16[2048,1024]{1,0:T(8,128)(2,1)}), bf16[256,1024]{1,0:T(8,128)(2,1)}) %reduce-scatter.18.cloned.1.call-update) | async-done | bytes 524304 | tf_op jit(solution)/shard_map/reduce_scatter | solution.py:219
  853.0 42.4 %all-reduce.4 = (f32[1024]{0:T(1024)}, f32[64]{0:T(128)}, f32[64]{0:T(128)}, f32[1024]{0:T(1024)}) all-reduce(f32[1024]{0:T(1024)S(1)} %get-tuple-element.207, f32[64]{0:T(128)S(1)} %get-tuple-element.205, f32[64]{0:T(128)S(1)} %get-tuple-element.203, f32[1024]{0:T(1024)S(1)} %copy-done.42), channel_id=1, replica_groups=mesh['dp'=4,'tensor'=8] {'dp','tensor'}, use_global_device_ids=true, to_apply=%region_22.23 | all-reduce | flops 2176 | bytes 17408 | tf_op jit(solution)/shard_map/psum | solution.py:254
  895.5 48.3 %reduce-scatter.14.cloned.1.call-done = bf16[256,1024]{1,0:T(8,128)(2,1)} async-done(((bf16[2048,1024]{1,0:T(8,128)(2,1)}), bf16[256,1024]{1,0:T(8,128)(2,1)}) %reduce-scatter.14.cloned.1.call-update) | async-done | bytes 524304 | tf_op jit(solution)/shard_map/reduce_scatter | solution.py:148
  (291 shorter events, 124.3 us)
Async XLA Ops:
  8.0 79.7 %all-gather.8.cloned.1.call-start = ((), (), s32[]{:S(2)}) async-start(), calls=%async_computation.11 | async-start | bytes 4718592 | tf_op jit(solution)/shard_map/all_gather | solution.py:95
  11.3 80.7 %copy-start.49 = (f32[64]{0:T(128)S(1)}, f32[64]{0:T(128)}, u32[]{:S(2)}) copy-start(f32[64]{0:T(128)} %param.27) | copy-start | bytes 772
  11.4 255.0 %reduce-scatter.12.cloned.1.call-start = ((), (), s32[]{:S(2)}) async-start(), calls=%async_computation.12 | async-start | bytes 4718592 | tf_op jit(solution)/shard_map/reduce_scatter | solution.py:138
  19.5 72.6 %copy-start.25 = (bf16[1024,64]{0,1:T(8,128)(2,1)}, bf16[1024,64]{0,1:T(8,128)(2,1)S(1)}, u32[]{:S(2)}) copy-start(bf16[1024,64]{0,1:T(8,128)(2,1)S(1)} %all_gather.35) | copy-start | bytes 393220
  25.3 70.4 %copy-start.23 = (bf16[1024,64]{0,1:T(8,128)(2,1)}, bf16[1024,64]{0,1:T(8,128)(2,1)S(1)}, u32[]{:S(2)}) copy-start(bf16[1024,64]{0,1:T(8,128)(2,1)S(1)} %all_gather.36) | copy-start | bytes 393220
  31.5 62.1 %copy-start.20 = (bf16[1024,128]{1,0:T(8,128)(2,1)}, bf16[1024,128]{1,0:T(8,128)(2,1)S(1)}, u32[]{:S(2)}) copy-start(bf16[1024,128]{1,0:T(8,128)(2,1)S(1)} %all_gather.34) | copy-start | bytes 786436
  37.6 56.0 %copy-start.53 = (f32[32]{0:T(128)}, f32[32]{0:T(128)S(1)}, u32[]{:S(2)}) copy-start(f32[32]{0:T(128)S(1)} %multiply_power_fusion) | copy-start | bytes 388
  37.8 55.8 %copy-start.33 = (f32[2048]{0:T(1024)}, f32[2048]{0:T(1024)S(1)}, u32[]{:S(2)}) copy-start(f32[2048]{0:T(1024)S(1)} %fusion.112) | copy-start | bytes 24580
  38.8 56.7 %copy-start.18 = (f32[2048,32]{0,1:T(8,128)}, f32[2048,32]{0,1:T(8,128)S(1)}, u32[]{:S(2)}) copy-start(f32[2048,32]{0,1:T(8,128)S(1)} %get-tuple-element.272) | copy-start | bytes 786436
  38.8 56.7 %copy-start.19 = (f32[2048,32]{0,1:T(8,128)}, f32[2048,32]{0,1:T(8,128)S(1)}, u32[]{:S(2)}) copy-start(f32[2048,32]{0,1:T(8,128)S(1)} %get-tuple-element.273) | copy-start | bytes 786436
  148.5 117.9 %copy-start.2 = (bf16[256,1024]{1,0:T(8,128)(2,1)S(1)}, bf16[256,1024]{1,0:T(8,128)(2,1)}, u32[]{:S(2)}) copy-start(bf16[256,1024]{1,0:T(8,128)(2,1)} %param.18) | copy-start | bytes 1572868
  148.5 119.2 %copy-start.37 = (f32[1024]{0:T(1024)S(1)}, f32[1024]{0:T(1024)}, u32[]{:S(2)}) copy-start(f32[1024]{0:T(1024)} %param.28) | copy-start | bytes 12292
  148.5 122.5 %all-gather.16.cloned.1.call-start = ((), (), s32[]{:S(2)}) async-start(), calls=%async_computation.16 | async-start | bytes 1474560 | tf_op jit(solution)/shard_map/all_gather | solution.py:84
  149.1 122.0 %all-gather.18.cloned.1.call-start = ((), (), s32[]{:S(2)}) async-start(), calls=%async_computation.18 | async-start | bytes 4718592 | tf_op jit(solution)/shard_map/all_gather | solution.py:153
  149.7 128.0 %all-gather.14.cloned.1.call-start = ((), (), s32[]{:S(2)}) async-start(), calls=%async_computation.15 | async-start | bytes 1474560 | tf_op jit(solution)/shard_map/all_gather | solution.py:83
  150.2 203.3 %all-gather.10.cloned.1.call-start = ((), (), s32[]{:S(2)}) async-start(), calls=%async_computation.13 | async-start | bytes 4718592 | tf_op jit(solution)/shard_map/all_gather | solution.py:143
  267.7 213.5 %copy-start.40 = (f32[256]{0:T(256)}, f32[256]{0:T(256)S(1)}, u32[]{:S(2)}) copy-start(f32[256]{0:T(256)S(1)} %fusion.115) | copy-start | bytes 3076
  269.8 101.3 %all-gather.12.cloned.1.call-start = ((), (), s32[]{:S(2)}) async-start(), calls=%async_computation.14 | async-start | bytes 1474560 | tf_op jit(solution)/shard_map/all_gather | solution.py:82
  270.5 208.5 %reduce-scatter.16.cloned.1.call-start = ((), (), s32[]{:S(2)}) async-start(), calls=%async_computation.19 | async-start | bytes 4718592 | tf_op jit(solution)/shard_map/reduce_scatter | solution.py:161
  371.1 11.0 %copy-start.57 = (bf16[1024,576]{0,1:T(8,128)(2,1)S(1)}, bf16[1024,576]{0,1:T(8,128)(2,1)}, u32[]{:S(2)}) copy-start(bf16[1024,576]{0,1:T(8,128)(2,1)} %all-gather.12.cloned.1.call-done) | copy-start | bytes 3538948
  391.0 88.1 %copy-start.6 = (bf16[256,1024]{1,0:T(8,128)(2,1)S(1)}, bf16[256,1024]{1,0:T(8,128)(2,1)}, u32[]{:S(2)}) copy-start(bf16[256,1024]{1,0:T(8,128)(2,1)} %reduce-scatter.12.cloned.1.call-done) | copy-start | bytes 1572868
  391.0 90.2 %copy-start.12 = (bf16[256,1024]{1,0:T(8,128)(2,1)S(1)}, bf16[256,1024]{1,0:T(8,128)(2,1)}, u32[]{:S(2)}) copy-start(bf16[256,1024]{1,0:T(8,128)(2,1)} %param.20) | copy-start | bytes 1572868
  391.0 165.3 %all-gather.20.cloned.1.call-start = ((), (), s32[]{:S(2)}) async-start(), calls=%async_computation.20 | async-start | bytes 4718592 | tf_op jit(solution)/shard_map/all_gather | solution.py:169
  481.2 8.9 copy-start.45
  483.5 224.0 %reduce-scatter.32.cloned.1.call-start = ((), (), s32[]{:S(2)}) async-start(), calls=%async_computation.28 | async-start | bytes 1474560 | tf_op jit(solution)/shard_map/reduce_scatter | solution.py:250
  490.1 219.2 %reduce-scatter.28.cloned.1.call-start = ((), (), s32[]{:S(2)}) async-start(), calls=%async_computation.26 | async-start | bytes 1474560 | tf_op jit(solution)/shard_map/reduce_scatter | solution.py:244
  497.2 214.0 %reduce-scatter.30.cloned.1.call-start = ((), (), s32[]{:S(2)}) async-start(), calls=%async_computation.27 | async-start | bytes 1474560 | tf_op jit(solution)/shard_map/reduce_scatter | solution.py:247
  503.9 209.2 %reduce-scatter.24.cloned.1.call-start = ((), (), s32[]{:S(2)}) async-start(), calls=%async_computation.24 | async-start | bytes 163840 | tf_op jit(solution)/shard_map/reduce_scatter | solution.py:238
  657.6 6.8 copy-start.36
  657.6 6.8 copy-start.5
  657.6 6.8 copy-start.28
  657.6 6.8 copy-start.52
  673.4 41.1 %reduce-scatter.22.cloned.1.call-start = ((), (), s32[]{:S(2)}) async-start(), calls=%async_computation.23 | async-start | bytes 163840 | tf_op jit(solution)/shard_map/reduce_scatter | solution.py:235
  677.1 59.5 %reduce-scatter.26.cloned.1.call-start = ((), (), s32[]{:S(2)}) async-start(), calls=%async_computation.25 | async-start | bytes 327680 | tf_op jit(solution)/shard_map/reduce_scatter | solution.py:241
  680.9 78.7 %reduce-scatter.20.cloned.1.call-start = ((), (), s32[]{:S(2)}) async-start(), calls=%async_computation.22 | async-start | bytes 327680 | tf_op jit(solution)/shard_map/reduce_scatter | solution.py:232
  689.7 161.8 %reduce-scatter.18.cloned.1.call-start = ((), (), s32[]{:S(2)}) async-start(), calls=%async_computation.21 | async-start | bytes 4718592 | tf_op jit(solution)/shard_map/reduce_scatter | solution.py:219
  699.0 244.8 %reduce-scatter.14.cloned.1.call-start = ((), (), s32[]{:S(2)}) async-start(), calls=%async_computation.17 | async-start | bytes 4718592 | tf_op jit(solution)/shard_map/reduce_scatter | solution.py:148
  707.3 144.2 %copy-start.3 = (bf16[256,1024]{1,0:T(8,128)(2,1)S(1)}, bf16[256,1024]{1,0:T(8,128)(2,1)}, u32[]{:S(2)}) copy-start(bf16[256,1024]{1,0:T(8,128)(2,1)} %param.18) | copy-start | bytes 1572868
  707.3 144.2 %copy-start.39 = (f32[1024]{0:T(1024)S(1)}, f32[1024]{0:T(1024)}, u32[]{:S(2)}) copy-start(f32[1024]{0:T(1024)} %param.21) | copy-start | bytes 12292
  707.3 144.2 %copy-start.44 = (f32[256]{0:T(256)S(1)}, f32[256]{0:T(256)}, u32[]{:S(2)}) copy-start(f32[256]{0:T(256)} %copy-done.43) | copy-start | bytes 3076
  707.3 145.7 %copy-start.42 = (f32[1024]{0:T(1024)S(1)}, f32[1024]{0:T(1024)}, u32[]{:S(2)}) copy-start(f32[1024]{0:T(1024)} %get-tuple-element.201) | copy-start | bytes 12292
  707.3 188.2 %copy-start.48 = (f32[256]{0:T(256)S(1)}, f32[256]{0:T(256)}, u32[]{:S(2)}) copy-start(f32[256]{0:T(256)} %copy-done.47) | copy-start | bytes 3076
  707.3 236.5 %copy-start.7 = (bf16[256,1024]{1,0:T(8,128)(2,1)S(1)}, bf16[256,1024]{1,0:T(8,128)(2,1)}, u32[]{:S(2)}) copy-start(bf16[256,1024]{1,0:T(8,128)(2,1)} %reduce-scatter.12.cloned.1.call-done) | copy-start | bytes 1572868
  707.3 236.5 %copy-start.13 = (bf16[256,1024]{1,0:T(8,128)(2,1)S(1)}, bf16[256,1024]{1,0:T(8,128)(2,1)}, u32[]{:S(2)}) copy-start(bf16[256,1024]{1,0:T(8,128)(2,1)} %param.20) | copy-start | bytes 1572868
  707.3 236.4 %copy-start.14 = (bf16[256,1024]{1,0:T(8,128)(2,1)S(1)}, bf16[256,1024]{1,0:T(8,128)(2,1)}, u32[]{:S(2)}) copy-start(bf16[256,1024]{1,0:T(8,128)(2,1)} %reduce-scatter.16.cloned.1.call-done) | copy-start | bytes 1572868
  707.4 236.4 %copy-start.38 = (f32[1024]{0:T(1024)S(1)}, f32[1024]{0:T(1024)}, u32[]{:S(2)}) copy-start(f32[1024]{0:T(1024)} %param.28) | copy-start | bytes 12292
  707.4 236.4 %copy-start.41 = (f32[256]{0:T(256)S(1)}, f32[256]{0:T(256)}, u32[]{:S(2)}) copy-start(f32[256]{0:T(256)} %copy-done.40) | copy-start | bytes 3076
  707.4 236.4 %copy-start.46 = (f32[256]{0:T(256)S(1)}, f32[256]{0:T(256)}, u32[]{:S(2)}) copy-start(f32[256]{0:T(256)} %copy-done.45) | copy-start | bytes 3076
  (30 other events, 99.6 us)
Sparse Core Ops, SparseCore 0:
  11.5 76.0 all-gather.7
  148.6 117.6 reduce-scatter.11
  391.1 87.8 reduce-scatter.15
Sparse Core Ops, SparseCore 1:
  150.5 15.7 all-gather.15
  168.3 91.5 all-gather.17
  261.2 16.3 all-gather.13
  280.6 72.9 all-gather.9
  355.2 15.8 all-gather.11
  483.6 72.7 all-gather.19
  558.7 24.1 reduce-scatter.31
  585.4 25.6 reduce-scatter.27
  613.5 25.6 reduce-scatter.29
  673.4 18.0 reduce-scatter.23
  694.4 19.6 reduce-scatter.21
  716.6 19.9 reduce-scatter.25
  739.5 20.0 reduce-scatter.19
  763.6 87.8 reduce-scatter.17
  855.2 88.6 reduce-scatter.13
where the time goes:
time: 960 us; the launch traced here: 955 us
  waiting for transfers between devices  575 us (60%)
  matrix products  169 us (18%)
  other arithmetic  70.9 us (7%)
  blocking collectives  67.2 us (7%)
  local copies, waits for them, and re-layouts  38.2 us (4%)
  between operations  17 us (2%)
  loops' own time  16.4 us (2%)
    reduce_scatter x1, waiting for transfers between devices, per_device(): lax.psum_scatter(mult(attn_heads, o_mat).astype(jnp.bfloat16), 'tensor',...  116 us
    reduce_scatter x1, waiting for transfers between devices, per_device(): lax.psum_scatter((mult_right(grad_query_low, q_mat) + mult_right(grad_key...  90.5 us
    reduce_scatter x1, waiting for transfers between devices, per_device(): lax.psum_scatter((mult_right(grad_gate, g_mat) + mult_right(grad_up, u_ma...  88 us
    all_gather x1, waiting for transfers between devices, per_device(): lax.all_gather(xf_full.astype(jnp.bfloat16), 'tensor', axis=0, tiled=True)  75.9 us
    all_gather x1, waiting for transfers between devices, per_device(): lax.all_gather(grad_hidden.astype(jnp.bfloat16), 'tensor', axis=0, tiled=...  52.3 us
    all_gather x1, waiting for transfers between devices, per_device(): lax.all_gather(xa_full.astype(jnp.bfloat16), 'tensor', axis=0, tiled=True)  48.9 us
    reduce_scatter x1, waiting for transfers between devices, per_device(): lax.psum_scatter(mult(activation, d_mat).astype(jnp.bfloat16), 'tensor',...  48.3 us
    psum x1, blocking collectives, per_device(): lax.psum((attn_gain_part, query_gain_part, key_gain_part, ffn_gain_part),...  42.4 us
  transfers between devices with their start and end apart: 18, of which 10 were waited for; matrix products, arithmetic and copies ran while one was open for 20% of the time, Pallas kernels for 0%

commit v1 on v0

v1 whole, which is shorter than its diff:
```python
import functools

import jax
import jax.numpy as jnp
from jax import lax
from jax.experimental import pallas as pl
from jax.experimental.pallas import tpu as pltpu
from jax.sharding import Mesh
from jax.sharding import PartitionSpec as P

EPSILON = 1e-05
ROPE_BASE = 1000000.0
BLOCK = 256
F32 = jnp.float32
BF16 = jnp.bfloat16
VMEM_LIMIT = 40 * 1024 * 1024


def nn(a, b):
    return lax.dot_general(a, b, (((1,), (0,)), ((), ())), preferred_element_type=F32)


def nt(a, b):
    return lax.dot_general(a, b, (((1,), (1,)), ((), ())), preferred_element_type=F32)


def tn(a, b):
    return lax.dot_general(a, b, (((0,), (0,)), ((), ())), preferred_element_type=F32)


def exact_nn(a, b):
    return lax.dot_general(
        a, b, (((1,), (0,)), ((), ())), preferred_element_type=F32, precision=lax.Precision.HIGHEST
    )


def params(**more):
    return pltpu.CompilerParams(vmem_limit_bytes=VMEM_LIMIT, **more)


def swap(v, axes, bit):
    size = lax.axis_size(axes)
    return lax.ppermute(v, axes, [(i, i ^ bit) for i in range(size)])


def line_gather(v, axis):
    size = lax.axis_size(axis)
    me = lax.axis_index(axis)
    from_left, from_right = [], []
    left = right = v
    for step in range(1, size):
        left = lax.ppermute(left, axis, [(i, i + 1) for i in range(step - 1, size - 1)])
        right = lax.ppermute(right, axis, [(i, i - 1) for i in range(1, size - step + 1)])
        from_left.append(left)
        from_right.append(right)
    slots = [v]
    for d in range(1, size):
        slots.append(jnp.where(me + d < size, from_right[d - 1], from_left[size - d - 1]))
    return slots


def line_scatter(parts, axis):
    size = lax.axis_size(axis)
    left = right = None
    for m in range(size - 1, 0, -1):
        up, down = parts[m].astype(F32), parts[size - m].astype(F32)
        if left is not None:
            up, down = up + left.astype(F32), down + right.astype(F32)
        left = lax.ppermute(up.astype(BF16), axis, [(i, i + 1) for i in range(size - m)])
        right = lax.ppermute(down.astype(BF16), axis, [(i, i - 1) for i in range(m, size)])
    return parts[0].astype(F32) + left.astype(F32) + right.astype(F32)


def quads(v):
    return jnp.split(v, 4, axis=-1)


def flip_y(v):
    a, b = jnp.split(v, 2, axis=-1)
    return jnp.concatenate([b, a], axis=-1)


def own_order(v, y, c):
    runs = lax.axis_size("r")
    if runs > 1:
        lead = v.shape[:-1]
        v = jnp.moveaxis(v.reshape(lead + (runs, 4, -1)), -3, -2).reshape(lead + (-1,))
    return exchange(v, y, c)


def exchange(v, y, c):
    a = quads(v)
    a = [jnp.where(c == 0, a[e], a[e ^ 1]) for e in range(4)]
    return jnp.concatenate([jnp.where(y == 0, a[e], a[e ^ 2]) for e in range(4)], axis=-1)


def arrays_order(v, y, c):
    v = exchange(v, y, c)
    runs = lax.axis_size("r")
    if runs > 1:
        lead = v.shape[:-1]
        v = jnp.moveaxis(v.reshape(lead + (4, runs, -1)), -2, -3).reshape(lead + (-1,))
    return v


def gather_runs(v):
    return lax.all_gather(v, "r", axis=v.ndim - 1, tiled=True) if lax.axis_size("r") > 1 else v


def scatter_runs(v):
    if lax.axis_size("r") == 1:
        return v
    return lax.psum_scatter(
        v.astype(BF16), "r", scatter_dimension=v.ndim - 1, tiled=True
    ).astype(F32)


def total_of(v):
    if lax.axis_size("r") > 1:
        v = lax.psum(v, "r")
    for axis in ("c", "x", "y", "z"):
        bit = 1
        while bit < lax.axis_size(axis):
            v = v + swap(v, axis, bit)
            bit *= 2
    return v


def gather_heads(w):
    slots = jnp.stack(line_gather(w, "z"))
    near = [slots] + [swap(slots, ("y", "x"), bit) for bit in (1, 2, 3)]
    far = [swap(v, "c", 1) for v in near]
    rows = [
        jnp.concatenate([near[ex], far[ex], near[ex + 2], far[ex + 2]], axis=-1) for ex in (0, 1)
    ]
    return jnp.concatenate(rows, axis=0)


def scatter_heads(g):
    e0, e1, e2, e3 = quads(g)
    from_core = swap(jnp.concatenate([e1, e3], axis=-1), "c", 1)
    both = (jnp.concatenate([e0, e2], axis=-1).astype(F32) + from_core.astype(F32)).astype(BF16)
    half, cols = g.shape[0] // 2, both.shape[-1] // 2
    mine = both[:half, :, :cols].astype(F32)
    mine = mine + swap(both[half:, :, :cols], ("y", "x"), 1).astype(F32)
    mine = mine + swap(both[:half, :, cols:], ("y", "x"), 2).astype(F32)
    mine = mine + swap(both[half:, :, cols:], ("y", "x"), 3).astype(F32)
    return line_scatter([mine[d] for d in range(half)], "z")


def gather_tokens(v):
    around = [swap(v, ("y", "x"), bit) for bit in (1, 2, 3)]
    return jnp.concatenate([v, around[0], flip_y(around[1]), flip_y(around[2])], axis=0)


def scatter_tokens(parts):
    near = swap(parts[1], ("y", "x"), 1).astype(F32) + parts[0]
    far = swap(parts[2], ("y", "x"), 2).astype(F32) + swap(parts[3], ("y", "x"), 3).astype(F32)
    return near + flip_y(far)


def lanes_of(shape):
    return lax.broadcasted_iota(jnp.int32, shape, len(shape) - 1)


def head_sums(v, head):
    width = v.shape[-1]
    row = lax.broadcasted_iota(jnp.int32, (width, width), 0) // head
    col = lax.broadcasted_iota(jnp.int32, (width, width), 1) // head
    return exact_nn(v, jnp.where(row == col, 1.0, 0.0).astype(F32))


def swap_halves(v, head):
    width, half = v.shape[-1], head // 2
    low = (lanes_of(v.shape) % head) < half
    return jnp.where(low, pltpu.roll(v, width - half, 1), pltpu.roll(v, half, 1))


def qkv_kernel(head, order, xa, w, cosine, sine, q_gain, k_gain, low, kept):
    del order
    proj = nt(xa[...], w[0])
    width = 2 * head
    kept[0] = proj

    def prep(v, gain):
        factor = lax.rsqrt(head_sums(v * v, head) * (1.0 / head) + EPSILON)
        n = v * factor * gain
        return n * cosine[...] + swap_halves(n, head) * sine[...]

    q = prep(proj[:, :width], q_gain[...])
    kv = proj[:, width:]
    k = prep(kv, k_gain[...])
    low[0, :, :width] = q.astype(BF16)
    low[0, :, width:] = jnp.where(lanes_of(kv.shape) < head, k, kv).astype(BF16)


def qkv_call(order, xa, w, cosine, sine, q_gain, k_gain, head):
    blocks, n, d = w.shape
    rows = xa.shape[0]
    whole = lambda shape: pl.BlockSpec(shape, lambda j, order: (0,) * len(shape))
    return pl.pallas_call(
        functools.partial(qkv_kernel, head),
        grid_spec=pltpu.PrefetchScalarGridSpec(
            num_scalar_prefetch=1,
            grid=(blocks,),
            in_specs=[
                whole((rows, d)),
                pl.BlockSpec((1, n, d), lambda j, order: (order[j], 0, 0)),
                whole((rows, 2 * head)),
                whole((rows, 2 * head)),
                whole((1, 2 * head)),
                whole((1, 2 * head)),
            ],
            out_specs=[
                pl.BlockSpec((1, rows, n), lambda j, order: (j, 0, 0)),
                pl.BlockSpec((1, rows, n), lambda j, order: (j, 0, 0)),
            ],
        ),
        out_shape=[
            jax.ShapeDtypeStruct((blocks, rows, n), BF16),
            jax.ShapeDtypeStruct((blocks, rows, n), F32),
        ],
        compiler_params=params(),
        cost_estimate=pl.CostEstimate(
            flops=2 * blocks * rows * n * d, bytes_accessed=2 * blocks * n * d, transcendentals=0
        ),
        name="qkv",
    )(order, xa, w, cosine, sine, q_gain, k_gain)


def stack_heads(v, head, scale=None):
    out = jnp.concatenate([v[:, :head], v[:, head : 2 * head]], axis=0)
    return out if scale is None else (out.astype(F32) * scale).astype(BF16)


def unstack(v_t):
    rows = v_t.shape[1] // 2
    return jnp.concatenate([v_t[:, :rows], v_t[:, rows:]], axis=0).T


def attend_kernel(head, first, qkv, start, context, log_total, turned):
    b = pl.program_id(0)
    width = 2 * head

    @pl.when(b == 0)
    def _():
        kv_t = qkv[:, width:].astype(F32).T
        row = lax.broadcasted_iota(jnp.int32, kv_t.shape, 0)
        turned[...] = jnp.where(row < head, 1.0, kv_t).astype(BF16)

    q2 = stack_heads(qkv[pl.ds(b * BLOCK, BLOCK), :width], head, head**-0.5)
    begin = start[0]
    key = lax.broadcasted_iota(jnp.int32, (BLOCK, 2 * BLOCK), 0)

    def block(j, acc, diagonal):
        s = nt(qkv[pl.ds(j * BLOCK, BLOCK), width : width + head], q2)
        allowed = key >= begin - j * BLOCK
        if diagonal:
            row = lanes_of((BLOCK, 2 * BLOCK)) % BLOCK
            allowed = allowed & (key <= row)
        p = jnp.where(allowed, jnp.exp(s), 0.0)
        return acc + nn(turned[:, pl.ds(j * BLOCK, BLOCK)], p.astype(BF16))

    acc = jnp.zeros((width, 2 * BLOCK), F32)
    acc = lax.fori_loop(first[b], b, lambda j, acc: block(j, acc, False), acc)
    acc = block(b, acc, True)
    total = acc[:1]
    context[...] = unstack(acc[head:] / total).astype(BF16)
    log_total[0] = jnp.log(total)


def attend_call(first, qkv, start, head):
    rows, n = qkv.shape
    blocks = rows // BLOCK
    return pl.pallas_call(
        functools.partial(attend_kernel, head),
        grid_spec=pltpu.PrefetchScalarGridSpec(
            num_scalar_prefetch=1,
            grid=(blocks,),
            in_specs=[
                pl.BlockSpec((rows, n), lambda b, first: (0, 0)),
                pl.BlockSpec((1, 1, 2 * BLOCK), lambda b, first: (b, 0, 0)),
            ],
            out_specs=[
                pl.BlockSpec((BLOCK, 2 * head), lambda b, first: (b, 0)),
                pl.BlockSpec((1, 1, 2 * BLOCK), lambda b, first: (b, 0, 0)),
            ],
            scratch_shapes=[pltpu.VMEM((2 * head, rows), BF16)],
        ),
        out_shape=[
            jax.ShapeDtypeStruct((rows, 2 * head), BF16),
            jax.ShapeDtypeStruct((blocks, 1, 2 * BLOCK), F32),
        ],
        compiler_params=params(),
        cost_estimate=pl.CostEstimate(
            flops=8 * rows * rows * head, bytes_accessed=3 * rows * n, transcendentals=rows * rows
        ),
        name="attend",
    )(first, qkv, start)


def attend_back_kernel(
    head, first, qkv, context, d_context, start, log_total, out, turned, d_key, d_value
):
    b = pl.program_id(0)
    width = 2 * head

    @pl.when(b == 0)
    def _():
        turned[...] = qkv[:, width:].astype(F32).T.astype(BF16)
        d_key[...] = jnp.zeros_like(d_key)
        d_value[...] = jnp.zeros_like(d_value)

    scale = head**-0.5
    q2 = stack_heads(qkv[pl.ds(b * BLOCK, BLOCK), :width], head, scale)
    g = d_context[...]
    g2 = stack_heads(g, head)
    begin = start[0]
    log_sum = log_total[0]
    picks = jnp.where(
        lanes_of((8, width)) // head == lax.broadcasted_iota(jnp.int32, (8, width), 0), 1.0, 0.0
    ).astype(F32)
    delta = lax.dot_general(
        picks,
        g.astype(F32) * context[...].astype(F32),
        (((1,), (1,)), ((), ())),
        preferred_element_type=F32,
        precision=lax.Precision.HIGHEST,
    )
    delta = jnp.concatenate([delta[0:1], delta[1:2]], axis=1)
    key = lax.broadcasted_iota(jnp.int32, (BLOCK, 2 * BLOCK), 0)

    def block(j, acc, diagonal):
        at = pl.ds(j * BLOCK, BLOCK)
        s = nt(qkv[at, width : width + head], q2)
        allowed = key >= begin - j * BLOCK
        if diagonal:
            row = lanes_of((BLOCK, 2 * BLOCK)) % BLOCK
            allowed = allowed & (key <= row)
        p = jnp.where(allowed, jnp.exp(s - log_sum), 0.0)
        d_p = nt(qkv[at, width + head :], g2)
        d_s = (p * (d_p - delta)).astype(BF16)
        d_value[at, :] += nn(p.astype(BF16), g2)
        d_key[at, :] += nn(d_s, q2)
        return acc + nn(turned[:, at], d_s)

    acc = jnp.zeros((width, 2 * BLOCK), F32)
    acc = lax.fori_loop(first[b], b, lambda j, acc: block(j, acc, False), acc)
    acc = block(b, acc, True)
    out[pl.ds(b * BLOCK, BLOCK), :width] = (unstack(acc[:head]) * scale).astype(BF16)

    @pl.when(b == pl.num_programs(0) - 1)
    def _():
        out[:, width:] = jnp.concatenate([d_key[...], d_value[...]], axis=1).astype(BF16)


def attend_back_call(first, qkv, context, d_context, start, log_total, head):
    rows, n = qkv.shape
    blocks = rows // BLOCK
    per_block = pl.BlockSpec((BLOCK, 2 * head), lambda b, first: (b, 0))
    per_row = pl.BlockSpec((1, 1, 2 * BLOCK), lambda b, first: (b, 0, 0))
    return pl.pallas_call(
        functools.partial(attend_back_kernel, head),
        grid_spec=pltpu.PrefetchScalarGridSpec(
            num_scalar_prefetch=1,
            grid=(blocks,),
            in_specs=[
                pl.BlockSpec((rows, n), lambda b, first: (0, 0)),
                per_block,
                per_block,
                per_row,
                per_row,
            ],
            out_specs=pl.BlockSpec((rows, n), lambda b, first: (0, 0)),
            scratch_shapes=[
                pltpu.VMEM((2 * head, rows), BF16),
                pltpu.VMEM((rows, head), F32),
                pltpu.VMEM((rows, head), F32),
            ],
        ),
        out_shape=jax.ShapeDtypeStruct((rows, n), BF16),
        compiler_params=params(),
        cost_estimate=pl.CostEstimate(
            flops=20 * rows * rows * head, bytes_accessed=6 * rows * n, transcendentals=rows * rows
        ),
        name="attend_back",
    )(first, qkv, context, d_context, start, log_total)


def project_kernel(order, context, w, x, gain, hidden, normed):
    del order
    j = pl.program_id(0)

    @pl.when(j == 0)
    def _():
        hidden[...] = x[...]

    hidden[...] += nn(context[0], w[0])

    @pl.when(j == pl.num_programs(0) - 1)
    def _():
        h = hidden[...]
        factor = lax.rsqrt(jnp.mean(h * h, axis=-1, keepdims=True) + EPSILON)
        normed[...] = (h * factor * gain[...]).astype(BF16)


def project_call(order, context, w, x, gain):
    blocks, n, d = w.shape
    rows = x.shape[0]
    whole = lambda shape: pl.BlockSpec(shape, lambda j, order: (0,) * len(shape))
    return pl.pallas_call(
        project_kernel,
        grid_spec=pltpu.PrefetchScalarGridSpec(
            num_scalar_prefetch=1,
            grid=(blocks,),
            in_specs=[
                pl.BlockSpec((1, rows, n), lambda j, order: (j, 0, 0)),
                pl.BlockSpec((1, n, d), lambda j, order: (order[j], 0, 0)),
                whole((rows, d)),
                whole((1, d)),
            ],
            out_specs=[whole((rows, d)), whole((rows, d))],
        ),
        out_shape=[jax.ShapeDtypeStruct((rows, d), F32), jax.ShapeDtypeStruct((rows, d), BF16)],
        compiler_params=params(),
        cost_estimate=pl.CostEstimate(
            flops=2 * blocks * rows * n * d, bytes_accessed=2 * blocks * n * d, transcendentals=0
        ),
        name="project",
    )(order, context, w, x, gain)


def project_back_kernel(order, context, w, d_hidden, d_context, grad):
    del order
    low = d_hidden[...]
    d_context[0] = nt(low, w[0]).astype(BF16)
    grad[0] = tn(context[0], low).astype(BF16)


def project_back_call(order, context, w, d_hidden):
    blocks, n, d = w.shape
    rows = d_hidden.shape[0]
    by_block = pl.BlockSpec((1, rows, n), lambda j, order: (j, 0, 0))
    by_order = pl.BlockSpec((1, n, d), lambda j, order: (order[j], 0, 0))
    return pl.pallas_call(
        project_back_kernel,
        grid_spec=pltpu.PrefetchScalarGridSpec(
            num_scalar_prefetch=1,
            grid=(blocks,),
            in_specs=[by_block, by_order, pl.BlockSpec((rows, d), lambda j, order: (0, 0))],
            out_specs=[by_block, by_order],
        ),
        out_shape=[
            jax.ShapeDtypeStruct((blocks, rows, n), BF16),
            jax.ShapeDtypeStruct((blocks, n, d), BF16),
        ],
        compiler_params=params(),
        cost_estimate=pl.CostEstimate(
            flops=4 * blocks * rows * n * d, bytes_accessed=4 * blocks * n * d, transcendentals=0
        ),
        name="project_back",
    )(order, context, w, d_hidden)


def qkv_back_kernel(
    head, order, grads, kept, xa, w, cosine, sine, q_gain, k_gain, d_xa, d_w, q_part, k_part
):
    del order
    j = pl.program_id(0)
    width = 2 * head

    @pl.when(j == 0)
    def _():
        d_xa[...] = jnp.zeros_like(d_xa)
        q_part[...] = jnp.zeros_like(q_part)
        k_part[...] = jnp.zeros_like(k_part)

    def back(g, v, gain):
        e = g * cosine[...] - swap_halves(g, head) * sine[...]
        m = lax.rsqrt(head_sums(v * v, head) * (1.0 / head) + EPSILON)
        u = gain * e
        mean = head_sums(u * v, head) * (1.0 / head)
        return m * u - v * (m * m * m * mean), jnp.sum(e * v * m, axis=0, keepdims=True)

    g, v = grads[0].astype(F32), kept[0]
    d_q, part = back(g[:, :width], v[:, :width], q_gain[...])
    q_part[...] += part
    d_k, part = back(g[:, width:], v[:, width:], k_gain[...])
    k_part[...] += part
    d_kv = jnp.where(lanes_of(d_k.shape) < head, d_k, g[:, width:])
    low = jnp.concatenate([d_q, d_kv], axis=1).astype(BF16)
    d_xa[...] += nn(low, w[0])
    d_w[0] = tn(low, xa[...]).astype(BF16)


def qkv_back_call(order, grads, kept, xa, w, cosine, sine, q_gain, k_gain, head):
    blocks, n, d = w.shape
    rows = xa.shape[0]
    whole = lambda shape: pl.BlockSpec(shape, lambda j, order: (0,) * len(shape))
    by_block = pl.BlockSpec((1, rows, n), lambda j, order: (j, 0, 0))
    by_order = pl.BlockSpec((1, n, d), lambda j, order: (order[j], 0, 0))
    lane = (1, 2 * head)
    return pl.pallas_call(
        functools.partial(qkv_back_kernel, head),
        grid_spec=pltpu.PrefetchScalarGridSpec(
            num_scalar_prefetch=1,
            grid=(blocks,),
            in_specs=[
                by_block,
                by_block,
                whole((rows, d)),
                by_order,
                whole((rows, 2 * head)),
                whole((rows, 2 * head)),
                whole(lane),
                whole(lane),
            ],
            out_specs=[whole((rows, d)), by_order, whole(lane), whole(lane)],
        ),
        out_shape=[
            jax.ShapeDtypeStruct((rows, d), F32),
            jax.ShapeDtypeStruct((blocks, n, d), BF16),
            jax.ShapeDtypeStruct(lane, F32),
            jax.ShapeDtypeStruct(lane, F32),
        ],
        compiler_params=params(),
        cost_estimate=pl.CostEstimate(
            flops=4 * blocks * rows * n * d, bytes_accessed=4 * blocks * n * d, transcendentals=0
        ),
        name="qkv_back",
    )(order, grads, kept, xa, w, cosine, sine, q_gain, k_gain)


def norm_factor(v):
    return lax.rsqrt(jnp.mean(v * v, axis=-1, keepdims=True) + EPSILON)


def norm_back(v, factor, gain, grad):
    u = gain * grad
    part = jnp.sum(grad * v * factor, axis=0)
    mean = jnp.mean(u * v, axis=-1, keepdims=True)
    return factor * u - v * (factor * factor * factor * mean), part


def per_device(
    tokens,
    segment_ids,
    cotangent,
    attn_gain,
    query_weight,
    key_weight,
    value_weight,
    output_weight,
    query_gain,
    key_gain,
    ffn_gain,
    gate_weight,
    up_weight,
    down_weight,
):
    y, c = lax.axis_index("y"), lax.axis_index("c")
    z, x_at = lax.axis_index("z"), lax.axis_index("x")
    z_size = lax.axis_size("z")
    head = query_gain.shape[0]
    rows = tokens.shape[0]
    nq, nk = query_weight.shape[1], key_weight.shape[1]

    qkv_w = gather_heads(
        gather_runs(jnp.concatenate([query_weight.T, key_weight.T, value_weight.T], axis=0))
    )
    out_w = gather_heads(gather_runs(output_weight))
    ffn = gather_runs(jnp.stack([gate_weight.T, up_weight.T, down_weight]))
    units = ffn.shape[1] // 2
    keep = jnp.where(y == 0, ffn[:, :units], ffn[:, units:])
    give = jnp.where(y == 0, ffn[:, units:], ffn[:, :units])
    ffn = jnp.concatenate([keep, swap(give, "y", 1)], axis=-1)
    near = jnp.concatenate(line_gather(ffn, "z"), axis=1)
    far = swap(near, "c", 1)
    a, b = jnp.split(near, 2, axis=-1)
    a_far, b_far = jnp.split(far, 2, axis=-1)
    ffn_w = jnp.concatenate([a, a_far, b, b_far], axis=-1)
    gate_w, up_w, down_w = ffn_w[0], ffn_w[1], ffn_w[2]

    segment = segment_ids[0]
    total_rows = segment.shape[0]
    index = jnp.arange(total_rows, dtype=jnp.int32)
    opens = jnp.concatenate([jnp.ones((1,), dtype=jnp.bool_), segment[1:] != segment[:-1]])
    begin = lax.cummax(jnp.where(opens, index, 0), axis=0)
    blocks = total_rows // BLOCK
    first = begin[::BLOCK] // BLOCK
    by_block = begin.reshape(blocks, 1, BLOCK)
    start = jnp.concatenate([by_block, by_block], axis=2)
    here = lax.axis_index(("z", "x")) * rows
    position = lax.dynamic_slice_in_dim(index - begin, here, rows).astype(F32)
    inverse = ROPE_BASE ** (-(jnp.arange(head // 2, dtype=F32) * 2.0) / head)
    angle = position[:, None] * inverse[None, :]
    cos_half, sin_half = jnp.cos(angle), jnp.sin(angle)
    cosine = jnp.concatenate([cos_half] * 4, axis=1)
    sine = jnp.concatenate([-sin_half, sin_half] * 2, axis=1)
    slots = jnp.arange(z_size, dtype=jnp.int32)
    order = jnp.stack([(slots - z) % z_size + z_size * x_at, (slots - z) % z_size + z_size * (1 - x_at)], axis=1)
    order = order.reshape(-1).astype(jnp.int32)

    x = own_order(tokens, y, c).astype(F32)
    grad_low = own_order(cotangent, y, c)
    grad_out = grad_low.astype(F32)
    gain_a = own_order(attn_gain[None], y, c)
    gain_f = own_order(ffn_gain[None], y, c)
    gain_q = jnp.concatenate([query_gain, query_gain])[None]
    gain_k = jnp.concatenate([key_gain, key_gain])[None]

    x_factor = norm_factor(x)
    xa = (x * x_factor * gain_a).astype(BF16)
    low, kept = qkv_call(order, xa, qkv_w, cosine, sine, gain_q, gain_k, head)

    def to_heads(v):
        return lax.all_to_all(v, ("z", "x"), 0, 0, tiled=True)

    qkv = to_heads(low).reshape(total_rows, nq + 2 * nk)
    context, log_total = attend_call(first, qkv, start, head)
    context_rows = to_heads(context.reshape(-1, rows, nq))
    hidden, xf = project_call(order, context_rows, out_w, x, gain_f)

    xf_all = gather_tokens(xf)
    dy_all = gather_tokens(grad_low)
    gate_pre = nt(xf_all, gate_w)
    up_pre = nt(xf_all, up_w)
    gate_sig = jax.nn.sigmoid(gate_pre)
    silu = gate_pre * gate_sig
    activation = (silu * up_pre).astype(BF16)
    d_act = nt(dy_all, down_w).astype(BF16).astype(F32)
    d_gate = (d_act * up_pre * (gate_sig * (1.0 + gate_pre * (1.0 - gate_sig)))).astype(BF16)
    d_up = (d_act * silu).astype(BF16)

    def rows_of(v, e):
        return v[e * rows : (e + 1) * rows]

    d_xf_parts = [
        nn(rows_of(d_gate, e), gate_w) + nn(rows_of(d_up, e), up_w) for e in range(4)
    ]
    d_xf = scatter_tokens([d_xf_parts[0]] + [v.astype(BF16) for v in d_xf_parts[1:]])
    ffn_parts = [nn(rows_of(activation, e), down_w) for e in range(4)]
    ffn_out = scatter_tokens([ffn_parts[0]] + [v.astype(BF16) for v in ffn_parts[1:]])
    block_out = arrays_order((hidden + ffn_out).astype(BF16), y, c)

    h_back, ffn_gain_part = norm_back(hidden, norm_factor(hidden), gain_f, d_xf)
    d_hidden = grad_out + h_back
    d_context_rows, out_grad = project_back_call(
        order, context_rows, out_w, d_hidden.astype(BF16)
    )
    d_context = to_heads(d_context_rows).reshape(total_rows, nq)
    d_qkv = attend_back_call(first, qkv, context, d_context, start, log_total, head)
    d_qkv_rows = to_heads(d_qkv.reshape(-1, rows, nq + 2 * nk))
    d_xa, qkv_grad, q_part, k_part = qkv_back_call(
        order, d_qkv_rows, kept, xa, qkv_w, cosine, sine, gain_q, gain_k, head
    )
    x_back, attn_gain_part = norm_back(x, x_factor, gain_a, d_xa)
    input_grad = arrays_order((d_hidden + x_back).astype(BF16), y, c)

    ffn_grad = jnp.stack([tn(d_gate, xf_all), tn(d_up, xf_all), tn(activation, dy_all)])
    e0, e1, e2, e3 = quads(ffn_grad.astype(BF16))
    from_core = swap(jnp.concatenate([e1, e3], axis=-1), "c", 1)
    both = jnp.concatenate([e0, e2], axis=-1).astype(F32) + from_core.astype(F32)
    both = both.astype(BF16)
    mine = line_scatter(
        [both[:, d * units : (d + 1) * units] for d in range(z_size)], "z"
    )
    own, other = jnp.split(mine, 2, axis=-1)
    other = swap(other.astype(BF16), "y", 1).astype(F32)
    ffn_grad = jnp.concatenate(
        [jnp.where(y == 0, own, other), jnp.where(y == 0, other, own)], axis=1
    )
    ffn_grad = scatter_runs(ffn_grad)
    out_grad = scatter_runs(scatter_heads(out_grad))
    qkv_grad = scatter_runs(scatter_heads(qkv_grad))

    d = x.shape[1]
    gains = total_of(
        jnp.concatenate(
            [
                arrays_order(attn_gain_part[None], y, c)[0],
                arrays_order(ffn_gain_part[None], y, c)[0],
                q_part[0, :head] + q_part[0, head:],
                k_part[0, :head],
            ]
        ).reshape(-1, 128)
    ).reshape(-1)
    return (
        block_out,
        input_grad,
        gains[:d],
        qkv_grad[:nq].T,
        qkv_grad[nq : nq + nk].T,
        qkv_grad[nq + nk :].T,
        out_grad,
        gains[2 * d : 2 * d + head],
        gains[2 * d + head :],
        gains[d : 2 * d],
        ffn_grad[0].T,
        ffn_grad[1].T,
        ffn_grad[2],
    )


def solution(mesh):
    dp, tensor = mesh.shape["dp"], mesh.shape["tensor"]
    cut = Mesh(
        mesh.devices.reshape(dp // 4, 2, 2, tensor // 2, 2), ("r", "y", "c", "z", "x")
    )
    data, model = ("r", "y", "c"), ("z", "x")
    both = data + model
    rows, wide, tall = P(both, None), P(data, model), P(model, data)
    in_specs = (
        rows, P(data, None), rows, P(), wide, wide, wide, tall, P(), P(), P(), wide, wide, tall
    )
    out_specs = (
        rows, rows, P(), wide, wide, wide, tall, P(), P(), P(), wide, wide, tall
    )
    return jax.shard_map(
        per_device, mesh=cut, in_specs=in_specs, out_specs=out_specs, check_vma=False
    )
```

time: 960 us -> 525 us (0.55)
  waiting for transfers between devices: 575 us -> 166 us
  starting transfers between devices: 1.18 us -> 144 us
  matrix products: 169 us -> 70.4 us
  blocking collectives: 67.2 us -> 0 us
  Pallas kernels: 0 us -> 54.7 us
  other arithmetic: 70.9 us -> 45.3 us
  loops' own time: 16.4 us -> 0 us
  between operations: 17 us -> 2.53 us
    reduce_scatter x11 -> x0, waiting for transfers between devices: 385 us -> none  [the longest x1 116 us: per_device(): lax.psum_scatter(mult(attn_heads, o_mat).astype(jnp.bfloat16), 'tensor',...]
    all_gather x7 -> x0, waiting for transfers between devices: 187 us -> none  [the longest x1 75.9 us: per_device(): lax.all_gather(xf_full.astype(jnp.bfloat16), 'tensor', axis=0, tiled=True)]
    ppermute x0 -> x79, waiting for transfers between devices: none -> 151 us  [the longest x43 86.4 us: swap(): return lax.ppermute(v, axes, [(i, i ^ bit) for i in range(size)])]
    ppermute x0 -> x79, starting transfers between devices: none -> 126 us  [the longest x9 45.1 us: line_scatter(): lax.ppermute(up.astype(BF16), axis, [(i, i + 1) for i in range(size - m)])]
    dot_general x49 -> x18, matrix products: 169 us -> 70.4 us  [the longest x3 28.9 us: nt(): lax.dot_general(a, b, (((1,), (1,)), ((), ())), preferred_element_type=F32)]
    pallas_call x0 -> x6, Pallas kernels: none -> 54.7 us  [the longest x1 17.3 us: attend_back_call(): pl.pallas_call(functools.partial(attend_back_kernel, head), grid_spec=plt...]
    psum x1 -> x0, blocking collectives: 42.4 us -> none  [per_device(): lax.psum((attn_gain_part, query_gain_part, key_gain_part, ffn_gain_part),...]
    dynamic_update_slice x8 -> x0, local copies, waits for them, and re-layouts: 25.6 us -> none  [per_device(): lax.scan(back_block, (zero_keys, zero_keys), (starts, log_total))]
  transfers between devices with their start and end apart: 18 -> 83, of which waited for: 10 -> 26; matrix products, arithmetic and copies ran while one was open for 20% -> 19% of each run, Pallas kernels for 0% -> 11%
where the time goes in v1:
time: 525 us; the launch traced here: 518 us
  waiting for transfers between devices  166 us (32%)
  starting transfers between devices  144 us (27%)
  matrix products  70.4 us (13%)
  Pallas kernels  54.7 us (10%)
  other arithmetic  45.3 us (9%)
  local copies, waits for them, and re-layouts  34.2 us (7%)
    ppermute x43, waiting for transfers between devices, swap(): return lax.ppermute(v, axes, [(i, i ^ bit) for i in range(size)])  86.4 us
    ppermute x9, starting transfers between devices, line_scatter(): lax.ppermute(up.astype(BF16), axis, [(i, i + 1) for i in range(size - m)])  45.1 us
    ppermute x43, starting transfers between devices, swap(): return lax.ppermute(v, axes, [(i, i ^ bit) for i in range(size)])  38.3 us
    ppermute x9, waiting for transfers between devices, line_gather(): lax.ppermute(right, axis, [(i, i - 1) for i in range(1, size - step + 1)])  32.3 us
    ppermute x9, waiting for transfers between devices, line_scatter(): lax.ppermute(up.astype(BF16), axis, [(i, i + 1) for i in range(size - m)])  31.6 us
    dot_general x3, matrix products, nt(): lax.dot_general(a, b, (((1,), (1,)), ((), ())), preferred_element_type=F32)  28.9 us
    ppermute x9, starting transfers between devices, line_gather(): lax.ppermute(left, axis, [(i, i + 1) for i in range(step - 1, size - 1)])  22.8 us
    dot_general x12, matrix products, nn(): lax.dot_general(a, b, (((1,), (0,)), ((), ())), preferred_element_type=F32)  22.4 us
  transfers between devices with their start and end apart: 83, of which 26 were waited for; matrix products, arithmetic and copies ran while one was open for 19% of the time, Pallas kernels for 11%

profile of v1, /device:TPU:0, one launch (start us, length us, event | category | flops | bytes accessed | tf_op | source)
XLA Modules:
  0.0 517.6 jit_solution(15084070472870306277)
XLA Ops:
  3.8 5.6 %collective-permute-start.1 = (bf16[256,256]{1,0:T(8,128)(2,1)S(1)}, bf16[256,256]{1,0:T(8,128)(2,1)S(1)}, u32[]{:S(2)}, u32[]{:S(2)}) collective-permute-start(bf16[256,256]{1,0:T(8,128)(2,1)S(1)} %get-tuple-element.176), channel_id=1, source_target_pairs={{0,2},{2,4},{4,6},{1,3},{3,5},{5,7},{8,10},{10,12},{12,14},{9,11},... | collective-permute-start | bytes 393224 | tf_op jit(solution)/shard_map/ppermute | solution.py:52
  10.7 5.2 collective-permute-start.14
  24.3 4.1 collective-permute-done.4
  30.4 4.8 collective-permute-done.5
  38.6 5.5 %collective-permute-start.31 = (bf16[3,288,512]{2,1,0:T(8,128)(2,1)}, bf16[3,288,512]{2,1,0:T(8,128)(2,1)}, u32[]{:S(2)}, u32[]{:S(2)}) collective-permute-start(bf16[3,288,512]{2,1,0:T(8,128)(2,1)} %pad_maximum_fusion.7), channel_id=1, source_target_pairs={{0,2},{2,4},{4,6},{1,3},{3,5},{5,7},{8,10},{10,12},{12,14},{9,11},... | collective-permute-start | bytes 2654216 | tf_op jit(solution)/shard_map/ppermute | solution.py:52
  49.6 9.3 %collective-permute-done.17 = bf16[128,256]{1,0:T(8,128)(2,1)S(1)} collective-permute-done((bf16[128,256]{1,0:T(8,128)(2,1)}, bf16[128,256]{1,0:T(8,128)(2,1)S(1)}, u32[]{:S(2)}, u32[]{:S(2)}) %collective-permute-start.17) | collective-permute-done | bytes 65568 | tf_op jit(solution)/shard_map/ppermute | solution.py:53
  61.7 3.3 collective-permute-done.18
  70.6 3.9 collective-permute-done.7
  80.3 10.8 %collective-permute-done.34 = bf16[3,288,512]{2,1,0:T(8,128)(2,1)} collective-permute-done((bf16[3,288,512]{2,1,0:T(8,128)(2,1)}, bf16[3,288,512]{2,1,0:T(8,128)(2,1)}, u32[]{:S(2)}, u32[]{:S(2)}) %collective-permute-start.34) | collective-permute-done | bytes 884768 | tf_op jit(solution)/shard_map/ppermute | solution.py:53
  96.6 9.5 %qkv.1 = (bf16[8,256,256]{2,1,0:T(8,128)(2,1)}, f32[8,256,256]{2,1,0:T(8,128)S(1)}) custom-call(s32[8]{0:T(128)S(1)} %reshape.195.order, bf16[256,1024]{1,0:T(8,128)(2,1)S(1)} %fusion.21.xa, bf16[8,256,1024]{2,1,0:T(8,128)(2,1)S(1)} %maximum_maximum_fusion.w, f32[256,128]{1,0:T(8,128)S(1)} %get-tuple-element.203.cosine, ...), custom_call_target="tpu_custom_call" | custom-call | flops 1073741824 | bytes 4194304 | tf_op jit(solution)/shard_map/qkv/pallas_call | solution.py:201
  109.3 6.6 %all-to-all-start = ((bf16[8,256,256]{2,1,0:T(8,128)(2,1)}), bf16[8,256,256]{2,1,0:T(8,128)(2,1)S(1)}, u32[]{:S(2)}, u32[]{:S(2)}) async-start(bf16[8,256,256]{2,1,0:T(8,128)(2,1)} %get-tuple-element.25), calls=%async_computation | async-start | bytes 2097152 | tf_op jit(solution)/shard_map/all_to_all | solution.py:617
  123.3 3.0 collective-permute-start.24
  126.5 11.1 %collective-permute-done.24 = bf16[4,128,256]{2,1,0:T(8,128)(2,1)S(1)} collective-permute-done((bf16[4,128,256]{2,1,0:T(8,128)(2,1)S(1)}, bf16[4,128,256]{2,1,0:T(8,128)(2,1)S(1)}, u32[]{:S(2)}, u32[]{:S(2)}) %collective-permute-start.24) | collective-permute-done | bytes 262176 | tf_op jit(solution)/shard_map/ppermute | solution.py:43
  141.2 11.8 %attend.1 = (bf16[2048,128]{1,0:T(8,128)(2,1)}, f32[8,1,512]{2,1,0:T(1,128)S(1)}) custom-call(s32[8]{0:T(128)S(1)} %and_select_fusion.first, bf16[2048,256]{1,0:T(8,128)(2,1)S(1)} %bitcast.164, s32[8,1,512]{2,1,0:T(1,128)S(1)} %pad_add_fusion.start), custom_call_target="tpu_custom_call" | custom-call | flops 2147483648 | bytes 1572864 | tf_op jit(solution)/shard_map/attend/pallas_call | solution.py:275
  152.9 3.7 all-to-all-start.1
  165.0 5.5 %all-to-all-done.1.context = bf16[8,256,128]{2,1,0:T(8,128)(2,1)S(1)} async-done(((bf16[8,256,128]{2,1,0:T(8,128)(2,1)}), bf16[8,256,128]{2,1,0:T(8,128)(2,1)S(1)}, u32[]{:S(2)}, u32[]{:S(2)}) %all-to-all-start.1) | async-done | bytes 524320 | tf_op jit(solution)/shard_map/all_to_all | solution.py:617
  171.7 3.2 project.1
  180.9 9.9 %collective-permute-done.28 = bf16[256,1024]{1,0:T(8,128)(2,1)S(1)} collective-permute-done((bf16[256,1024]{1,0:T(8,128)(2,1)S(1)}, bf16[256,1024]{1,0:T(8,128)(2,1)S(1)}, u32[]{:S(2)}, u32[]{:S(2)}) %collective-permute-start.28) | collective-permute-done | bytes 524320 | tf_op jit(solution)/shard_map/ppermute | solution.py:43
  190.8 9.4 %collective-permute-done.27 = bf16[256,1024]{1,0:T(8,128)(2,1)S(1)} collective-permute-done((bf16[256,1024]{1,0:T(8,128)(2,1)S(1)}, bf16[256,1024]{1,0:T(8,128)(2,1)S(1)}, u32[]{:S(2)}, u32[]{:S(2)}) %collective-permute-start.27) | collective-permute-done | bytes 524320 | tf_op jit(solution)/shard_map/ppermute | solution.py:43
  204.0 5.7 %convolution_convert_fusion.3 = bf16[1024,1152]{1,0:T(8,128)(2,1)} fusion(bf16[3,1152,1024]{2,1,0:T(8,128)(2,1)S(1)} %pad_maximum_fusion, bf16[256,512]{1,0:T(8,128)(2,1)S(1)} %copy-done.45, bf16[256,512]{1,0:T(8,128)(2,1)S(1)} %copy-done.44, bf16[256,512]{1,0:T(8,128)(2,1)S(1)} %copy-done.47, bf16[256,512]{1,0:T(8,128)(2,1)S(1)} %copy-done.46, ...), kind=kOutput, calls=%fused_computation.16 | convolution fusion | flops 2435973120 | bytes 6815744 | tf_op jit(solution)/shard_map/dot_general | solution.py:24
  209.7 10.3 %fusion.12 = f32[1024,1152]{1,0:T(8,128)} fusion(bf16[3,1152,1024]{2,1,0:T(8,128)(2,1)S(1)} %pad_maximum_fusion, bf16[256,512]{1,0:T(8,128)(2,1)S(1)} %get-tuple-element.168, bf16[256,512]{1,0:T(8,128)(2,1)S(1)} %get-tuple-element.167, bf16[256,512]{1,0:T(8,128)(2,1)S(1)} %get-tuple-element.166, bf16[256,512]{1,0:T(8,128)(2,1)S(1)} %get-tuple-element.165, ...), kind=kOutput, calls=%fused_computation.56 | convolution fusion | flops 2428502016 | bytes 9175040 | tf_op jit(solution)/shard_map/dot_general | solution.py:24
  220.0 12.8 %fusion.1 = (bf16[1024,1152]{1,0:T(8,128)(2,1)S(1)}, bf16[1024,1152]{1,0:T(8,128)(2,1)S(1)}, bf16[1024,1152]{1,0:T(8,128)(2,1)S(1)}) fusion(bf16[1024,1152]{1,0:T(8,128)(2,1)} %convolution_convert_fusion.3, f32[1024,1152]{1,0:T(8,128)} %fusion.12, bf16[3,1152,1024]{2,1,0:T(8,128)(2,1)S(1)} %pad_maximum_fusion, bf16[256,512]{1,0:T(8,128)(2,1)S(1)} %get-tuple-element.168, ...), kind=kOutput, calls=%fused_computation.6 | convolution fusion | flops 2447376384 | bytes 18612224 | tf_op jit(solution)/shard_map/dot_general | solution.py:24
  253.1 3.7 fusion.6
  256.8 7.6 %fusion.5 = bf16[1,1152,1024]{2,1,0:T(8,128)(2,1)S(1)} fusion(bf16[1024,1152]{1,0:T(8,128)(2,1)S(1)} %copy-done.61, bf16[256,512]{1,0:T(8,128)(2,1)S(1)} %get-tuple-element.168, bf16[256,512]{1,0:T(8,128)(2,1)S(1)} %get-tuple-element.167, bf16[256,512]{1,0:T(8,128)(2,1)S(1)} %get-tuple-element.166, bf16[256,512]{1,0:T(8,128)(2,1)S(1)} %get-tuple-element.165, ...), kind=kOutput, calls=%fused_computation.20 | convolution fusion | flops 2429681664 | bytes 6815744 | tf_op jit(solution)/shard_map/dot_general | solution.py:28
  264.5 7.8 %fusion.4 = bf16[1,1152,1024]{2,1,0:T(8,128)(2,1)S(1)} fusion(bf16[1024,1152]{1,0:T(8,128)(2,1)S(1)} %get-tuple-element.95, bf16[256,512]{1,0:T(8,128)(2,1)S(1)} %get-tuple-element.168, bf16[256,512]{1,0:T(8,128)(2,1)S(1)} %get-tuple-element.167, bf16[256,512]{1,0:T(8,128)(2,1)S(1)} %get-tuple-element.166, bf16[256,512]{1,0:T(8,128)(2,1)S(1)} %get-tuple-element.165, ...), kind=kOutput, calls=%fused_computation.19 | convolution fusion | flops 2429681664 | bytes 6815744 | tf_op jit(solution)/shard_map/dot_general | solution.py:28
  282.4 9.9 %collective-permute-done.44 = bf16[256,1024]{1,0:T(8,128)(2,1)S(1)} collective-permute-done((bf16[256,1024]{1,0:T(8,128)(2,1)}, bf16[256,1024]{1,0:T(8,128)(2,1)S(1)}, u32[]{:S(2)}, u32[]{:S(2)}) %collective-permute-start.44) | collective-permute-done | bytes 524320 | tf_op jit(solution)/shard_map/ppermute | solution.py:43
  298.3 3.6 project_back.1
  304.1 4.6 all-to-all-start.2
  313.3 3.7 fusion.29
  317.1 6.8 %all-to-all-done.2 = bf16[8,256,128]{2,1,0:T(8,128)(2,1)S(1)} async-done(((bf16[8,256,128]{2,1,0:T(8,128)(2,1)}), bf16[8,256,128]{2,1,0:T(8,128)(2,1)S(1)}, u32[]{:S(2)}, u32[]{:S(2)}) %all-to-all-start.2) | async-done | bytes 524320 | tf_op jit(solution)/shard_map/all_to_all | solution.py:617
  323.8 17.3 %attend_back.1 = bf16[2048,256]{1,0:T(8,128)(2,1)} custom-call(s32[8]{0:T(128)S(1)} %and_select_fusion.first, bf16[2048,256]{1,0:T(8,128)(2,1)S(1)} %bitcast.165, bf16[2048,128]{1,0:T(8,128)(2,1)} %get-tuple-element.26.context, bf16[2048,128]{1,0:T(8,128)(2,1)S(1)} %bitcast.166, s32[8,1,512]{2,1,0:T(1,128)S(1)} %pad_add_fusion.start, ...), custom_call_target="tpu_custom_call" | custom-call | flops 5368709120 | bytes 3145728 | tf_op jit(solution)/shard_map/attend_back/pallas_call | solution.py:362
  341.2 3.8 all-to-all-start.3
  350.1 13.7 %collective-permute-done.64 = bf16[4,128,256]{2,1,0:T(8,128)(2,1)S(1)} collective-permute-done((bf16[4,128,256]{2,1,0:T(8,128)(2,1)S(1)}, bf16[4,128,256]{2,1,0:T(8,128)(2,1)S(1)}, u32[]{:S(2)}, u32[]{:S(2)}) %collective-permute-start.64) | collective-permute-done | bytes 262176 | tf_op jit(solution)/shard_map/ppermute | solution.py:43
  363.8 5.1 collective-permute-done.62
  369.1 3.4 collective-permute-start.65
  374.4 4.3 collective-permute-start.66
  382.6 9.5 %collective-permute-start.67 = (bf16[128,256]{1,0:T(8,128)(2,1)}, bf16[128,256]{1,0:T(8,128)(2,1)}, u32[]{:S(2)}, u32[]{:S(2)}) collective-permute-start(bf16[128,256]{1,0:T(8,128)(2,1)} %get-tuple-element.143), channel_id=1, source_target_pairs={{0,2},{2,4},{4,6},{1,3},{3,5},{5,7},{8,10},{10,12},{12,14},{9,11},... | collective-permute-start | bytes 196616 | tf_op jit(solution)/shard_map/ppermute | solution.py:69
  395.8 9.3 %qkv_back.1 = (f32[256,1024]{1,0:T(8,128)S(1)}, bf16[8,256,1024]{2,1,0:T(8,128)(2,1)S(1)}, f32[1,128]{1,0:T(1,128)S(1)}, f32[1,128]{1,0:T(1,128)S(1)}) custom-call(s32[8]{0:T(128)S(1)} %reshape.195.order, bf16[8,256,256]{2,1,0:T(8,128)(2,1)S(1)} %all-to-all-done.3.grads, f32[8,256,256]{2,1,0:T(8,128)S(1)} %copy-done.7, bf16[256,1024]{1,0:T(8,128)(2,1)S(1)} %fusion.21.xa, ...), custom_call_target="tpu_custom_call" | custom-call | flops 2147483648 | bytes 8388608 | tf_op jit(solution)/shard_map/qkv_back/pallas_call | solution.py:503
  415.6 3.5 collective-permute-start.72
  421.5 3.7 collective-permute-done.48
  425.5 13.4 %collective-permute-done.49 = f32[17,128]{1,0:T(8,128)S(1)} collective-permute-done((f32[17,128]{1,0:T(8,128)S(1)}, f32[17,128]{1,0:T(8,128)S(1)}, u32[]{:S(2)}, u32[]{:S(2)}) %collective-permute-start.49) | collective-permute-done | bytes 8736 | tf_op jit(solution)/shard_map/ppermute | solution.py:43
  449.8 12.7 %collective-permute-done.73 = bf16[3,288,512]{2,1,0:T(8,128)(2,1)S(1)} collective-permute-done((bf16[3,288,512]{2,1,0:T(8,128)(2,1)S(1)}, bf16[3,288,512]{2,1,0:T(8,128)(2,1)S(1)}, u32[]{:S(2)}, u32[]{:S(2)}) %collective-permute-start.73) | collective-permute-done | bytes 884768 | tf_op jit(solution)/shard_map/ppermute | solution.py:69
  464.4 7.5 %collective-permute-start.74 = (bf16[3,288,512]{2,1,0:T(8,128)(2,1)S(1)}, bf16[3,288,512]{2,1,0:T(8,128)(2,1)S(1)}, u32[]{:S(2)}, u32[]{:S(2)}) collective-permute-start(bf16[3,288,512]{2,1,0:T(8,128)(2,1)S(1)} %get-tuple-element.106), channel_id=1, source_target_pairs={{0,2},{2,4},{4,6},{1,3},{3,5},{5,7},{8,10},{10,12},{12,14},{9,11},... | collective-permute-start | bytes 2654216 | tf_op jit(solution)/shard_map/ppermute | solution.py:69
  472.2 3.9 collective-permute-start.55
  477.3 14.6 %collective-permute-done.55 = bf16[256,256]{1,0:T(8,128)(2,1)S(1)} collective-permute-done((bf16[256,256]{1,0:T(8,128)(2,1)S(1)}, bf16[256,256]{1,0:T(8,128)(2,1)S(1)}, u32[]{:S(2)}, u32[]{:S(2)}) %collective-permute-start.55) | collective-permute-done | bytes 131104 | tf_op jit(solution)/shard_map/ppermute | solution.py:69
  492.0 4.4 collective-permute-start.56
  500.2 6.9 %collective-permute-start.57 = (bf16[256,256]{1,0:T(8,128)(2,1)S(1)}, bf16[256,256]{1,0:T(8,128)(2,1)S(1)}, u32[]{:S(2)}, u32[]{:S(2)}) collective-permute-start(bf16[256,256]{1,0:T(8,128)(2,1)S(1)} %get-tuple-element.131), channel_id=1, source_target_pairs={{0,2},{2,4},{4,6},{1,3},{3,5},{5,7},{8,10},{10,12},{12,14},{9,11},... | collective-permute-start | bytes 393224 | tf_op jit(solution)/shard_map/ppermute | solution.py:69
  511.1 4.8 collective-permute-done.78
  (385 shorter events, 170.7 us)
Async XLA Ops:
  2.5 19.0 %collective-permute-start = (bf16[256,256]{1,0:T(8,128)(2,1)S(1)}, bf16[256,256]{1,0:T(8,128)(2,1)S(1)}, u32[]{:S(2)}, u32[]{:S(2)}) collective-permute-start(bf16[256,256]{1,0:T(8,128)(2,1)S(1)} %get-tuple-element.176), channel_id=1, source_target_pairs={{2,0},{4,2},{6,4},{3,1},{5,3},{7,5},{10,8},{12,10},{14,12},{11,9},... | collective-permute-start | bytes 393224 | tf_op jit(solution)/shard_map/ppermute | solution.py:53
  3.8 19.1 %collective-permute-start.1 = (bf16[256,256]{1,0:T(8,128)(2,1)S(1)}, bf16[256,256]{1,0:T(8,128)(2,1)S(1)}, u32[]{:S(2)}, u32[]{:S(2)}) collective-permute-start(bf16[256,256]{1,0:T(8,128)(2,1)S(1)} %get-tuple-element.176), channel_id=1, source_target_pairs={{0,2},{2,4},{4,6},{1,3},{3,5},{5,7},{8,10},{10,12},{12,14},{9,11},... | collective-permute-start | bytes 393224 | tf_op jit(solution)/shard_map/ppermute | solution.py:52
  9.4 37.9 %collective-permute-start.13 = (bf16[128,256]{1,0:T(8,128)(2,1)}, bf16[128,256]{1,0:T(8,128)(2,1)}, u32[]{:S(2)}, u32[]{:S(2)}) collective-permute-start(bf16[128,256]{1,0:T(8,128)(2,1)} %param.21), channel_id=1, source_target_pairs={{2,0},{4,2},{6,4},{3,1},{5,3},{7,5},{10,8},{12,10},{14,12},{11,9},... | collective-permute-start | bytes 196616 | tf_op jit(solution)/shard_map/ppermute | solution.py:53
  10.7 38.2 %collective-permute-start.14 = (bf16[128,256]{1,0:T(8,128)(2,1)}, bf16[128,256]{1,0:T(8,128)(2,1)}, u32[]{:S(2)}, u32[]{:S(2)}) collective-permute-start(bf16[128,256]{1,0:T(8,128)(2,1)} %param.21), channel_id=1, source_target_pairs={{0,2},{2,4},{4,6},{1,3},{3,5},{5,7},{8,10},{10,12},{12,14},{9,11},... | collective-permute-start | bytes 196616 | tf_op jit(solution)/shard_map/ppermute | solution.py:52
  17.9 18.3 %collective-permute-start.29 = (bf16[3,288,256]{2,1,0:T(8,128)(2,1)}, bf16[3,288,256]{2,1,0:T(8,128)(2,1)S(1)}, u32[]{:S(2)}, u32[]{:S(2)}) collective-permute-start(bf16[3,288,256]{2,1,0:T(8,128)(2,1)} %get-tuple-element.142), channel_id=1, source_target_pairs={{0,16},{16,0},{1,17},{17,1},{2,18},{18,2},{3,19},{19,3},{4,20},{20... | collective-permute-start | bytes 1327112 | tf_op jit(solution)/shard_map/ppermute | solution.py:43
  37.3 29.5 %collective-permute-start.30 = (bf16[3,288,512]{2,1,0:T(8,128)(2,1)}, bf16[3,288,512]{2,1,0:T(8,128)(2,1)}, u32[]{:S(2)}, u32[]{:S(2)}) collective-permute-start(bf16[3,288,512]{2,1,0:T(8,128)(2,1)} %pad_maximum_fusion.7), channel_id=1, source_target_pairs={{2,0},{4,2},{6,4},{3,1},{5,3},{7,5},{10,8},{12,10},{14,12},{11,9},... | collective-permute-start | bytes 2654216 | tf_op jit(solution)/shard_map/ppermute | solution.py:53
  38.6 29.5 %collective-permute-start.31 = (bf16[3,288,512]{2,1,0:T(8,128)(2,1)}, bf16[3,288,512]{2,1,0:T(8,128)(2,1)}, u32[]{:S(2)}, u32[]{:S(2)}) collective-permute-start(bf16[3,288,512]{2,1,0:T(8,128)(2,1)} %pad_maximum_fusion.7), channel_id=1, source_target_pairs={{0,2},{2,4},{4,6},{1,3},{3,5},{5,7},{8,10},{10,12},{12,14},{9,11},... | collective-permute-start | bytes 2654216 | tf_op jit(solution)/shard_map/ppermute | solution.py:52
  45.0 20.3 %collective-permute-start.11 = (bf16[4,256,256]{2,1,0:T(8,128)(2,1)}, bf16[4,256,256]{2,1,0:T(8,128)(2,1)S(1)}, u32[]{:S(2)}, u32[]{:S(2)}) collective-permute-start(bf16[4,256,256]{2,1,0:T(8,128)(2,1)} %pad_maximum_fusion.10), channel_id=1, source_target_pairs={{0,17},{1,16},{16,1},{17,0},{2,19},{3,18},{18,3},{19,2},{4,21},{5,... | collective-permute-start | bytes 1572872 | tf_op jit(solution)/shard_map/ppermute | solution.py:43
  66.8 24.3 %collective-permute-start.34 = (bf16[3,288,512]{2,1,0:T(8,128)(2,1)}, bf16[3,288,512]{2,1,0:T(8,128)(2,1)}, u32[]{:S(2)}, u32[]{:S(2)}) collective-permute-start(bf16[3,288,512]{2,1,0:T(8,128)(2,1)} %collective-permute-done.30), channel_id=1, source_target_pairs={{2,0},{4,2},{3,1},{5,3},{10,8},{12,10},{11,9},{13,11},{18,16},{20,... | collective-permute-start | bytes 2654216 | tf_op jit(solution)/shard_map/ppermute | solution.py:53
  68.1 24.3 %collective-permute-start.32 = (bf16[3,288,512]{2,1,0:T(8,128)(2,1)}, bf16[3,288,512]{2,1,0:T(8,128)(2,1)}, u32[]{:S(2)}, u32[]{:S(2)}) collective-permute-start(bf16[3,288,512]{2,1,0:T(8,128)(2,1)} %collective-permute-done.31), channel_id=1, source_target_pairs={{2,4},{4,6},{3,5},{5,7},{10,12},{12,14},{11,13},{13,15},{18,20},{2... | collective-permute-start | bytes 2654216 | tf_op jit(solution)/shard_map/ppermute | solution.py:52
  76.0 81.3 %collective-permute-start.42 = (bf16[256,1024]{1,0:T(8,128)(2,1)}, bf16[256,1024]{1,0:T(8,128)(2,1)}, u32[]{:S(2)}, u32[]{:S(2)}) collective-permute-start(bf16[256,1024]{1,0:T(8,128)(2,1)} %pad_maximum_fusion.12), channel_id=1, source_target_pairs={{0,17},{1,16},{16,1},{17,0},{2,19},{3,18},{18,3},{19,2},{4,21},{5,... | collective-permute-start | bytes 1572872 | tf_op jit(solution)/shard_map/ppermute | solution.py:43
  77.5 79.9 %collective-permute-start.41 = (bf16[256,1024]{1,0:T(8,128)(2,1)}, bf16[256,1024]{1,0:T(8,128)(2,1)}, u32[]{:S(2)}, u32[]{:S(2)}) collective-permute-start(bf16[256,1024]{1,0:T(8,128)(2,1)} %pad_maximum_fusion.12), channel_id=1, source_target_pairs={{0,16},{1,17},{16,0},{17,1},{2,18},{3,19},{18,2},{19,3},{4,20},{5,... | collective-permute-start | bytes 1572872 | tf_op jit(solution)/shard_map/ppermute | solution.py:43
  79.0 43.4 %collective-permute-start.16 = (bf16[128,256]{1,0:T(8,128)(2,1)S(1)}, bf16[128,256]{1,0:T(8,128)(2,1)}, u32[]{:S(2)}, u32[]{:S(2)}) collective-permute-start(bf16[128,256]{1,0:T(8,128)(2,1)S(1)} %collective-permute-done.15), channel_id=1, source_target_pairs={{4,6},{5,7},{12,14},{13,15},{20,22},{21,23},{28,30},{29,31}} | collective-permute-start | bytes 196616 | tf_op jit(solution)/shard_map/ppermute | solution.py:52
  91.1 26.2 %collective-permute-start.35 = (bf16[3,288,512]{2,1,0:T(8,128)(2,1)}, bf16[3,288,512]{2,1,0:T(8,128)(2,1)}, u32[]{:S(2)}, u32[]{:S(2)}) collective-permute-start(bf16[3,288,512]{2,1,0:T(8,128)(2,1)} %collective-permute-done.34), channel_id=1, source_target_pairs={{2,0},{3,1},{10,8},{11,9},{18,16},{19,17},{26,24},{27,25}} | collective-permute-start | bytes 2654216 | tf_op jit(solution)/shard_map/ppermute | solution.py:53
  92.4 26.2 %collective-permute-start.33 = (bf16[3,288,512]{2,1,0:T(8,128)(2,1)}, bf16[3,288,512]{2,1,0:T(8,128)(2,1)}, u32[]{:S(2)}, u32[]{:S(2)}) collective-permute-start(bf16[3,288,512]{2,1,0:T(8,128)(2,1)} %collective-permute-done.32), channel_id=1, source_target_pairs={{4,6},{5,7},{12,14},{13,15},{20,22},{21,23},{28,30},{29,31}} | collective-permute-start | bytes 2654216 | tf_op jit(solution)/shard_map/ppermute | solution.py:52
  109.3 31.9 %all-to-all-start = ((bf16[8,256,256]{2,1,0:T(8,128)(2,1)}), bf16[8,256,256]{2,1,0:T(8,128)(2,1)S(1)}, u32[]{:S(2)}, u32[]{:S(2)}) async-start(bf16[8,256,256]{2,1,0:T(8,128)(2,1)} %get-tuple-element.25), calls=%async_computation | async-start | bytes 2097152 | tf_op jit(solution)/shard_map/all_to_all | solution.py:617
  122.4 77.9 %collective-permute-start.36 = (bf16[3,1152,512]{2,1,0:T(8,128)(2,1)}, bf16[3,1152,512]{2,1,0:T(8,128)(2,1)}, u32[]{:S(2)}, u32[]{:S(2)}) collective-permute-start(bf16[3,1152,512]{2,1,0:T(8,128)(2,1)} %pad_maximum_fusion.2), channel_id=1, source_target_pairs={{0,8},{8,0},{1,9},{9,1},{2,10},{10,2},{3,11},{11,3},{4,12},{12,4},... | collective-permute-start | bytes 10616840 | tf_op jit(solution)/shard_map/ppermute | solution.py:43
  126.5 30.2 %collective-permute-start.22 = (bf16[4,128,256]{2,1,0:T(8,128)(2,1)S(1)}, bf16[4,128,256]{2,1,0:T(8,128)(2,1)S(1)}, u32[]{:S(2)}, u32[]{:S(2)}) collective-permute-start(bf16[4,128,256]{2,1,0:T(8,128)(2,1)S(1)} %pad_maximum_fusion.14), channel_id=1, source_target_pairs={{0,1},{1,0},{16,17},{17,16},{2,3},{3,2},{18,19},{19,18},{4,5},{5,4... | collective-permute-start | bytes 786440 | tf_op jit(solution)/shard_map/ppermute | solution.py:43
  137.7 19.1 %collective-permute-start.20 = (bf16[4,128,256]{2,1,0:T(8,128)(2,1)S(1)}, bf16[4,128,256]{2,1,0:T(8,128)(2,1)S(1)}, u32[]{:S(2)}, u32[]{:S(2)}) collective-permute-start(bf16[4,128,256]{2,1,0:T(8,128)(2,1)S(1)} %pad_maximum_fusion.14), channel_id=1, source_target_pairs={{0,16},{1,17},{16,0},{17,1},{2,18},{3,19},{18,2},{19,3},{4,20},{5,... | collective-permute-start | bytes 786440 | tf_op jit(solution)/shard_map/ppermute | solution.py:43
  152.9 17.5 %all-to-all-start.1 = ((bf16[8,256,128]{2,1,0:T(8,128)(2,1)}), bf16[8,256,128]{2,1,0:T(8,128)(2,1)S(1)}, u32[]{:S(2)}, u32[]{:S(2)}) async-start(bf16[8,256,128]{2,1,0:T(8,128)(2,1)} %bitcast.16), calls=%async_computation.1 | async-start | bytes 1048576 | tf_op jit(solution)/shard_map/all_to_all | solution.py:617
  161.5 42.1 %collective-permute-start.40 = (bf16[256,1024]{1,0:T(8,128)(2,1)}, bf16[256,1024]{1,0:T(8,128)(2,1)}, u32[]{:S(2)}, u32[]{:S(2)}) collective-permute-start(bf16[256,1024]{1,0:T(8,128)(2,1)} %pad_maximum_fusion.12), channel_id=1, source_target_pairs={{0,1},{1,0},{16,17},{17,16},{2,3},{3,2},{18,19},{19,18},{4,5},{5,4... | collective-permute-start | bytes 1572872 | tf_op jit(solution)/shard_map/ppermute | solution.py:43
  178.8 21.5 %collective-permute-start.27 = (bf16[256,1024]{1,0:T(8,128)(2,1)S(1)}, bf16[256,1024]{1,0:T(8,128)(2,1)S(1)}, u32[]{:S(2)}, u32[]{:S(2)}) collective-permute-start(bf16[256,1024]{1,0:T(8,128)(2,1)S(1)} %get-tuple-element.28), channel_id=1, source_target_pairs={{0,16},{1,17},{16,0},{17,1},{2,18},{3,19},{18,2},{19,3},{4,20},{5,... | collective-permute-start | bytes 1572872 | tf_op jit(solution)/shard_map/ppermute | solution.py:43
  180.1 29.6 %collective-permute-start.26 = (bf16[256,1024]{1,0:T(8,128)(2,1)S(1)}, bf16[256,1024]{1,0:T(8,128)(2,1)S(1)}, u32[]{:S(2)}, u32[]{:S(2)}) collective-permute-start(bf16[256,1024]{1,0:T(8,128)(2,1)S(1)} %get-tuple-element.28), channel_id=1, source_target_pairs={{0,1},{1,0},{16,17},{17,16},{2,3},{3,2},{18,19},{19,18},{4,5},{5,4... | collective-permute-start | bytes 1572872 | tf_op jit(solution)/shard_map/ppermute | solution.py:43
  243.7 68.1 %collective-permute-start.39 = (bf16[256,1024]{1,0:T(8,128)(2,1)}, bf16[256,1024]{1,0:T(8,128)(2,1)}, u32[]{:S(2)}, u32[]{:S(2)}) collective-permute-start(bf16[256,1024]{1,0:T(8,128)(2,1)} %convolution_convert_fusion.4), channel_id=1, source_target_pairs={{0,17},{1,16},{16,1},{17,0},{2,19},{3,18},{18,3},{19,2},{4,21},{5,... | collective-permute-start | bytes 1572872 | tf_op jit(solution)/shard_map/ppermute | solution.py:43
  245.3 66.6 %collective-permute-start.38 = (bf16[256,1024]{1,0:T(8,128)(2,1)}, bf16[256,1024]{1,0:T(8,128)(2,1)}, u32[]{:S(2)}, u32[]{:S(2)}) collective-permute-start(bf16[256,1024]{1,0:T(8,128)(2,1)} %convolution_convert_fusion.5), channel_id=1, source_target_pairs={{0,16},{1,17},{16,0},{17,1},{2,18},{3,19},{18,2},{19,3},{4,20},{5,... | collective-permute-start | bytes 1572872 | tf_op jit(solution)/shard_map/ppermute | solution.py:43
  246.3 67.0 %collective-permute-start.37 = (bf16[256,1024]{1,0:T(8,128)(2,1)}, bf16[256,1024]{1,0:T(8,128)(2,1)}, u32[]{:S(2)}, u32[]{:S(2)}) collective-permute-start(bf16[256,1024]{1,0:T(8,128)(2,1)} %convolution_convert_fusion.6), channel_id=1, source_target_pairs={{0,1},{1,0},{16,17},{17,16},{2,3},{3,2},{18,19},{19,18},{4,5},{5,4... | collective-permute-start | bytes 1572872 | tf_op jit(solution)/shard_map/ppermute | solution.py:43
  248.8 32.4 %collective-permute-start.45 = (bf16[256,1024]{1,0:T(8,128)(2,1)}, bf16[256,1024]{1,0:T(8,128)(2,1)S(1)}, u32[]{:S(2)}, u32[]{:S(2)}) collective-permute-start(bf16[256,1024]{1,0:T(8,128)(2,1)} %fusion.11), channel_id=1, source_target_pairs={{0,17},{1,16},{16,1},{17,0},{2,19},{3,18},{18,3},{19,2},{4,21},{5,... | collective-permute-start | bytes 1572872 | tf_op jit(solution)/shard_map/ppermute | solution.py:43
  252.0 40.4 %collective-permute-start.44 = (bf16[256,1024]{1,0:T(8,128)(2,1)}, bf16[256,1024]{1,0:T(8,128)(2,1)S(1)}, u32[]{:S(2)}, u32[]{:S(2)}) collective-permute-start(bf16[256,1024]{1,0:T(8,128)(2,1)} %fusion.10), channel_id=1, source_target_pairs={{0,16},{1,17},{16,0},{17,1},{2,18},{3,19},{18,2},{19,3},{4,20},{5,... | collective-permute-start | bytes 1572872 | tf_op jit(solution)/shard_map/ppermute | solution.py:43
  293.1 118.7 %collective-permute-start.71 = (bf16[3,1152,512]{2,1,0:T(8,128)(2,1)}, bf16[3,1152,512]{2,1,0:T(8,128)(2,1)}, u32[]{:S(2)}, u32[]{:S(2)}) collective-permute-start(bf16[3,1152,512]{2,1,0:T(8,128)(2,1)} %pad_maximum_fusion.3), channel_id=1, source_target_pairs={{0,8},{8,0},{1,9},{9,1},{2,10},{10,2},{3,11},{11,3},{4,12},{12,4},... | collective-permute-start | bytes 10616840 | tf_op jit(solution)/shard_map/ppermute | solution.py:43
  304.1 19.7 %all-to-all-start.2 = ((bf16[8,256,128]{2,1,0:T(8,128)(2,1)}), bf16[8,256,128]{2,1,0:T(8,128)(2,1)S(1)}, u32[]{:S(2)}, u32[]{:S(2)}) async-start(bf16[8,256,128]{2,1,0:T(8,128)(2,1)} %copy-done.11), calls=%async_computation.2 | async-start | bytes 1048576 | tf_op jit(solution)/shard_map/all_to_all | solution.py:617
  311.6 33.3 %collective-permute-start.61 = (bf16[8,128,512]{2,1,0:T(8,128)(2,1)}, bf16[8,128,512]{2,1,0:T(8,128)(2,1)}, u32[]{:S(2)}, u32[]{:S(2)}) collective-permute-start(bf16[8,128,512]{2,1,0:T(8,128)(2,1)} %pad_maximum_fusion.5), channel_id=1, source_target_pairs={{0,8},{8,0},{1,9},{9,1},{2,10},{10,2},{3,11},{11,3},{4,12},{12,4},... | collective-permute-start | bytes 3145736 | tf_op jit(solution)/shard_map/ppermute | solution.py:43
  341.2 50.9 %all-to-all-start.3 = ((bf16[8,256,256]{2,1,0:T(8,128)(2,1)}), bf16[8,256,256]{2,1,0:T(8,128)(2,1)S(1)}, u32[]{:S(2)}, u32[]{:S(2)}) async-start(bf16[8,256,256]{2,1,0:T(8,128)(2,1)} %bitcast.32), calls=%async_computation.3 | async-start | bytes 2097152 | tf_op jit(solution)/shard_map/all_to_all | solution.py:617
  346.5 17.3 %collective-permute-start.64 = (bf16[4,128,256]{2,1,0:T(8,128)(2,1)S(1)}, bf16[4,128,256]{2,1,0:T(8,128)(2,1)S(1)}, u32[]{:S(2)}, u32[]{:S(2)}) collective-permute-start(bf16[4,128,256]{2,1,0:T(8,128)(2,1)S(1)} %get-tuple-element.129), channel_id=1, source_target_pairs={{0,17},{1,16},{16,1},{17,0},{2,19},{3,18},{18,3},{19,2},{4,21},{5,... | collective-permute-start | bytes 786440 | tf_op jit(solution)/shard_map/ppermute | solution.py:43
  350.0 18.9 %collective-permute-start.62 = (bf16[4,128,256]{2,1,0:T(8,128)(2,1)S(1)}, bf16[4,128,256]{2,1,0:T(8,128)(2,1)S(1)}, u32[]{:S(2)}, u32[]{:S(2)}) collective-permute-start(bf16[4,128,256]{2,1,0:T(8,128)(2,1)S(1)} %get-tuple-element.128), channel_id=1, source_target_pairs={{0,1},{1,0},{16,17},{17,16},{2,3},{3,2},{18,19},{19,18},{4,5},{5,4... | collective-permute-start | bytes 786440 | tf_op jit(solution)/shard_map/ppermute | solution.py:43
  381.3 37.8 %collective-permute-start.70 = (bf16[128,256]{1,0:T(8,128)(2,1)}, bf16[128,256]{1,0:T(8,128)(2,1)S(1)}, u32[]{:S(2)}, u32[]{:S(2)}) collective-permute-start(bf16[128,256]{1,0:T(8,128)(2,1)} %get-tuple-element.144), channel_id=1, source_target_pairs={{2,0},{4,2},{6,4},{3,1},{5,3},{7,5},{10,8},{12,10},{14,12},{11,9},... | collective-permute-start | bytes 196616 | tf_op jit(solution)/shard_map/ppermute | solution.py:70
  382.6 37.3 %collective-permute-start.67 = (bf16[128,256]{1,0:T(8,128)(2,1)}, bf16[128,256]{1,0:T(8,128)(2,1)}, u32[]{:S(2)}, u32[]{:S(2)}) collective-permute-start(bf16[128,256]{1,0:T(8,128)(2,1)} %get-tuple-element.143), channel_id=1, source_target_pairs={{0,2},{2,4},{4,6},{1,3},{3,5},{5,7},{8,10},{10,12},{12,14},{9,11},... | collective-permute-start | bytes 196616 | tf_op jit(solution)/shard_map/ppermute | solution.py:69
  410.7 33.8 %collective-permute-start.51 = (bf16[8,256,512]{2,1,0:T(8,128)(2,1)S(1)}, bf16[8,256,512]{2,1,0:T(8,128)(2,1)S(1)}, u32[]{:S(2)}, u32[]{:S(2)}) collective-permute-start(bf16[8,256,512]{2,1,0:T(8,128)(2,1)S(1)} %pad_maximum_fusion.4), channel_id=1, source_target_pairs={{0,8},{8,0},{1,9},{9,1},{2,10},{10,2},{3,11},{11,3},{4,12},{12,4},... | collective-permute-start | bytes 6291464 | tf_op jit(solution)/shard_map/ppermute | solution.py:43
  415.6 25.9 %collective-permute-start.72 = (bf16[3,288,512]{2,1,0:T(8,128)(2,1)S(1)}, bf16[3,288,512]{2,1,0:T(8,128)(2,1)S(1)}, u32[]{:S(2)}, u32[]{:S(2)}) collective-permute-start(bf16[3,288,512]{2,1,0:T(8,128)(2,1)S(1)} %get-tuple-element.110), channel_id=1, source_target_pairs={{0,2},{1,3},{8,10},{9,11},{16,18},{17,19},{24,26},{25,27}} | collective-permute-start | bytes 2654216 | tf_op jit(solution)/shard_map/ppermute | solution.py:69
  419.1 22.4 %collective-permute-start.75 = (bf16[3,288,512]{2,1,0:T(8,128)(2,1)S(1)}, bf16[3,288,512]{2,1,0:T(8,128)(2,1)S(1)}, u32[]{:S(2)}, u32[]{:S(2)}) collective-permute-start(bf16[3,288,512]{2,1,0:T(8,128)(2,1)S(1)} %get-tuple-element.111), channel_id=1, source_target_pairs={{6,4},{7,5},{14,12},{15,13},{22,20},{23,21},{30,28},{31,29}} | collective-permute-start | bytes 2654216 | tf_op jit(solution)/shard_map/ppermute | solution.py:70
  442.0 20.5 %collective-permute-start.73 = (bf16[3,288,512]{2,1,0:T(8,128)(2,1)S(1)}, bf16[3,288,512]{2,1,0:T(8,128)(2,1)S(1)}, u32[]{:S(2)}, u32[]{:S(2)}) collective-permute-start(bf16[3,288,512]{2,1,0:T(8,128)(2,1)S(1)} %get-tuple-element.108), channel_id=1, source_target_pairs={{0,2},{2,4},{1,3},{3,5},{8,10},{10,12},{9,11},{11,13},{16,18},{18,... | collective-permute-start | bytes 2654216 | tf_op jit(solution)/shard_map/ppermute | solution.py:69
  443.8 18.7 %collective-permute-start.76 = (bf16[3,288,512]{2,1,0:T(8,128)(2,1)S(1)}, bf16[3,288,512]{2,1,0:T(8,128)(2,1)S(1)}, u32[]{:S(2)}, u32[]{:S(2)}) collective-permute-start(bf16[3,288,512]{2,1,0:T(8,128)(2,1)S(1)} %get-tuple-element.109), channel_id=1, source_target_pairs={{4,2},{6,4},{5,3},{7,5},{12,10},{14,12},{13,11},{15,13},{20,18},{2... | collective-permute-start | bytes 2654216 | tf_op jit(solution)/shard_map/ppermute | solution.py:70
  445.3 26.5 %collective-permute-start.54 = (bf16[4,256,256]{2,1,0:T(8,128)(2,1)S(1)}, bf16[4,256,256]{2,1,0:T(8,128)(2,1)S(1)}, u32[]{:S(2)}, u32[]{:S(2)}) collective-permute-start(bf16[4,256,256]{2,1,0:T(8,128)(2,1)S(1)} %get-tuple-element.123), channel_id=1, source_target_pairs={{0,17},{1,16},{16,1},{17,0},{2,19},{3,18},{18,3},{19,2},{4,21},{5,... | collective-permute-start | bytes 1572872 | tf_op jit(solution)/shard_map/ppermute | solution.py:43
  445.4 26.5 %collective-permute-start.53 = (bf16[4,256,256]{2,1,0:T(8,128)(2,1)S(1)}, bf16[4,256,256]{2,1,0:T(8,128)(2,1)S(1)}, u32[]{:S(2)}, u32[]{:S(2)}) collective-permute-start(bf16[4,256,256]{2,1,0:T(8,128)(2,1)S(1)} %get-tuple-element.124), channel_id=1, source_target_pairs={{0,16},{1,17},{16,0},{17,1},{2,18},{3,19},{18,2},{19,3},{4,20},{5,... | collective-permute-start | bytes 1572872 | tf_op jit(solution)/shard_map/ppermute | solution.py:43
  447.4 24.4 %collective-permute-start.52 = (bf16[4,256,256]{2,1,0:T(8,128)(2,1)S(1)}, bf16[4,256,256]{2,1,0:T(8,128)(2,1)S(1)}, u32[]{:S(2)}, u32[]{:S(2)}) collective-permute-start(bf16[4,256,256]{2,1,0:T(8,128)(2,1)S(1)} %get-tuple-element.122), channel_id=1, source_target_pairs={{0,1},{1,0},{16,17},{17,16},{2,3},{3,2},{18,19},{19,18},{4,5},{5,4... | collective-permute-start | bytes 1572872 | tf_op jit(solution)/shard_map/ppermute | solution.py:43
  463.1 44.1 %collective-permute-start.77 = (bf16[3,288,512]{2,1,0:T(8,128)(2,1)S(1)}, bf16[3,288,512]{2,1,0:T(8,128)(2,1)S(1)}, u32[]{:S(2)}, u32[]{:S(2)}) collective-permute-start(bf16[3,288,512]{2,1,0:T(8,128)(2,1)S(1)} %get-tuple-element.107), channel_id=1, source_target_pairs={{2,0},{4,2},{6,4},{3,1},{5,3},{7,5},{10,8},{12,10},{14,12},{11,9},... | collective-permute-start | bytes 2654216 | tf_op jit(solution)/shard_map/ppermute | solution.py:70
  464.4 42.8 %collective-permute-start.74 = (bf16[3,288,512]{2,1,0:T(8,128)(2,1)S(1)}, bf16[3,288,512]{2,1,0:T(8,128)(2,1)S(1)}, u32[]{:S(2)}, u32[]{:S(2)}) collective-permute-start(bf16[3,288,512]{2,1,0:T(8,128)(2,1)S(1)} %get-tuple-element.106), channel_id=1, source_target_pairs={{0,2},{2,4},{4,6},{1,3},{3,5},{5,7},{8,10},{10,12},{12,14},{9,11},... | collective-permute-start | bytes 2654216 | tf_op jit(solution)/shard_map/ppermute | solution.py:69
  472.2 19.8 %collective-permute-start.55 = (bf16[256,256]{1,0:T(8,128)(2,1)S(1)}, bf16[256,256]{1,0:T(8,128)(2,1)S(1)}, u32[]{:S(2)}, u32[]{:S(2)}) collective-permute-start(bf16[256,256]{1,0:T(8,128)(2,1)S(1)} %get-tuple-element.135), channel_id=1, source_target_pairs={{0,2},{1,3},{8,10},{9,11},{16,18},{17,19},{24,26},{25,27}} | collective-permute-start | bytes 393224 | tf_op jit(solution)/shard_map/ppermute | solution.py:69
  476.0 15.9 %collective-permute-start.58 = (bf16[256,256]{1,0:T(8,128)(2,1)S(1)}, bf16[256,256]{1,0:T(8,128)(2,1)S(1)}, u32[]{:S(2)}, u32[]{:S(2)}) collective-permute-start(bf16[256,256]{1,0:T(8,128)(2,1)S(1)} %get-tuple-element.136), channel_id=1, source_target_pairs={{6,4},{7,5},{14,12},{15,13},{22,20},{23,21},{30,28},{31,29}} | collective-permute-start | bytes 393224 | tf_op jit(solution)/shard_map/ppermute | solution.py:70
  (97 other events, 1391.5 us)

commit v2 on v1

--- a/solution.py
+++ b/solution.py
@@ -15,6 +15,9 @@
 BF16 = jnp.bfloat16
 VMEM_LIMIT = 40 * 1024 * 1024
 
+NEAR = ("zl", "x")
+TENSOR = ("zh", "zl", "x")
+
 
 def nn(a, b):
     return lax.dot_general(a, b, (((1,), (0,)), ((), ())), preferred_element_type=F32)
@@ -26,12 +29,6 @@
 
 def tn(a, b):
     return lax.dot_general(a, b, (((0,), (0,)), ((), ())), preferred_element_type=F32)
-
-
-def exact_nn(a, b):
-    return lax.dot_general(
-        a, b, (((1,), (0,)), ((), ())), preferred_element_type=F32, precision=lax.Precision.HIGHEST
-    )
 
 
 def params(**more):
@@ -43,41 +40,8 @@
     return lax.ppermute(v, axes, [(i, i ^ bit) for i in range(size)])
 
 
-def line_gather(v, axis):
-    size = lax.axis_size(axis)
-    me = lax.axis_index(axis)
-    from_left, from_right = [], []
-    left = right = v
-    for step in range(1, size):
-        left = lax.ppermute(left, axis, [(i, i + 1) for i in range(step - 1, size - 1)])
-        right = lax.ppermute(right, axis, [(i, i - 1) for i in range(1, size - step + 1)])
-        from_left.append(left)
-        from_right.append(right)
-    slots = [v]
-    for d in range(1, size):
-        slots.append(jnp.where(me + d < size, from_right[d - 1], from_left[size - d - 1]))
-    return slots
-
-
-def line_scatter(parts, axis):
-    size = lax.axis_size(axis)
-    left = right = None
-    for m in range(size - 1, 0, -1):
-        up, down = parts[m].astype(F32), parts[size - m].astype(F32)
-        if left is not None:
-            up, down = up + left.astype(F32), down + right.astype(F32)
-        left = lax.ppermute(up.astype(BF16), axis, [(i, i + 1) for i in range(size - m)])
-        right = lax.ppermute(down.astype(BF16), axis, [(i, i - 1) for i in range(m, size)])
-    return parts[0].astype(F32) + left.astype(F32) + right.astype(F32)
-
-
 def quads(v):
     return jnp.split(v, 4, axis=-1)
-
-
-def flip_y(v):
-    a, b = jnp.split(v, 2, axis=-1)
-    return jnp.concatenate([b, a], axis=-1)
 
 
 def own_order(v, y, c):
@@ -118,7 +82,7 @@
 def total_of(v):
     if lax.axis_size("r") > 1:
         v = lax.psum(v, "r")
-    for axis in ("c", "x", "y", "z"):
+    for axis in ("c", "x", "y", "zl", "zh"):
         bit = 1
         while bit < lax.axis_size(axis):
             v = v + swap(v, axis, bit)
@@ -126,37 +90,55 @@
     return v
 
 
-def gather_heads(w):
-    slots = jnp.stack(line_gather(w, "z"))
-    near = [slots] + [swap(slots, ("y", "x"), bit) for bit in (1, 2, 3)]
-    far = [swap(v, "c", 1) for v in near]
-    rows = [
-        jnp.concatenate([near[ex], far[ex], near[ex + 2], far[ex + 2]], axis=-1) for ex in (0, 1)
-    ]
-    return jnp.concatenate(rows, axis=0)
-
-
-def scatter_heads(g):
+def gather_pair(w):
+    pair = []
+    for v in (w, swap(w, "zh", 1)):
+        both = jnp.concatenate([v, swap(v, "y", 1)], axis=-1)
+        pair.append((both, swap(both, "c", 1)))
+    return [weave(a, b) for a, b in pair]
+
+
+def weave(near, far):
+    (a, b), (a_far, b_far) = jnp.split(near, 2, axis=-1), jnp.split(far, 2, axis=-1)
+    return jnp.concatenate([a, a_far, b, b_far], axis=-1)
+
+
+def fold_core(g):
     e0, e1, e2, e3 = quads(g)
     from_core = swap(jnp.concatenate([e1, e3], axis=-1), "c", 1)
-    both = (jnp.concatenate([e0, e2], axis=-1).astype(F32) + from_core.astype(F32)).astype(BF16)
-    half, cols = g.shape[0] // 2, both.shape[-1] // 2
-    mine = both[:half, :, :cols].astype(F32)
-    mine = mine + swap(both[half:, :, :cols], ("y", "x"), 1).astype(F32)
-    mine = mine + swap(both[:half, :, cols:], ("y", "x"), 2).astype(F32)
-    mine = mine + swap(both[half:, :, cols:], ("y", "x"), 3).astype(F32)
-    return line_scatter([mine[d] for d in range(half)], "z")
-
-
-def gather_tokens(v):
-    around = [swap(v, ("y", "x"), bit) for bit in (1, 2, 3)]
-    return jnp.concatenate([v, around[0], flip_y(around[1]), flip_y(around[2])], axis=0)
-
-
-def scatter_tokens(parts):
-    near = swap(parts[1], ("y", "x"), 1).astype(F32) + parts[0]
-    far = swap(parts[2], ("y", "x"), 2).astype(F32) + swap(parts[3], ("y", "x"), 3).astype(F32)
-    return near + flip_y(far)
+    return (jnp.concatenate([e0, e2], axis=-1).astype(F32) + from_core.astype(F32)).astype(BF16)
+
+
+def fold_y(g):
+    a, b = jnp.split(g, 2, axis=-1)
+    return a.astype(F32) + swap(b, "y", 1).astype(F32)
+
+
+def scatter_pair(own, other):
+    other = fold_y(fold_core(other)).astype(BF16)
+    return fold_y(fold_core(own)) + swap(other, "zh", 1).astype(F32)
+
+
+def gather_near(v):
+    return [v] + [swap(v, NEAR, bit) for bit in (1, 2, 3)]
+
+
+def scatter_near(parts):
+    return [parts[0]] + [swap(parts[bit], NEAR, bit) for bit in (1, 2, 3)]
+
+
+def gather_out(w):
+    pair = jnp.stack([w, swap(w, "zh", 1)])
+    both = jnp.concatenate([pair, swap(pair, "y", 1)], axis=-1)
+    every = jnp.stack(gather_near(both))
+    return weave(every, swap(every, "c", 1))
+
+
+def scatter_out(g):
+    parts = scatter_near([v for v in fold_core(g)])
+    total = sum(v.astype(F32) for v in parts).astype(BF16)
+    pair = fold_y(total)
+    return pair[0] + swap(pair[1].astype(BF16), "zh", 1).astype(F32)
 
 
 def lanes_of(shape):
@@ -167,7 +149,9 @@
     width = v.shape[-1]
     row = lax.broadcasted_iota(jnp.int32, (width, width), 0) // head
     col = lax.broadcasted_iota(jnp.int32, (width, width), 1) // head
-    return exact_nn(v, jnp.where(row == col, 1.0, 0.0).astype(F32))
+    ones = jnp.where(row == col, 1.0, 0.0).astype(BF16)
+    high = v.astype(BF16)
+    return nn(high, ones) + nn((v - high.astype(F32)).astype(BF16), ones)
 
 
 def swap_halves(v, head):
@@ -178,14 +162,14 @@
 
 def qkv_kernel(head, order, xa, w, cosine, sine, q_gain, k_gain, low, kept):
     del order
-    proj = nt(xa[...], w[0])
+    proj = nt(xa[0], w[...])
     width = 2 * head
     kept[0] = proj
 
     def prep(v, gain):
         factor = lax.rsqrt(head_sums(v * v, head) * (1.0 / head) + EPSILON)
         n = v * factor * gain
-        return n * cosine[...] + swap_halves(n, head) * sine[...]
+        return n * cosine[0] + swap_halves(n, head) * sine[0]
 
     q = prep(proj[:, :width], q_gain[...])
     kv = proj[:, width:]
@@ -195,25 +179,26 @@
 
 
 def qkv_call(order, xa, w, cosine, sine, q_gain, k_gain, head):
-    blocks, n, d = w.shape
-    rows = xa.shape[0]
+    blocks, rows, d = xa.shape
+    n = w.shape[0]
     whole = lambda shape: pl.BlockSpec(shape, lambda j, order: (0,) * len(shape))
+    by_block = lambda *shape: pl.BlockSpec((1,) + shape, lambda j, order: (j, 0, 0))
     return pl.pallas_call(
         functools.partial(qkv_kernel, head),
         grid_spec=pltpu.PrefetchScalarGridSpec(
             num_scalar_prefetch=1,
             grid=(blocks,),
             in_specs=[
-                whole((rows, d)),
-                pl.BlockSpec((1, n, d), lambda j, order: (order[j], 0, 0)),
-                whole((rows, 2 * head)),
-                whole((rows, 2 * head)),
+                by_block(rows, d),
+                whole((n, d)),
+                by_block(rows, 2 * head),
+                by_block(rows, 2 * head),
                 whole((1, 2 * head)),
                 whole((1, 2 * head)),
             ],
             out_specs=[
-                pl.BlockSpec((1, rows, n), lambda j, order: (j, 0, 0)),
-                pl.BlockSpec((1, rows, n), lambda j, order: (j, 0, 0)),
+                pl.BlockSpec((1, rows, n), lambda j, order: (order[j], 0, 0)),
+                by_block(rows, n),
             ],
         ),
         out_shape=[
@@ -222,7 +207,7 @@
         ],
         compiler_params=params(),
         cost_estimate=pl.CostEstimate(
-            flops=2 * blocks * rows * n * d, bytes_accessed=2 * blocks * n * d, transcendentals=0
+            flops=2 * blocks * rows * n * d, bytes_accessed=4 * blocks * rows * d, transcendentals=0
         ),
         name="qkv",
     )(order, xa, w, cosine, sine, q_gain, k_gain)
@@ -430,16 +415,31 @@
     )(order, context, w, x, gain)
 
 
-def project_back_kernel(order, context, w, d_hidden, d_context, grad):
+def project_back_kernel(
+    order, context, w, hidden, gain, dy, p0, p1, p2, p3, d_context, grad, d_hidden, part, low
+):
     del order
-    low = d_hidden[...]
-    d_context[0] = nt(low, w[0]).astype(BF16)
-    grad[0] = tn(context[0], low).astype(BF16)
-
-
-def project_back_call(order, context, w, d_hidden):
+
+    @pl.when(pl.program_id(0) == 0)
+    def _():
+        h = hidden[...]
+        g = (p0[...].astype(F32) + p1[...].astype(F32)) + (p2[...].astype(F32) + p3[...].astype(F32))
+        n = lax.rsqrt(jnp.mean(h * h, axis=-1, keepdims=True) + EPSILON)
+        part[...] = jnp.sum(g * h * n, axis=0, keepdims=True)
+        u = gain[...] * g
+        mean = jnp.mean(u * h, axis=-1, keepdims=True)
+        out = dy[...].astype(F32) + (n * u - h * (n * n * n * mean))
+        d_hidden[...] = out
+        low[...] = out.astype(BF16)
+
+    d_context[0] = nt(low[...], w[0]).astype(BF16)
+    grad[0] = tn(context[0], low[...]).astype(BF16)
+
+
+def project_back_call(order, context, w, hidden, gain, dy, parts):
     blocks, n, d = w.shape
-    rows = d_hidden.shape[0]
+    rows = hidden.shape[0]
+    whole = lambda shape: pl.BlockSpec(shape, lambda j, order: (0,) * len(shape))
     by_block = pl.BlockSpec((1, rows, n), lambda j, order: (j, 0, 0))
     by_order = pl.BlockSpec((1, n, d), lambda j, order: (order[j], 0, 0))
     return pl.pallas_call(
@@ -447,58 +447,93 @@
         grid_spec=pltpu.PrefetchScalarGridSpec(
             num_scalar_prefetch=1,
             grid=(blocks,),
-            in_specs=[by_block, by_order, pl.BlockSpec((rows, d), lambda j, order: (0, 0))],
-            out_specs=[by_block, by_order],
+            in_specs=[by_block, by_order, whole((rows, d)), whole((1, d))]
+            + [whole((rows, d))] * 5,
+            out_specs=[by_block, by_order, whole((rows, d)), whole((1, d))],
+            scratch_shapes=[pltpu.VMEM((rows, d), BF16)],
         ),
         out_shape=[
             jax.ShapeDtypeStruct((blocks, rows, n), BF16),
             jax.ShapeDtypeStruct((blocks, n, d), BF16),
+            jax.ShapeDtypeStruct((rows, d), F32),
+            jax.ShapeDtypeStruct((1, d), F32),
         ],
         compiler_params=params(),
         cost_estimate=pl.CostEstimate(
             flops=4 * blocks * rows * n * d, bytes_accessed=4 * blocks * n * d, transcendentals=0
         ),
         name="project_back",
-    )(order, context, w, d_hidden)
+    )(order, context, w, hidden, gain, dy, *parts)
 
 
 def qkv_back_kernel(
-    head, order, grads, kept, xa, w, cosine, sine, q_gain, k_gain, d_xa, d_w, q_part, k_part
+    head,
+    where,
+    d_own,
+    d_other,
+    kept_own,
+    kept_other,
+    xa,
+    w_own,
+    w_other,
+    cosine,
+    sine,
+    q_gain,
+    k_gain,
+    d_xa,
+    dw_own,
+    dw_other,
+    q_part,
+    k_part,
+    sums,
 ):
-    del order
+    del where
     j = pl.program_id(0)
+    last = pl.num_programs(0) - 1
     width = 2 * head
 
     @pl.when(j == 0)
     def _():
-        d_xa[...] = jnp.zeros_like(d_xa)
         q_part[...] = jnp.zeros_like(q_part)
         k_part[...] = jnp.zeros_like(k_part)
+        sums[...] = jnp.zeros_like(sums)
 
     def back(g, v, gain):
-        e = g * cosine[...] - swap_halves(g, head) * sine[...]
+        e = g * cosine[0] - swap_halves(g, head) * sine[0]
         m = lax.rsqrt(head_sums(v * v, head) * (1.0 / head) + EPSILON)
         u = gain * e
         mean = head_sums(u * v, head) * (1.0 / head)
         return m * u - v * (m * m * m * mean), jnp.sum(e * v * m, axis=0, keepdims=True)
 
-    g, v = grads[0].astype(F32), kept[0]
-    d_q, part = back(g[:, :width], v[:, :width], q_gain[...])
-    q_part[...] += part
-    d_k, part = back(g[:, width:], v[:, width:], k_gain[...])
-    k_part[...] += part
-    d_kv = jnp.where(lanes_of(d_k.shape) < head, d_k, g[:, width:])
-    low = jnp.concatenate([d_q, d_kv], axis=1).astype(BF16)
-    d_xa[...] += nn(low, w[0])
-    d_w[0] = tn(low, xa[...]).astype(BF16)
-
-
-def qkv_back_call(order, grads, kept, xa, w, cosine, sine, q_gain, k_gain, head):
-    blocks, n, d = w.shape
-    rows = xa.shape[0]
-    whole = lambda shape: pl.BlockSpec(shape, lambda j, order: (0,) * len(shape))
-    by_block = pl.BlockSpec((1, rows, n), lambda j, order: (j, 0, 0))
-    by_order = pl.BlockSpec((1, n, d), lambda j, order: (order[j], 0, 0))
+    total = None
+    for s, (grads, kept, w) in enumerate(
+        ((d_own, kept_own, w_own), (d_other, kept_other, w_other))
+    ):
+        g, v = grads[0].astype(F32), kept[0]
+        d_q, part = back(g[:, :width], v[:, :width], q_gain[...])
+        q_part[...] += part
+        d_k, part = back(g[:, width:], v[:, width:], k_gain[...])
+        k_part[...] += part
+        d_kv = jnp.where(lanes_of(d_k.shape) < head, d_k, g[:, width:])
+        low = jnp.concatenate([d_q, d_kv], axis=1).astype(BF16)
+        here = nn(low, w[...])
+        total = here if total is None else total + here
+        sums[s] += tn(low, xa[0])
+    d_xa[0] = total.astype(BF16)
+
+    @pl.when(j == last)
+    def _():
+        dw_own[...] = sums[0].astype(BF16)
+        dw_other[...] = sums[1].astype(BF16)
+
+
+def qkv_back_call(
+    where, d_own, d_other, kept, xa, w, cosine, sine, q_gain, k_gain, head
+):
+    blocks, rows, d = xa.shape
+    n = w[0].shape[0]
+    whole = lambda shape: pl.BlockSpec(shape, lambda j, where: (0,) * len(shape))
+    by_block = lambda *shape: pl.BlockSpec((1,) + shape, lambda j, where: (j, 0, 0))
     lane = (1, 2 * head)
     return pl.pallas_call(
         functools.partial(qkv_back_kernel, head),
@@ -506,29 +541,113 @@
             num_scalar_prefetch=1,
             grid=(blocks,),
             in_specs=[
-                by_block,
-                by_block,
-                whole((rows, d)),
-                by_order,
-                whole((rows, 2 * head)),
-                whole((rows, 2 * head)),
+                pl.BlockSpec((1, rows, n), lambda j, where: (where[4] * 4 + where[j], 0, 0)),
+                pl.BlockSpec((1, rows, n), lambda j, where: (where[j], 0, 0)),
+                by_block(rows, n),
+                by_block(rows, n),
+                by_block(rows, d),
+                whole((n, d)),
+                whole((n, d)),
+                by_block(rows, 2 * head),
+                by_block(rows, 2 * head),
                 whole(lane),
                 whole(lane),
             ],
-            out_specs=[whole((rows, d)), by_order, whole(lane), whole(lane)],
+            out_specs=[by_block(rows, d), whole((n, d)), whole((n, d)), whole(lane), whole(lane)],
+            scratch_shapes=[pltpu.VMEM((2, n, d), F32)],
         ),
         out_shape=[
-            jax.ShapeDtypeStruct((rows, d), F32),
-            jax.ShapeDtypeStruct((blocks, n, d), BF16),
+            jax.ShapeDtypeStruct((blocks, rows, d), BF16),
+            jax.ShapeDtypeStruct((n, d), BF16),
+            jax.ShapeDtypeStruct((n, d), BF16),
             jax.ShapeDtypeStruct(lane, F32),
             jax.ShapeDtypeStruct(lane, F32),
         ],
         compiler_params=params(),
         cost_estimate=pl.CostEstimate(
-            flops=4 * blocks * rows * n * d, bytes_accessed=4 * blocks * n * d, transcendentals=0
+            flops=8 * blocks * rows * n * d, bytes_accessed=8 * blocks * rows * d, transcendentals=0
         ),
         name="qkv_back",
-    )(order, grads, kept, xa, w, cosine, sine, q_gain, k_gain)
+    )(where, d_own, d_other, kept[0], kept[1], xa, w[0], w[1], cosine, sine, q_gain, k_gain)
+
+
+def ffn_kernel(xf, dy, w, acts, out, d_xf):
+    gate, up = nt(xf[...], w[0]), nt(xf[...], w[1])
+    d_act = nt(dy[...], w[2]).astype(BF16).astype(F32)
+    sig = 1.0 / (1.0 + jnp.exp(-gate))
+    silu = gate * sig
+    act = (silu * up).astype(BF16)
+    d_gate = (d_act * up * (sig * (1.0 + gate * (1.0 - sig)))).astype(BF16)
+    d_up = (d_act * silu).astype(BF16)
+    d_xf[...] = (nn(d_gate, w[0]) + nn(d_up, w[1])).astype(BF16)
+    out[...] = nn(act, w[2]).astype(BF16)
+    acts[0] = d_gate
+    acts[1] = d_up
+    acts[2] = act
+
+
+def ffn_call(xf, dy, w):
+    rows, d = xf.shape
+    units = w.shape[1]
+    tokens = pl.BlockSpec((BLOCK, d), lambda j: (j, 0))
+    return pl.pallas_call(
+        ffn_kernel,
+        grid=(rows // BLOCK,),
+        in_specs=[tokens, tokens, pl.BlockSpec((3, units, d), lambda j: (0, 0, 0))],
+        out_specs=[pl.BlockSpec((3, BLOCK, units), lambda j: (0, j, 0)), tokens, tokens],
+        out_shape=[
+            jax.ShapeDtypeStruct((3, rows, units), BF16),
+            jax.ShapeDtypeStruct((rows, d), BF16),
+            jax.ShapeDtypeStruct((rows, d), BF16),
+        ],
+        compiler_params=params(),
+        cost_estimate=pl.CostEstimate(
+            flops=12 * rows * units * d,
+            bytes_accessed=6 * units * d + 8 * rows * d,
+            transcendentals=rows * units,
+        ),
+        name="ffn",
+    )(xf, dy, w)
+
+
+def ffn_grad_kernel(a_own, a_rest, x_own, x_rest, y_own, y_rest, grad):
+    which = pl.program_id(0)
+
+    @pl.when(which < 2)
+    def _():
+        grad[0] = (tn(a_own[0], x_own[...]) + tn(a_rest[0], x_rest[...])).astype(BF16)
+
+    @pl.when(which == 2)
+    def _():
+        grad[0] = (tn(a_own[0], y_own[...]) + tn(a_rest[0], y_rest[...])).astype(BF16)
+
+
+def ffn_grad_call(a_own, a_rest, x_own, x_rest, y_own, y_rest):
+    three, own, units = a_own.shape
+    rest, d = x_rest.shape
+    tile = units // 3
+    whole = lambda shape: pl.BlockSpec(shape, lambda k, j: (0,) * len(shape))
+    return pl.pallas_call(
+        ffn_grad_kernel,
+        grid=(three, 3),
+        in_specs=[
+            pl.BlockSpec((1, own, tile), lambda k, j: (k, 0, j)),
+            pl.BlockSpec((1, rest, tile), lambda k, j: (k, 0, j)),
+            whole((own, d)),
+            whole((rest, d)),
+            whole((own, d)),
+            whole((rest, d)),
+        ],
+        out_specs=pl.BlockSpec((1, tile, d), lambda k, j: (k, j, 0)),
+        out_shape=jax.ShapeDtypeStruct((three, units, d), BF16),
+        compiler_params=params(),
+        cost_estimate=pl.CostEstimate(
+            flops=6 * units * d * (own + rest),
+            bytes_accessed=2 * units * (4 * d + 3 * (own + rest)),
+            transcendentals=0,
+        ),
+        name="ffn_grad",
+    )(a_own, a_rest, x_own, x_rest, y_own, y_rest)
 
 
 def norm_factor(v):
@@ -558,28 +677,37 @@
     up_weight,
     down_weight,
 ):
-    y, c = lax.axis_index("y"), lax.axis_index("c")
-    z, x_at = lax.axis_index("z"), lax.axis_index("x")
-    z_size = lax.axis_size("z")
+    y, c, zh = lax.axis_index("y"), lax.axis_index("c"), lax.axis_index("zh")
+    near = lax.axis_index(NEAR)
     head = query_gain.shape[0]
     rows = tokens.shape[0]
     nq, nk = query_weight.shape[1], key_weight.shape[1]
-
-    qkv_w = gather_heads(
+    n = nq + 2 * nk
+
+    x = own_order(tokens, y, c).astype(F32)
+    gain_a = own_order(attn_gain[None], y, c)
+    gain_f = own_order(ffn_gain[None], y, c)
+    gain_q = jnp.concatenate([query_gain, query_gain])[None]
+    gain_k = jnp.concatenate([key_gain, key_gain])[None]
+    x_factor = norm_factor(x)
+    xa = (x * x_factor * gain_a).astype(BF16)
+    xa_all = jnp.stack(gather_near(xa))
+    qkv_w = gather_pair(
         gather_runs(jnp.concatenate([query_weight.T, key_weight.T, value_weight.T], axis=0))
     )
-    out_w = gather_heads(gather_runs(output_weight))
-    ffn = gather_runs(jnp.stack([gate_weight.T, up_weight.T, down_weight]))
-    units = ffn.shape[1] // 2
-    keep = jnp.where(y == 0, ffn[:, :units], ffn[:, units:])
-    give = jnp.where(y == 0, ffn[:, units:], ffn[:, :units])
-    ffn = jnp.concatenate([keep, swap(give, "y", 1)], axis=-1)
-    near = jnp.concatenate(line_gather(ffn, "z"), axis=1)
-    far = swap(near, "c", 1)
-    a, b = jnp.split(near, 2, axis=-1)
-    a_far, b_far = jnp.split(far, 2, axis=-1)
-    ffn_w = jnp.concatenate([a, a_far, b, b_far], axis=-1)
-    gate_w, up_w, down_w = ffn_w[0], ffn_w[1], ffn_w[2]
+
+    xa_all, qkv_w, later = lax.optimization_barrier(
+        (xa_all, qkv_w, (cotangent, output_weight, gate_weight, up_weight, down_weight))
+    )
+    cotangent, output_weight, gate_weight, up_weight, down_weight = later
+    dy = own_order(cotangent, y, c)
+    ffn_w = gather_pair(gather_runs(jnp.stack([gate_weight.T, up_weight.T, down_weight])))
+    units = ffn_w[0].shape[1]
+    ffn_w = jnp.concatenate(ffn_w, axis=1)
+    out_w = gather_out(gather_runs(output_weight))
+    out_w = out_w.reshape((8,) + out_w.shape[2:])
+    dy_all = gather_near(dy)
+    dy_rest = jnp.concatenate(dy_all[1:], axis=0)
 
     segment = segment_ids[0]
     total_rows = segment.shape[0]
@@ -590,96 +718,67 @@
     first = begin[::BLOCK] // BLOCK
     by_block = begin.reshape(blocks, 1, BLOCK)
     start = jnp.concatenate([by_block, by_block], axis=2)
-    here = lax.axis_index(("z", "x")) * rows
-    position = lax.dynamic_slice_in_dim(index - begin, here, rows).astype(F32)
+    four = jnp.arange(4, dtype=jnp.int32) ^ near
+    position = lax.dynamic_slice_in_dim(index - begin, zh * 4 * rows, 4 * rows).astype(F32)
     inverse = ROPE_BASE ** (-(jnp.arange(head // 2, dtype=F32) * 2.0) / head)
-    angle = position[:, None] * inverse[None, :]
+    angle = (position[:, None] * inverse[None, :]).reshape(4, rows, head // 2)[four]
     cos_half, sin_half = jnp.cos(angle), jnp.sin(angle)
-    cosine = jnp.concatenate([cos_half] * 4, axis=1)
-    sine = jnp.concatenate([-sin_half, sin_half] * 2, axis=1)
-    slots = jnp.arange(z_size, dtype=jnp.int32)
-    order = jnp.stack([(slots - z) % z_size + z_size * x_at, (slots - z) % z_size + z_size * (1 - x_at)], axis=1)
-    order = order.reshape(-1).astype(jnp.int32)
-
-    x = own_order(tokens, y, c).astype(F32)
-    grad_low = own_order(cotangent, y, c)
-    grad_out = grad_low.astype(F32)
-    gain_a = own_order(attn_gain[None], y, c)
-    gain_f = own_order(ffn_gain[None], y, c)
-    gain_q = jnp.concatenate([query_gain, query_gain])[None]
-    gain_k = jnp.concatenate([key_gain, key_gain])[None]
-
-    x_factor = norm_factor(x)
-    xa = (x * x_factor * gain_a).astype(BF16)
-    low, kept = qkv_call(order, xa, qkv_w, cosine, sine, gain_q, gain_k, head)
+    cosine = jnp.concatenate([cos_half] * 4, axis=2)
+    sine = jnp.concatenate([-sin_half, sin_half] * 2, axis=2)
+    where = jnp.concatenate([four, zh[None]]).astype(jnp.int32)
+    eight = jnp.arange(8, dtype=jnp.int32)
+    order = (((eight % 4) ^ near) * 2 + ((eight // 4) ^ zh)).astype(jnp.int32)
+
+    low, kept = zip(
+        *[qkv_call(where, xa_all, w, cosine, sine, gain_q, gain_k, head) for w in qkv_w]
+    )
+    here, there = low[0], swap(low[1], "zh", 1)
+    qkv = jnp.concatenate(
+        [jnp.where(zh == 0, here, there), jnp.where(zh == 0, there, here)], axis=0
+    ).reshape(total_rows, n)
+    context, log_total = attend_call(first, qkv, start, head)
 
     def to_heads(v):
-        return lax.all_to_all(v, ("z", "x"), 0, 0, tiled=True)
-
-    qkv = to_heads(low).reshape(total_rows, nq + 2 * nk)
-    context, log_total = attend_call(first, qkv, start, head)
+        return lax.all_to_all(v, TENSOR, 0, 0, tiled=True)
+
     context_rows = to_heads(context.reshape(-1, rows, nq))
     hidden, xf = project_call(order, context_rows, out_w, x, gain_f)
 
-    xf_all = gather_tokens(xf)
-    dy_all = gather_tokens(grad_low)
-    gate_pre = nt(xf_all, gate_w)
-    up_pre = nt(xf_all, up_w)
-    gate_sig = jax.nn.sigmoid(gate_pre)
-    silu = gate_pre * gate_sig
-    activation = (silu * up_pre).astype(BF16)
-    d_act = nt(dy_all, down_w).astype(BF16).astype(F32)
-    d_gate = (d_act * up_pre * (gate_sig * (1.0 + gate_pre * (1.0 - gate_sig)))).astype(BF16)
-    d_up = (d_act * silu).astype(BF16)
-
-    def rows_of(v, e):
-        return v[e * rows : (e + 1) * rows]
-
-    d_xf_parts = [
-        nn(rows_of(d_gate, e), gate_w) + nn(rows_of(d_up, e), up_w) for e in range(4)
-    ]
-    d_xf = scatter_tokens([d_xf_parts[0]] + [v.astype(BF16) for v in d_xf_parts[1:]])
-    ffn_parts = [nn(rows_of(activation, e), down_w) for e in range(4)]
-    ffn_out = scatter_tokens([ffn_parts[0]] + [v.astype(BF16) for v in ffn_parts[1:]])
-    block_out = arrays_order((hidden + ffn_out).astype(BF16), y, c)
-
-    h_back, ffn_gain_part = norm_back(hidden, norm_factor(hidden), gain_f, d_xf)
-    d_hidden = grad_out + h_back
-    d_context_rows, out_grad = project_back_call(
-        order, context_rows, out_w, d_hidden.astype(BF16)
+    xf_all = gather_near(xf)
+    acts_own, out_own, d_xf_own = ffn_call(xf, dy, ffn_w)
+    xf_rest = jnp.concatenate(xf_all[1:], axis=0)
+    acts_rest, out_rest, d_xf_rest = ffn_call(xf_rest, dy_rest, ffn_w)
+    d_xf = scatter_near([d_xf_own] + jnp.split(d_xf_rest, 3, axis=0))
+    ffn_grad = ffn_grad_call(acts_own, acts_rest, xf, xf_rest, dy, dy_rest)
+
+    d_context_rows, out_grad, d_hidden, ffn_gain_part = project_back_call(
+        order, context_rows, out_w, hidden, gain_f, dy, d_xf
     )
     d_context = to_heads(d_context_rows).reshape(total_rows, nq)
     d_qkv = attend_back_call(first, qkv, context, d_context, start, log_total, head)
-    d_qkv_rows = to_heads(d_qkv.reshape(-1, rows, nq + 2 * nk))
-    d_xa, qkv_grad, q_part, k_part = qkv_back_call(
-        order, d_qkv_rows, kept, xa, qkv_w, cosine, sine, gain_q, gain_k, head
-    )
+    d_qkv = d_qkv.reshape(-1, rows, n)
+    d_other = swap(jnp.where(zh == 0, d_qkv[4:], d_qkv[:4]), "zh", 1)
+    d_xa, dw_own, dw_other, q_part, k_part = qkv_back_call(
+        where, d_qkv, d_other, kept, xa_all, qkv_w, cosine, sine, gain_q, gain_k, head
+    )
+    d_xa = sum(v.astype(F32) for v in scatter_near([v for v in d_xa]))
     x_back, attn_gain_part = norm_back(x, x_factor, gain_a, d_xa)
     input_grad = arrays_order((d_hidden + x_back).astype(BF16), y, c)
 
-    ffn_grad = jnp.stack([tn(d_gate, xf_all), tn(d_up, xf_all), tn(activation, dy_all)])
-    e0, e1, e2, e3 = quads(ffn_grad.astype(BF16))
-    from_core = swap(jnp.concatenate([e1, e3], axis=-1), "c", 1)
-    both = jnp.concatenate([e0, e2], axis=-1).astype(F32) + from_core.astype(F32)
-    both = both.astype(BF16)
-    mine = line_scatter(
-        [both[:, d * units : (d + 1) * units] for d in range(z_size)], "z"
-    )
-    own, other = jnp.split(mine, 2, axis=-1)
-    other = swap(other.astype(BF16), "y", 1).astype(F32)
-    ffn_grad = jnp.concatenate(
-        [jnp.where(y == 0, own, other), jnp.where(y == 0, other, own)], axis=1
-    )
-    ffn_grad = scatter_runs(ffn_grad)
-    out_grad = scatter_runs(scatter_heads(out_grad))
-    qkv_grad = scatter_runs(scatter_heads(qkv_grad))
+    ffn_out = scatter_near([out_own] + jnp.split(out_rest, 3, axis=0))
+    ffn_out = sum(v.astype(F32) for v in ffn_out)
+    block_out = arrays_order((hidden + ffn_out).astype(BF16), y, c)
+
+    qkv_grad = scatter_runs(scatter_pair(dw_own, dw_other))
+    ffn_grad = scatter_runs(scatter_pair(ffn_grad[:, :units], ffn_grad[:, units:]))
+    out_grad = scatter_runs(scatter_out(out_grad.reshape((4, 2) + out_grad.shape[1:])))
 
     d = x.shape[1]
     gains = total_of(
         jnp.concatenate(
             [
                 arrays_order(attn_gain_part[None], y, c)[0],
-                arrays_order(ffn_gain_part[None], y, c)[0],
+                arrays_order(ffn_gain_part, y, c)[0],
                 q_part[0, :head] + q_part[0, head:],
                 k_part[0, :head],
             ]
@@ -705,9 +804,9 @@
 def solution(mesh):
     dp, tensor = mesh.shape["dp"], mesh.shape["tensor"]
     cut = Mesh(
-        mesh.devices.reshape(dp // 4, 2, 2, tensor // 2, 2), ("r", "y", "c", "z", "x")
-    )
-    data, model = ("r", "y", "c"), ("z", "x")
+        mesh.devices.reshape(dp // 4, 2, 2, tensor // 4, 2, 2), ("r", "y", "c", "zh", "zl", "x")
+    )
+    data, model = ("r", "y", "c"), TENSOR
     both = data + model
     rows, wide, tall = P(both, None), P(data, model), P(model, data)
     in_specs = (

time: 525 us -> 476 us (0.907)
  matrix products: 70.4 us -> 0 us
  starting transfers between devices: 144 us -> 99.2 us
  other arithmetic: 45.3 us -> 87.8 us
  Pallas kernels: 54.7 us -> 80.2 us
  waiting for transfers between devices: 166 us -> 157 us
  local copies, waits for them, and re-layouts: 34.2 us -> 43 us
    ppermute x36 -> x0, starting transfers between devices: 87.4 us -> none  [the longest x9 45.1 us: line_scatter(): lax.ppermute(up.astype(BF16), axis, [(i, i + 1) for i in range(size - m)])]
    dot_general x18 -> x0, matrix products: 70.4 us -> none  [the longest x3 28.9 us: nt(): lax.dot_general(a, b, (((1,), (1,)), ((), ())), preferred_element_type=F32)]
    ppermute x36 -> x0, waiting for transfers between devices: 64.5 us -> none  [the longest x9 32.3 us: line_gather(): lax.ppermute(right, axis, [(i, i - 1) for i in range(1, size - step + 1)])]
    ppermute x43 -> x57, waiting for transfers between devices: 86.4 us -> 146 us  [swap(): return lax.ppermute(v, axes, [(i, i ^ bit) for i in range(size)])]
    concatenate x9 -> x17, other arithmetic: 12.3 us -> 58.4 us  [the longest x1 42.5 us: per_device(): ffn_w = jnp.concatenate(ffn_w, axis=1)]
    ppermute x43 -> x57, starting transfers between devices: 38.3 us -> 82.2 us  [swap(): return lax.ppermute(v, axes, [(i, i ^ bit) for i in range(size)])]
    pallas_call x0 -> x3, Pallas kernels: none -> 34.7 us  [the longest x2 22.7 us: ffn_call(): pl.pallas_call(ffn_kernel, grid=(rows // BLOCK,), in_specs=[tokens, token...]
    all_to_all x4 -> x2, waiting for transfers between devices: 15.2 us -> 11 us  [to_heads(): return lax.all_to_all(v, TENSOR, 0, 0, tiled=True)]
  transfers between devices with their start and end apart: 83 -> 59, of which waited for: 26 -> 29; matrix products, arithmetic and copies ran while one was open for 19% -> 14% of each run, Pallas kernels for 11% -> 12%
where the time goes in v2:
time: 476 us; the launch traced here: 470 us
  waiting for transfers between devices  157 us (33%)
  starting transfers between devices  99.2 us (21%)
  other arithmetic  87.8 us (18%)
  Pallas kernels  80.2 us (17%)
  local copies, waits for them, and re-layouts  43 us (9%)
    ppermute x57, waiting for transfers between devices, swap(): return lax.ppermute(v, axes, [(i, i ^ bit) for i in range(size)])  146 us
    ppermute x57, starting transfers between devices, swap(): return lax.ppermute(v, axes, [(i, i ^ bit) for i in range(size)])  82.2 us
    concatenate x1, other arithmetic, per_device(): ffn_w = jnp.concatenate(ffn_w, axis=1)  42.5 us
    pallas_call x2, Pallas kernels, ffn_call(): pl.pallas_call(ffn_kernel, grid=(rows // BLOCK,), in_specs=[tokens, token...  22.7 us
    unnamed x138, local copies, waits for them, and re-layouts  18 us
    all_to_all x2, starting transfers between devices, to_heads(): return lax.all_to_all(v, TENSOR, 0, 0, tiled=True)  17 us
    pallas_call x1, Pallas kernels, attend_back_call(): pl.pallas_call(functools.partial(attend_back_kernel, head), grid_spec=plt...  14.2 us
    pallas_call x1, Pallas kernels, ffn_grad_call(): pl.pallas_call(ffn_grad_kernel, grid=(three, 3), in_specs=[pl.BlockSpec((...  12 us
  transfers between devices with their start and end apart: 59, of which 29 were waited for; matrix products, arithmetic and copies ran while one was open for 14% of the time, Pallas kernels for 12%

profile of v2, /device:TPU:0, one launch (start us, length us, event | category | flops | bytes accessed | tf_op | source)
XLA Modules:
  0.0 469.6 jit_solution(8547459195359967741)
XLA Ops:
  2.4 4.1 collective-permute-start.5
  10.3 2.6 collective-permute-start.2
  17.0 2.6 fusion.35
  20.6 5.3 %collective-permute-done.6 = bf16[256,256]{1,0:T(8,128)(2,1)S(1)} collective-permute-done((bf16[256,256]{1,0:T(8,128)(2,1)S(1)}, bf16[256,256]{1,0:T(8,128)(2,1)S(1)}, u32[]{:S(2)}, u32[]{:S(2)}) %collective-permute-start.6) | collective-permute-done | bytes 131104 | tf_op jit(solution)/shard_map/ppermute | solution.py:40
  26.3 9.5 %collective-permute-done.1 = bf16[256,1024]{1,0:T(8,128)(2,1)} collective-permute-done((bf16[256,1024]{1,0:T(8,128)(2,1)S(1)}, bf16[256,1024]{1,0:T(8,128)(2,1)}, u32[]{:S(2)}, u32[]{:S(2)}) %collective-permute-start.1) | collective-permute-done | bytes 524320 | tf_op jit(solution)/shard_map/ppermute | solution.py:40
  40.6 2.3 collective-permute-start.17
  43.1 2.8 collective-permute-done.9
  47.8 3.1 pad_maximum_fusion.13
  52.7 16.1 %collective-permute-start.12 = (bf16[2,128,512]{2,1,0:T(8,128)(2,1)S(1)}, bf16[2,128,512]{2,1,0:T(8,128)(2,1)S(1)}, u32[]{:S(2)}, u32[]{:S(2)}) collective-permute-start(bf16[2,128,512]{2,1,0:T(8,128)(2,1)S(1)} %get-tuple-element.169), channel_id=1, source_target_pairs={{0,2},{1,3},{2,0},{3,1},{4,6},{5,7},{6,4},{7,5},{8,10},{9,11},{10,... | collective-permute-start | bytes 786440 | tf_op jit(solution)/shard_map/ppermute | solution.py:40
  68.8 3.5 qkv.3
  72.3 4.2 collective-permute-start.8
  76.5 2.4 collective-permute-start.11
  79.7 3.5 qkv.2
  84.1 2.5 collective-permute-done.11
  88.7 3.2 collective-permute-done.13
  91.9 5.0 %collective-permute-start.24 = (bf16[256,1024]{1,0:T(8,128)(2,1)}, bf16[256,1024]{1,0:T(8,128)(2,1)}, u32[]{:S(2)}, u32[]{:S(2)}) collective-permute-start(bf16[256,1024]{1,0:T(8,128)(2,1)} %pad_maximum_fusion.15.dy.y_own), channel_id=1, source_target_pairs={{0,2},{1,3},{2,0},{3,1},{4,6},{5,7},{6,4},{7,5},{8,10},{9,11},{10,... | collective-permute-start | bytes 1572872 | tf_op jit(solution)/shard_map/ppermute | solution.py:40
  97.9 7.9 %collective-permute-done.8 = bf16[4,256,256]{2,1,0:T(8,128)(2,1)S(1)} collective-permute-done((bf16[4,256,256]{2,1,0:T(8,128)(2,1)S(1)}, bf16[4,256,256]{2,1,0:T(8,128)(2,1)S(1)}, u32[]{:S(2)}, u32[]{:S(2)}) %collective-permute-start.8) | collective-permute-done | bytes 524320 | tf_op jit(solution)/shard_map/ppermute | solution.py:40
  106.1 9.5 %attend.1 = (bf16[2048,128]{1,0:T(8,128)(2,1)S(1)}, f32[8,1,512]{2,1,0:T(1,128)S(1)}) custom-call(s32[8]{0:T(128)S(1)} %and_select_fusion.first, bf16[2048,256]{1,0:T(8,128)(2,1)S(1)} %bitcast.116, s32[8,1,512]{2,1,0:T(1,128)S(1)} %pad_add_fusion.start), custom_call_target="tpu_custom_call" | custom-call | flops 2147483648 | bytes 1572864 | tf_op jit(solution)/shard_map/attend/pallas_call | solution.py:260
  116.3 12.6 %all-to-all-start = ((bf16[8,256,128]{2,1,0:T(8,128)(2,1)}), bf16[8,256,128]{2,1,0:T(8,128)(2,1)S(1)}, u32[]{:S(2)}, u32[]{:S(2)}) async-start(bf16[8,256,128]{2,1,0:T(8,128)(2,1)} %bitcast.119), calls=%async_computation | async-start | bytes 1048576 | tf_op jit(solution)/shard_map/all_to_all | solution.py:742
  129.0 2.8 pad_maximum_fusion.2
  133.6 2.8 pad_maximum_fusion.3
  146.8 3.2 project.1
  159.8 4.8 %collective-permute-done.20 = bf16[256,1024]{1,0:T(8,128)(2,1)S(1)} collective-permute-done((bf16[256,1024]{1,0:T(8,128)(2,1)S(1)}, bf16[256,1024]{1,0:T(8,128)(2,1)S(1)}, u32[]{:S(2)}, u32[]{:S(2)}) %collective-permute-start.20) | collective-permute-done | bytes 524320 | tf_op jit(solution)/shard_map/ppermute | solution.py:40
  166.3 10.6 %collective-permute-done.22 = bf16[256,1024]{1,0:T(8,128)(2,1)S(1)} collective-permute-done((bf16[256,1024]{1,0:T(8,128)(2,1)S(1)}, bf16[256,1024]{1,0:T(8,128)(2,1)S(1)}, u32[]{:S(2)}, u32[]{:S(2)}) %collective-permute-start.22) | collective-permute-done | bytes 524320 | tf_op jit(solution)/shard_map/ppermute | solution.py:40
  180.9 42.5 %maximum_maximum_fusion.w = bf16[3,1152,1024]{2,1,0:T(8,128)(2,1)S(1)} fusion(bf16[3,576,256]{2,1,0:T(8,128)(2,1)S(1)} %get-tuple-element.124, bf16[3,576,256]{2,1,0:T(8,128)(2,1)} %collective-permute-done.18, bf16[3,576,256]{2,1,0:T(8,128)(2,1)S(1)} %get-tuple-element.123, bf16[3,576,256]{2,1,0:T(8,128)(2,1)} %collective-permute-done.17, ...), kind=kLoop, calls=%fused_computation.1 | loop fusion | flops 70778880 | bytes 14155776 | tf_op jit(solution)/shard_map/concatenate | solution.py:706
  223.4 6.0 %ffn.2 = (bf16[3,256,1152]{2,1,0:T(8,128)(2,1)S(1)}, bf16[256,1024]{1,0:T(8,128)(2,1)S(1)}, bf16[256,1024]{1,0:T(8,128)(2,1)S(1)}) custom-call(bf16[256,1024]{1,0:T(8,128)(2,1)S(1)} %get-tuple-element.52.xf.x_own, bf16[256,1024]{1,0:T(8,128)(2,1)} %pad_maximum_fusion.15.dy.y_own, bf16[3,1152,1024]{2,1,0:T(8,128)(2,1)S(1)} %maximum_maximum_fusion.w), custom_call_target="tpu_custom_call" | custom-call | flops 3623878656 | bytes 9175040 | tf_op jit(solution)/shard_map/ffn/pallas_call | solution.py:593
  231.6 16.7 %ffn.3 = (bf16[3,768,1152]{2,1,0:T(8,128)(2,1)S(1)}, bf16[768,1024]{1,0:T(8,128)(2,1)S(1)}, bf16[768,1024]{1,0:T(8,128)(2,1)S(1)}) custom-call(bf16[768,1024]{1,0:T(8,128)(2,1)S(1)} %copy-done.23, bf16[768,1024]{1,0:T(8,128)(2,1)S(1)} %copy-done.25, bf16[3,1152,1024]{2,1,0:T(8,128)(2,1)} %copy-done.2), custom_call_target="tpu_custom_call" | custom-call | flops 10871635968 | bytes 13369344 | tf_op jit(solution)/shard_map/ffn/pallas_call | solution.py:593
  256.2 2.5 copy-done.31
  258.7 12.0 %ffn_grad.1 = bf16[3,1152,1024]{2,1,0:T(8,128)(2,1)} custom-call(bf16[3,256,1152]{2,1,0:T(8,128)(2,1)S(1)} %copy-done.33, bf16[3,768,1152]{2,1,0:T(8,128)(2,1)S(1)} %copy-done.31, bf16[256,1024]{1,0:T(8,128)(2,1)S(1)} %get-tuple-element.52.xf.x_own, bf16[768,1024]{1,0:T(8,128)(2,1)S(1)} %copy-done.23, bf16[256,1024]{1,0:T(8,128)(2,1)} %pad_maximum_fusion.15.dy.y_own, ...), custom_call_target="tpu_custom_call" | custom-call | flops 7247757312 | bytes 16515072 | tf_op jit(solution)/shard_map/ffn_grad/pallas_call | solution.py:630
  270.7 18.8 %collective-permute-done.31.p3 = bf16[256,1024]{1,0:T(8,128)(2,1)S(1)} collective-permute-done((bf16[256,1024]{1,0:T(8,128)(2,1)S(1)}, bf16[256,1024]{1,0:T(8,128)(2,1)S(1)}, u32[]{:S(2)}, u32[]{:S(2)}) %collective-permute-start.31) | collective-permute-done | bytes 524320 | tf_op jit(solution)/shard_map/ppermute | solution.py:40
  290.0 5.3 %fusion.25 = (bf16[3,576,256]{2,1,0:T(8,128)(2,1)}, bf16[3,576,256]{2,1,0:T(8,128)(2,1)S(1)}, bf16[3,576,256]{2,1,0:T(8,128)(2,1)S(1)}, bf16[3,576,256]{2,1,0:T(...) fusion(bf16[3,1152,1024]{2,1,0:T(8,128)(2,1)} %ffn_grad.1), kind=kLoop, calls=%fused_computation.193 | loop fusion | bytes 14155776 | tf_op jit(solution)/shard_map/split | solution.py:44
  300.4 5.4 %project_back.1 = (bf16[8,256,128]{2,1,0:T(8,128)(2,1)S(1)}, bf16[8,128,1024]{2,1,0:T(8,128)(2,1)S(1)}, f32[256,1024]{1,0:T(8,128)S(1)}, f32[1,1024]{1,0:T(1,128)S(1)}) custom-call(s32[8]{0:T(128)S(1)} %fusion.20.order, bf16[8,256,128]{2,1,0:T(8,128)(2,1)S(1)} %all-to-all-done.context, bf16[8,128,1024]{2,1,0:T(8,128)(2,1)S(1)} %bitcast.114, ...), custom_call_target="tpu_custom_call" | custom-call | flops 1073741824 | bytes 4194304 | tf_op jit(solution)/shard_map/project_back/pallas_call | solution.py:445
  309.0 4.4 all-to-all-start.1
  313.4 2.4 add_convert_fusion.4
  319.5 9.3 %all-to-all-done.1 = bf16[8,256,128]{2,1,0:T(8,128)(2,1)} async-done(((bf16[8,256,128]{2,1,0:T(8,128)(2,1)}), bf16[8,256,128]{2,1,0:T(8,128)(2,1)}, u32[]{:S(2)}, u32[]{:S(2)}) %all-to-all-start.1) | async-done | bytes 524320 | tf_op jit(solution)/shard_map/all_to_all | solution.py:742
  330.1 14.2 %attend_back.1 = bf16[2048,256]{1,0:T(8,128)(2,1)S(1)} custom-call(s32[8]{0:T(128)S(1)} %and_select_fusion.first, bf16[2048,256]{1,0:T(8,128)(2,1)S(1)} %bitcast.117, bf16[2048,128]{1,0:T(8,128)(2,1)S(1)} %copy-done.20, bf16[2048,128]{1,0:T(8,128)(2,1)} %bitcast.35.d_context, s32[8,1,512]{2,1,0:T(1,128)S(1)} %pad_add_fusion.start, ...), custom_call_target="tpu_custom_call" | custom-call | flops 5368709120 | bytes 3145728 | tf_op jit(solution)/shard_map/attend_back/pallas_call | solution.py:347
  352.7 4.0 collective-permute-start.53
  361.2 11.6 %collective-permute-done.48 = bf16[2,128,512]{2,1,0:T(8,128)(2,1)S(1)} collective-permute-done((bf16[2,128,512]{2,1,0:T(8,128)(2,1)S(1)}, bf16[2,128,512]{2,1,0:T(8,128)(2,1)S(1)}, u32[]{:S(2)}, u32[]{:S(2)}) %collective-permute-start.48) | collective-permute-done | bytes 262176 | tf_op jit(solution)/shard_map/ppermute | solution.py:40
  373.0 2.5 collective-permute-start.50
  375.5 6.3 %qkv_back.1 = (bf16[4,256,1024]{2,1,0:T(8,128)(2,1)S(1)}, bf16[256,1024]{1,0:T(8,128)(2,1)S(1)}, bf16[256,1024]{1,0:T(8,128)(2,1)S(1)}, f32[1,128]{1,0:T(1,128)S(1)}, f32[1,128]{1,0:T(1,128)S(1)}) custom-call(s32[5]{0:T(128)S(1)} %pad_add_fusion.1.order.where, bf16[8,256,256]{2,1,0:T(8,128)(2,1)S(1)} %bitcast.118, ...), custom_call_target="tpu_custom_call" | custom-call | flops 2147483648 | bytes 8388608 | tf_op jit(solution)/shard_map/qkv_back/pallas_call | solution.py:538
  384.1 4.3 collective-permute-done.51
  389.0 2.6 collective-permute-start.34
  392.8 3.9 collective-permute-done.44
  397.7 10.4 %collective-permute-done.33 = bf16[256,1024]{1,0:T(8,128)(2,1)S(1)} collective-permute-done((bf16[256,1024]{1,0:T(8,128)(2,1)S(1)}, bf16[256,1024]{1,0:T(8,128)(2,1)S(1)}, u32[]{:S(2)}, u32[]{:S(2)}) %collective-permute-start.33) | collective-permute-done | bytes 524320 | tf_op jit(solution)/shard_map/ppermute | solution.py:40
  411.1 4.9 %collective-permute-done.34 = bf16[256,1024]{1,0:T(8,128)(2,1)S(1)} collective-permute-done((bf16[256,1024]{1,0:T(8,128)(2,1)S(1)}, bf16[256,1024]{1,0:T(8,128)(2,1)S(1)}, u32[]{:S(2)}, u32[]{:S(2)}) %collective-permute-start.34) | collective-permute-done | bytes 524320 | tf_op jit(solution)/shard_map/ppermute | solution.py:40
  428.0 15.3 %collective-permute-done.39 = f32[17,128]{1,0:T(8,128)S(1)} collective-permute-done((f32[17,128]{1,0:T(8,128)S(1)}, f32[17,128]{1,0:T(8,128)S(1)}, u32[]{:S(2)}, u32[]{:S(2)}) %collective-permute-start.39) | collective-permute-done | bytes 8736 | tf_op jit(solution)/shard_map/ppermute | solution.py:40
  443.2 3.1 collective-permute-start.40
  448.0 17.0 %collective-permute-done.40 = f32[17,128]{1,0:T(8,128)S(1)} collective-permute-done((f32[17,128]{1,0:T(8,128)S(1)}, f32[17,128]{1,0:T(8,128)S(1)}, u32[]{:S(2)}, u32[]{:S(2)}) %collective-permute-start.40) | collective-permute-done | bytes 8736 | tf_op jit(solution)/shard_map/ppermute | solution.py:40
  (338 shorter events, 115.0 us)
Async XLA Ops:
  2.4 17.6 %collective-permute-start.5 = (bf16[256,256]{1,0:T(8,128)(2,1)S(1)}, bf16[256,256]{1,0:T(8,128)(2,1)S(1)}, u32[]{:S(2)}, u32[]{:S(2)}) collective-permute-start(bf16[256,256]{1,0:T(8,128)(2,1)S(1)} %pad_maximum_fusion.23), channel_id=1, source_target_pairs={{0,4},{4,0},{1,5},{5,1},{2,6},{6,2},{3,7},{7,3},{8,12},{12,8},{9,1... | collective-permute-start | bytes 393224 | tf_op jit(solution)/shard_map/ppermute | solution.py:40
  6.5 13.4 %collective-permute-start.3 = (bf16[256,256]{1,0:T(8,128)(2,1)S(1)}, bf16[256,256]{1,0:T(8,128)(2,1)S(1)}, u32[]{:S(2)}, u32[]{:S(2)}) collective-permute-start(bf16[256,256]{1,0:T(8,128)(2,1)S(1)} %pad_maximum_fusion.23), channel_id=1, source_target_pairs={{0,16},{16,0},{1,17},{17,1},{2,18},{18,2},{3,19},{19,3},{4,20},{20... | collective-permute-start | bytes 393224 | tf_op jit(solution)/shard_map/ppermute | solution.py:40
  10.3 16.0 %collective-permute-start.2 = (bf16[256,1024]{1,0:T(8,128)(2,1)S(1)}, bf16[256,1024]{1,0:T(8,128)(2,1)}, u32[]{:S(2)}, u32[]{:S(2)}) collective-permute-start(bf16[256,1024]{1,0:T(8,128)(2,1)S(1)} %fusion.2), channel_id=1, source_target_pairs={{0,3},{1,2},{2,1},{3,0},{4,7},{5,6},{6,5},{7,4},{8,11},{9,10},{10,... | collective-permute-start | bytes 1572872 | tf_op jit(solution)/shard_map/ppermute | solution.py:40
  12.9 22.9 %collective-permute-start.1 = (bf16[256,1024]{1,0:T(8,128)(2,1)S(1)}, bf16[256,1024]{1,0:T(8,128)(2,1)}, u32[]{:S(2)}, u32[]{:S(2)}) collective-permute-start(bf16[256,1024]{1,0:T(8,128)(2,1)S(1)} %fusion.2), channel_id=1, source_target_pairs={{0,2},{1,3},{2,0},{3,1},{4,6},{5,7},{6,4},{7,5},{8,10},{9,11},{10,... | collective-permute-start | bytes 1572872 | tf_op jit(solution)/shard_map/ppermute | solution.py:40
  13.4 23.0 %collective-permute-start = (bf16[256,1024]{1,0:T(8,128)(2,1)S(1)}, bf16[256,1024]{1,0:T(8,128)(2,1)}, u32[]{:S(2)}, u32[]{:S(2)}) collective-permute-start(bf16[256,1024]{1,0:T(8,128)(2,1)S(1)} %fusion.2), channel_id=1, source_target_pairs={{0,1},{1,0},{2,3},{3,2},{4,5},{5,4},{6,7},{7,6},{8,9},{9,8},{10,11... | collective-permute-start | bytes 1572872 | tf_op jit(solution)/shard_map/ppermute | solution.py:40
  25.9 12.2 %collective-permute-start.7 = (bf16[256,512]{1,0:T(8,128)(2,1)S(1)}, bf16[256,512]{1,0:T(8,128)(2,1)S(1)}, u32[]{:S(2)}, u32[]{:S(2)}) collective-permute-start(bf16[256,512]{1,0:T(8,128)(2,1)S(1)} %pad_maximum_fusion.19), channel_id=1, source_target_pairs={{0,8},{8,0},{1,9},{9,1},{2,10},{10,2},{3,11},{11,3},{4,12},{12,4},... | collective-permute-start | bytes 786440 | tf_op jit(solution)/shard_map/ppermute | solution.py:40
  40.6 56.2 %collective-permute-start.17 = (bf16[3,576,256]{2,1,0:T(8,128)(2,1)}, bf16[3,576,256]{2,1,0:T(8,128)(2,1)}, u32[]{:S(2)}, u32[]{:S(2)}) collective-permute-start(bf16[3,576,256]{2,1,0:T(8,128)(2,1)} %pad_maximum_fusion.9), channel_id=1, source_target_pairs={{0,4},{4,0},{1,5},{5,1},{2,6},{6,2},{3,7},{7,3},{8,12},{12,8},{9,1... | collective-permute-start | bytes 2654216 | tf_op jit(solution)/shard_map/ppermute | solution.py:40
  52.7 26.3 %collective-permute-start.12 = (bf16[2,128,512]{2,1,0:T(8,128)(2,1)S(1)}, bf16[2,128,512]{2,1,0:T(8,128)(2,1)S(1)}, u32[]{:S(2)}, u32[]{:S(2)}) collective-permute-start(bf16[2,128,512]{2,1,0:T(8,128)(2,1)S(1)} %get-tuple-element.169), channel_id=1, source_target_pairs={{0,2},{1,3},{2,0},{3,1},{4,6},{5,7},{6,4},{7,5},{8,10},{9,11},{10,... | collective-permute-start | bytes 786440 | tf_op jit(solution)/shard_map/ppermute | solution.py:40
  72.3 33.5 %collective-permute-start.8 = (bf16[4,256,256]{2,1,0:T(8,128)(2,1)S(1)}, bf16[4,256,256]{2,1,0:T(8,128)(2,1)S(1)}, u32[]{:S(2)}, u32[]{:S(2)}) collective-permute-start(bf16[4,256,256]{2,1,0:T(8,128)(2,1)S(1)} %get-tuple-element.48), channel_id=1, source_target_pairs={{0,4},{4,0},{1,5},{5,1},{2,6},{6,2},{3,7},{7,3},{8,12},{12,8},{9,1... | collective-permute-start | bytes 1572872 | tf_op jit(solution)/shard_map/ppermute | solution.py:40
  76.5 10.1 %collective-permute-start.11 = (bf16[2,128,512]{2,1,0:T(8,128)(2,1)S(1)}, bf16[2,128,512]{2,1,0:T(8,128)(2,1)S(1)}, u32[]{:S(2)}, u32[]{:S(2)}) collective-permute-start(bf16[2,128,512]{2,1,0:T(8,128)(2,1)S(1)} %get-tuple-element.169), channel_id=1, source_target_pairs={{0,1},{1,0},{2,3},{3,2},{4,5},{5,4},{6,7},{7,6},{8,9},{9,8},{10,11... | collective-permute-start | bytes 786440 | tf_op jit(solution)/shard_map/ppermute | solution.py:40
  78.9 12.9 %collective-permute-start.13 = (bf16[2,128,512]{2,1,0:T(8,128)(2,1)S(1)}, bf16[2,128,512]{2,1,0:T(8,128)(2,1)S(1)}, u32[]{:S(2)}, u32[]{:S(2)}) collective-permute-start(bf16[2,128,512]{2,1,0:T(8,128)(2,1)S(1)} %get-tuple-element.169), channel_id=1, source_target_pairs={{0,3},{1,2},{2,1},{3,0},{4,7},{5,6},{6,5},{7,4},{8,11},{9,10},{10,... | collective-permute-start | bytes 786440 | tf_op jit(solution)/shard_map/ppermute | solution.py:40
  79.0 50.0 %collective-permute-start.15 = (bf16[3,576,256]{2,1,0:T(8,128)(2,1)}, bf16[3,576,256]{2,1,0:T(8,128)(2,1)}, u32[]{:S(2)}, u32[]{:S(2)}) collective-permute-start(bf16[3,576,256]{2,1,0:T(8,128)(2,1)} %pad_maximum_fusion.9), channel_id=1, source_target_pairs={{0,16},{16,0},{1,17},{17,1},{2,18},{18,2},{3,19},{19,3},{4,20},{20... | collective-permute-start | bytes 2654216 | tf_op jit(solution)/shard_map/ppermute | solution.py:40
  86.6 63.4 %collective-permute-start.25 = (bf16[256,1024]{1,0:T(8,128)(2,1)}, bf16[256,1024]{1,0:T(8,128)(2,1)}, u32[]{:S(2)}, u32[]{:S(2)}) collective-permute-start(bf16[256,1024]{1,0:T(8,128)(2,1)} %pad_maximum_fusion.15.dy.y_own), channel_id=1, source_target_pairs={{0,3},{1,2},{2,1},{3,0},{4,7},{5,6},{6,5},{7,4},{8,11},{9,10},{10,... | collective-permute-start | bytes 1572872 | tf_op jit(solution)/shard_map/ppermute | solution.py:40
  91.9 59.7 %collective-permute-start.24 = (bf16[256,1024]{1,0:T(8,128)(2,1)}, bf16[256,1024]{1,0:T(8,128)(2,1)}, u32[]{:S(2)}, u32[]{:S(2)}) collective-permute-start(bf16[256,1024]{1,0:T(8,128)(2,1)} %pad_maximum_fusion.15.dy.y_own), channel_id=1, source_target_pairs={{0,2},{1,3},{2,0},{3,1},{4,6},{5,7},{6,4},{7,5},{8,10},{9,11},{10,... | collective-permute-start | bytes 1572872 | tf_op jit(solution)/shard_map/ppermute | solution.py:40
  96.8 36.8 %collective-permute-start.18 = (bf16[3,576,256]{2,1,0:T(8,128)(2,1)}, bf16[3,576,256]{2,1,0:T(8,128)(2,1)}, u32[]{:S(2)}, u32[]{:S(2)}) collective-permute-start(bf16[3,576,256]{2,1,0:T(8,128)(2,1)} %collective-permute-done.17), channel_id=1, source_target_pairs={{0,16},{16,0},{1,17},{17,1},{2,18},{18,2},{3,19},{19,3},{4,20},{20... | collective-permute-start | bytes 2654216 | tf_op jit(solution)/shard_map/ppermute | solution.py:40
  105.9 31.8 %collective-permute-start.14 = (bf16[4,2,128,512]{3,2,1,0:T(8,128)(2,1)}, bf16[4,2,128,512]{3,2,1,0:T(8,128)(2,1)}, u32[]{:S(2)}, u32[]{:S(2)}) collective-permute-start(bf16[4,2,128,512]{3,2,1,0:T(8,128)(2,1)} %pad_maximum_fusion.7), channel_id=1, source_target_pairs={{0,8},{8,0},{1,9},{9,1},{2,10},{10,2},{3,11},{11,3},{4,12},{12,4},... | collective-permute-start | bytes 3145736 | tf_op jit(solution)/shard_map/ppermute | solution.py:40
  116.3 27.6 %all-to-all-start = ((bf16[8,256,128]{2,1,0:T(8,128)(2,1)}), bf16[8,256,128]{2,1,0:T(8,128)(2,1)S(1)}, u32[]{:S(2)}, u32[]{:S(2)}) async-start(bf16[8,256,128]{2,1,0:T(8,128)(2,1)} %bitcast.119), calls=%async_computation | async-start | bytes 1048576 | tf_op jit(solution)/shard_map/all_to_all | solution.py:742
  131.8 45.3 %collective-permute-start.16 = (bf16[3,576,512]{2,1,0:T(8,128)(2,1)}, bf16[3,576,512]{2,1,0:T(8,128)(2,1)}, u32[]{:S(2)}, u32[]{:S(2)}) collective-permute-start(bf16[3,576,512]{2,1,0:T(8,128)(2,1)} %pad_maximum_fusion.2), channel_id=1, source_target_pairs={{0,8},{8,0},{1,9},{9,1},{2,10},{10,2},{3,11},{11,3},{4,12},{12,4},... | collective-permute-start | bytes 5308424 | tf_op jit(solution)/shard_map/ppermute | solution.py:40
  136.4 42.8 %collective-permute-start.19 = (bf16[3,576,512]{2,1,0:T(8,128)(2,1)}, bf16[3,576,512]{2,1,0:T(8,128)(2,1)}, u32[]{:S(2)}, u32[]{:S(2)}) collective-permute-start(bf16[3,576,512]{2,1,0:T(8,128)(2,1)} %pad_maximum_fusion.3), channel_id=1, source_target_pairs={{0,8},{8,0},{1,9},{9,1},{2,10},{10,2},{3,11},{11,3},{4,12},{12,4},... | collective-permute-start | bytes 5308424 | tf_op jit(solution)/shard_map/ppermute | solution.py:40
  137.7 15.7 %collective-permute-start.23 = (bf16[256,1024]{1,0:T(8,128)(2,1)}, bf16[256,1024]{1,0:T(8,128)(2,1)}, u32[]{:S(2)}, u32[]{:S(2)}) collective-permute-start(bf16[256,1024]{1,0:T(8,128)(2,1)} %pad_maximum_fusion.15.dy.y_own), channel_id=1, source_target_pairs={{0,1},{1,0},{2,3},{3,2},{4,5},{5,4},{6,7},{7,6},{8,9},{9,8},{10,11... | collective-permute-start | bytes 1572872 | tf_op jit(solution)/shard_map/ppermute | solution.py:40
  150.0 14.6 %collective-permute-start.20 = (bf16[256,1024]{1,0:T(8,128)(2,1)S(1)}, bf16[256,1024]{1,0:T(8,128)(2,1)S(1)}, u32[]{:S(2)}, u32[]{:S(2)}) collective-permute-start(bf16[256,1024]{1,0:T(8,128)(2,1)S(1)} %get-tuple-element.52.xf.x_own), channel_id=1, source_target_pairs={{0,1},{1,0},{2,3},{3,2},{4,5},{5,4},{6,7},{7,6},{8,9},{9,8},{10,11... | collective-permute-start | bytes 1572872 | tf_op jit(solution)/shard_map/ppermute | solution.py:40
  151.6 14.8 %collective-permute-start.21 = (bf16[256,1024]{1,0:T(8,128)(2,1)S(1)}, bf16[256,1024]{1,0:T(8,128)(2,1)S(1)}, u32[]{:S(2)}, u32[]{:S(2)}) collective-permute-start(bf16[256,1024]{1,0:T(8,128)(2,1)S(1)} %get-tuple-element.52.xf.x_own), channel_id=1, source_target_pairs={{0,2},{1,3},{2,0},{3,1},{4,6},{5,7},{6,4},{7,5},{8,10},{9,11},{10,... | collective-permute-start | bytes 1572872 | tf_op jit(solution)/shard_map/ppermute | solution.py:40
  153.4 23.6 %collective-permute-start.22 = (bf16[256,1024]{1,0:T(8,128)(2,1)S(1)}, bf16[256,1024]{1,0:T(8,128)(2,1)S(1)}, u32[]{:S(2)}, u32[]{:S(2)}) collective-permute-start(bf16[256,1024]{1,0:T(8,128)(2,1)S(1)} %get-tuple-element.52.xf.x_own), channel_id=1, source_target_pairs={{0,3},{1,2},{2,1},{3,0},{4,7},{5,6},{6,5},{7,4},{8,11},{9,10},{10,... | collective-permute-start | bytes 1572872 | tf_op jit(solution)/shard_map/ppermute | solution.py:40
  249.5 63.8 %collective-permute-start.26 = (bf16[256,1024]{1,0:T(8,128)(2,1)}, bf16[256,1024]{1,0:T(8,128)(2,1)}, u32[]{:S(2)}, u32[]{:S(2)}) collective-permute-start(bf16[256,1024]{1,0:T(8,128)(2,1)} %get-tuple-element.128), channel_id=1, source_target_pairs={{0,1},{1,0},{2,3},{3,2},{4,5},{5,4},{6,7},{7,6},{8,9},{9,8},{10,11... | collective-permute-start | bytes 1572872 | tf_op jit(solution)/shard_map/ppermute | solution.py:40
  251.0 62.4 %collective-permute-start.28 = (bf16[256,1024]{1,0:T(8,128)(2,1)}, bf16[256,1024]{1,0:T(8,128)(2,1)}, u32[]{:S(2)}, u32[]{:S(2)}) collective-permute-start(bf16[256,1024]{1,0:T(8,128)(2,1)} %get-tuple-element.129), channel_id=1, source_target_pairs={{0,3},{1,2},{2,1},{3,0},{4,7},{5,6},{6,5},{7,4},{8,11},{9,10},{10,... | collective-permute-start | bytes 1572872 | tf_op jit(solution)/shard_map/ppermute | solution.py:40
  251.3 62.1 %collective-permute-start.27 = (bf16[256,1024]{1,0:T(8,128)(2,1)}, bf16[256,1024]{1,0:T(8,128)(2,1)}, u32[]{:S(2)}, u32[]{:S(2)}) collective-permute-start(bf16[256,1024]{1,0:T(8,128)(2,1)} %get-tuple-element.130), channel_id=1, source_target_pairs={{0,2},{1,3},{2,0},{3,1},{4,6},{5,7},{6,4},{7,5},{8,10},{9,11},{10,... | collective-permute-start | bytes 1572872 | tf_op jit(solution)/shard_map/ppermute | solution.py:40
  253.2 36.3 %collective-permute-start.31 = (bf16[256,1024]{1,0:T(8,128)(2,1)S(1)}, bf16[256,1024]{1,0:T(8,128)(2,1)S(1)}, u32[]{:S(2)}, u32[]{:S(2)}) collective-permute-start(bf16[256,1024]{1,0:T(8,128)(2,1)S(1)} %get-tuple-element.125), channel_id=1, source_target_pairs={{0,3},{1,2},{2,1},{3,0},{4,7},{5,6},{6,5},{7,4},{8,11},{9,10},{10,... | collective-permute-start | bytes 1572872 | tf_op jit(solution)/shard_map/ppermute | solution.py:40
  254.4 43.7 %collective-permute-start.30 = (bf16[256,1024]{1,0:T(8,128)(2,1)S(1)}, bf16[256,1024]{1,0:T(8,128)(2,1)S(1)}, u32[]{:S(2)}, u32[]{:S(2)}) collective-permute-start(bf16[256,1024]{1,0:T(8,128)(2,1)S(1)} %get-tuple-element.126), channel_id=1, source_target_pairs={{0,2},{1,3},{2,0},{3,1},{4,6},{5,7},{6,4},{7,5},{8,10},{9,11},{10,... | collective-permute-start | bytes 1572872 | tf_op jit(solution)/shard_map/ppermute | solution.py:40
  289.5 10.9 %collective-permute-start.29 = (bf16[256,1024]{1,0:T(8,128)(2,1)S(1)}, bf16[256,1024]{1,0:T(8,128)(2,1)S(1)}, u32[]{:S(2)}, u32[]{:S(2)}) collective-permute-start(bf16[256,1024]{1,0:T(8,128)(2,1)S(1)} %get-tuple-element.127), channel_id=1, source_target_pairs={{0,1},{1,0},{2,3},{3,2},{4,5},{5,4},{6,7},{7,6},{8,9},{9,8},{10,11... | collective-permute-start | bytes 1572872 | tf_op jit(solution)/shard_map/ppermute | solution.py:40
  298.1 51.6 %collective-permute-start.52 = (bf16[3,576,512]{2,1,0:T(8,128)(2,1)}, bf16[3,576,512]{2,1,0:T(8,128)(2,1)}, u32[]{:S(2)}, u32[]{:S(2)}) collective-permute-start(bf16[3,576,512]{2,1,0:T(8,128)(2,1)} %pad_maximum_fusion.4), channel_id=1, source_target_pairs={{0,8},{8,0},{1,9},{9,1},{2,10},{10,2},{3,11},{11,3},{4,12},{12,4},... | collective-permute-start | bytes 5308424 | tf_op jit(solution)/shard_map/ppermute | solution.py:40
  300.3 52.3 %collective-permute-start.54 = (bf16[3,576,512]{2,1,0:T(8,128)(2,1)}, bf16[3,576,512]{2,1,0:T(8,128)(2,1)}, u32[]{:S(2)}, u32[]{:S(2)}) collective-permute-start(bf16[3,576,512]{2,1,0:T(8,128)(2,1)} %pad_maximum_fusion.5), channel_id=1, source_target_pairs={{0,8},{8,0},{1,9},{9,1},{2,10},{10,2},{3,11},{11,3},{4,12},{12,4},... | collective-permute-start | bytes 5308424 | tf_op jit(solution)/shard_map/ppermute | solution.py:40
  309.0 19.9 %all-to-all-start.1 = ((bf16[8,256,128]{2,1,0:T(8,128)(2,1)}), bf16[8,256,128]{2,1,0:T(8,128)(2,1)}, u32[]{:S(2)}, u32[]{:S(2)}) async-start(bf16[8,256,128]{2,1,0:T(8,128)(2,1)} %copy-done.21), calls=%async_computation.1 | async-start | bytes 1048576 | tf_op jit(solution)/shard_map/all_to_all | solution.py:742
  318.1 26.3 %collective-permute-start.46 = (bf16[4,2,128,512]{3,2,1,0:T(8,128)(2,1)}, bf16[4,2,128,512]{3,2,1,0:T(8,128)(2,1)}, u32[]{:S(2)}, u32[]{:S(2)}) collective-permute-start(bf16[4,2,128,512]{3,2,1,0:T(8,128)(2,1)} %pad_maximum_fusion.8), channel_id=1, source_target_pairs={{0,8},{8,0},{1,9},{9,1},{2,10},{10,2},{3,11},{11,3},{4,12},{12,4},... | collective-permute-start | bytes 3145736 | tf_op jit(solution)/shard_map/ppermute | solution.py:40
  344.3 31.2 %collective-permute-start.32 = (bf16[4,256,256]{2,1,0:T(8,128)(2,1)S(1)}, bf16[4,256,256]{2,1,0:T(8,128)(2,1)S(1)}, u32[]{:S(2)}, u32[]{:S(2)}) collective-permute-start(bf16[4,256,256]{2,1,0:T(8,128)(2,1)S(1)} %bitcast.136), channel_id=1, source_target_pairs={{0,4},{4,0},{1,5},{5,1},{2,6},{6,2},{3,7},{7,3},{8,12},{12,8},{9,1... | collective-permute-start | bytes 1572872 | tf_op jit(solution)/shard_map/ppermute | solution.py:40
  346.2 13.9 %collective-permute-start.47 = (bf16[2,128,512]{2,1,0:T(8,128)(2,1)S(1)}, bf16[2,128,512]{2,1,0:T(8,128)(2,1)S(1)}, u32[]{:S(2)}, u32[]{:S(2)}) collective-permute-start(bf16[2,128,512]{2,1,0:T(8,128)(2,1)S(1)} %get-tuple-element.131), channel_id=1, source_target_pairs={{0,1},{1,0},{2,3},{3,2},{4,5},{5,4},{6,7},{7,6},{8,9},{9,8},{10,11... | collective-permute-start | bytes 786440 | tf_op jit(solution)/shard_map/ppermute | solution.py:40
  347.6 13.5 %collective-permute-start.49 = (bf16[2,128,512]{2,1,0:T(8,128)(2,1)S(1)}, bf16[2,128,512]{2,1,0:T(8,128)(2,1)S(1)}, u32[]{:S(2)}, u32[]{:S(2)}) collective-permute-start(bf16[2,128,512]{2,1,0:T(8,128)(2,1)S(1)} %get-tuple-element.132), channel_id=1, source_target_pairs={{0,3},{1,2},{2,1},{3,0},{4,7},{5,6},{6,5},{7,4},{8,11},{9,10},{10,... | collective-permute-start | bytes 786440 | tf_op jit(solution)/shard_map/ppermute | solution.py:40
  349.7 23.1 %collective-permute-start.48 = (bf16[2,128,512]{2,1,0:T(8,128)(2,1)S(1)}, bf16[2,128,512]{2,1,0:T(8,128)(2,1)S(1)}, u32[]{:S(2)}, u32[]{:S(2)}) collective-permute-start(bf16[2,128,512]{2,1,0:T(8,128)(2,1)S(1)} %get-tuple-element.133), channel_id=1, source_target_pairs={{0,2},{1,3},{2,0},{3,1},{4,6},{5,7},{6,4},{7,5},{8,10},{9,11},{10,... | collective-permute-start | bytes 786440 | tf_op jit(solution)/shard_map/ppermute | solution.py:40
  352.7 113.5 %collective-permute-start.53 = (bf16[3,576,256]{2,1,0:T(8,128)(2,1)}, bf16[3,576,256]{2,1,0:T(8,128)(2,1)}, u32[]{:S(2)}, u32[]{:S(2)}) collective-permute-start(bf16[3,576,256]{2,1,0:T(8,128)(2,1)} %split.367), channel_id=1, source_target_pairs={{0,16},{16,0},{1,17},{17,1},{2,18},{18,2},{3,19},{19,3},{4,20},{20... | collective-permute-start | bytes 2654216 | tf_op jit(solution)/shard_map/ppermute | solution.py:40
  373.0 9.7 %collective-permute-start.50 = (bf16[2,128,256]{2,1,0:T(8,128)(2,1)S(1)}, bf16[2,128,256]{2,1,0:T(8,128)(2,1)S(1)}, u32[]{:S(2)}, u32[]{:S(2)}) collective-permute-start(bf16[2,128,256]{2,1,0:T(8,128)(2,1)S(1)} %split.361), channel_id=1, source_target_pairs={{0,16},{16,0},{1,17},{17,1},{2,18},{18,2},{3,19},{19,3},{4,20},{20... | collective-permute-start | bytes 393224 | tf_op jit(solution)/shard_map/ppermute | solution.py:40
  383.0 25.2 %collective-permute-start.33 = (bf16[256,1024]{1,0:T(8,128)(2,1)S(1)}, bf16[256,1024]{1,0:T(8,128)(2,1)S(1)}, u32[]{:S(2)}, u32[]{:S(2)}) collective-permute-start(bf16[256,1024]{1,0:T(8,128)(2,1)S(1)} %get-tuple-element.115), channel_id=1, source_target_pairs={{0,1},{1,0},{2,3},{3,2},{4,5},{5,4},{6,7},{7,6},{8,9},{9,8},{10,11... | collective-permute-start | bytes 1572872 | tf_op jit(solution)/shard_map/ppermute | solution.py:40
  388.4 20.5 %collective-permute-start.35 = (bf16[256,1024]{1,0:T(8,128)(2,1)S(1)}, bf16[256,1024]{1,0:T(8,128)(2,1)S(1)}, u32[]{:S(2)}, u32[]{:S(2)}) collective-permute-start(bf16[256,1024]{1,0:T(8,128)(2,1)S(1)} %get-tuple-element.116), channel_id=1, source_target_pairs={{0,3},{1,2},{2,1},{3,0},{4,7},{5,6},{6,5},{7,4},{8,11},{9,10},{10,... | collective-permute-start | bytes 1572872 | tf_op jit(solution)/shard_map/ppermute | solution.py:40
  389.0 27.0 %collective-permute-start.34 = (bf16[256,1024]{1,0:T(8,128)(2,1)S(1)}, bf16[256,1024]{1,0:T(8,128)(2,1)S(1)}, u32[]{:S(2)}, u32[]{:S(2)}) collective-permute-start(bf16[256,1024]{1,0:T(8,128)(2,1)S(1)} %get-tuple-element.117), channel_id=1, source_target_pairs={{0,2},{1,3},{2,0},{3,1},{4,6},{5,7},{6,4},{7,5},{8,10},{9,11},{10,... | collective-permute-start | bytes 1572872 | tf_op jit(solution)/shard_map/ppermute | solution.py:40
  396.8 25.9 %collective-permute-start.55 = (bf16[3,576,256]{2,1,0:T(8,128)(2,1)}, bf16[3,576,256]{2,1,0:T(8,128)(2,1)}, u32[]{:S(2)}, u32[]{:S(2)}) collective-permute-start(bf16[3,576,256]{2,1,0:T(8,128)(2,1)} %split.373), channel_id=1, source_target_pairs={{0,16},{16,0},{1,17},{17,1},{2,18},{18,2},{3,19},{19,3},{4,20},{20... | collective-permute-start | bytes 2654216 | tf_op jit(solution)/shard_map/ppermute | solution.py:40
  408.1 11.9 %collective-permute-start.42 = (bf16[256,256]{1,0:T(8,128)(2,1)}, bf16[256,256]{1,0:T(8,128)(2,1)}, u32[]{:S(2)}, u32[]{:S(2)}) collective-permute-start(bf16[256,256]{1,0:T(8,128)(2,1)} %split.353), channel_id=1, source_target_pairs={{0,16},{16,0},{1,17},{17,1},{2,18},{18,2},{3,19},{19,3},{4,20},{20... | collective-permute-start | bytes 393224 | tf_op jit(solution)/shard_map/ppermute | solution.py:40
  408.9 11.1 %collective-permute-start.45 = (bf16[256,256]{1,0:T(8,128)(2,1)}, bf16[256,256]{1,0:T(8,128)(2,1)}, u32[]{:S(2)}, u32[]{:S(2)}) collective-permute-start(bf16[256,256]{1,0:T(8,128)(2,1)} %add_convert_fusion.7), channel_id=1, source_target_pairs={{0,4},{4,0},{1,5},{5,1},{2,6},{6,2},{3,7},{7,3},{8,12},{12,8},{9,1... | collective-permute-start | bytes 393224 | tf_op jit(solution)/shard_map/ppermute | solution.py:40
  424.2 42.0 %collective-permute-start.56 = (bf16[3,576,256]{2,1,0:T(8,128)(2,1)S(1)}, bf16[3,576,256]{2,1,0:T(8,128)(2,1)}, u32[]{:S(2)}, u32[]{:S(2)}) collective-permute-start(bf16[3,576,256]{2,1,0:T(8,128)(2,1)S(1)} %add_convert_fusion.3), channel_id=1, source_target_pairs={{0,4},{4,0},{1,5},{5,1},{2,6},{6,2},{3,7},{7,3},{8,12},{12,8},{9,1... | collective-permute-start | bytes 2654216 | tf_op jit(solution)/shard_map/ppermute | solution.py:40
  426.3 16.9 %collective-permute-start.39 = (f32[17,128]{1,0:T(8,128)S(1)}, f32[17,128]{1,0:T(8,128)S(1)}, u32[]{:S(2)}, u32[]{:S(2)}) collective-permute-start(f32[17,128]{1,0:T(8,128)S(1)} %add.154), channel_id=1, source_target_pairs={{0,2},{2,0},{1,3},{3,1},{4,6},{6,4},{5,7},{7,5},{8,10},{10,8},{9,1... | collective-permute-start | bytes 26120 | tf_op jit(solution)/shard_map/ppermute | solution.py:40
  443.2 21.7 %collective-permute-start.40 = (f32[17,128]{1,0:T(8,128)S(1)}, f32[17,128]{1,0:T(8,128)S(1)}, u32[]{:S(2)}, u32[]{:S(2)}) collective-permute-start(f32[17,128]{1,0:T(8,128)S(1)} %add.155), channel_id=1, source_target_pairs={{0,4},{4,0},{1,5},{5,1},{2,6},{6,2},{3,7},{7,3},{8,12},{12,8},{9,1... | collective-permute-start | bytes 26120 | tf_op jit(solution)/shard_map/ppermute | solution.py:40
  (77 other events, 904.1 us)
